TPU v7x, 32 devices: a whole 2x2x4 slice. The times are simulated.
32 devices in a mesh: shard: 4 (over z), ctx: 4 (over x, core), batch: 2 (over y).
Axes of the slice: x: 2, y: 2, z: 4, core: 2. Of those that a mesh axis runs over, the one named last changes fastest.
Arguments:
- tokens: bfloat16 [16, 2048, 1536], P(('shard', 'batch'), 'ctx'), may hold values from -6 to 6
- span_order: int32 [16, 16], P(('shard', 'batch')), may hold values from 0 to 15, as said below
- token_positions: int32 [16, 2048], P(('shard', 'batch'), 'ctx'), may hold values from 0 to 4094, as said below
- attn_gain: bfloat16 [1536], P('shard'), may hold values from 0.099609375 to 1.8984375
- w_query: bfloat16 [1536, 1536], P('shard'), may hold values from -0.15625 to 0.15625
- w_key: bfloat16 [1536, 768], P('shard'), may hold values from -0.15625 to 0.15625
- w_value: bfloat16 [1536, 768], P('shard'), may hold values from -0.15625 to 0.15625
- w_out: bfloat16 [1536, 1536], P('shard'), may hold values from -1.75 to 1.75
- mlp_gain: bfloat16 [1536], P('shard'), may hold values from 0.099609375 to 1.8984375
- w_gate: bfloat16 [1536, 4096], P('shard'), may hold values from -0.15625 to 0.15625
- w_up: bfloat16 [1536, 4096], P('shard'), may hold values from -0.15625 to 0.15625
- w_down: bfloat16 [4096, 1536], P('shard'), may hold values from -0.09375 to 0.09375
- cotangent: bfloat16 [16, 2048, 1536], P(('shard', 'batch'), 'ctx'), may hold values from -6 to 6
Outputs:
- layer_out: bfloat16 [16, 2048, 1536], P(('shard', 'batch'), 'ctx')
- grad_tokens: bfloat16 [16, 2048, 1536], P(('shard', 'batch'), 'ctx')
- grad_attn_gain: float32 [1536], P('shard')
- grad_w_query: float32 [1536, 1536], P('shard')
- grad_w_key: float32 [1536, 768], P('shard')
- grad_w_value: float32 [1536, 768], P('shard')
- grad_w_out: float32 [1536, 1536], P('shard')
- grad_mlp_gain: float32 [1536], P('shard')
- grad_w_gate: float32 [1536, 4096], P('shard')
- grad_w_up: float32 [1536, 4096], P('shard')
- grad_w_down: float32 [4096, 1536], P('shard')
Inputs may be any that keep to these rules, and one draw needn't show every extreme that they name: span_order[s] names each of the 16 spans of sequence s once; slots 2 i and 2 i + 1 hold spans c and 15 - c for some c. Taken in true token order, token_positions[s] starts at 0, rises by 1 to 3 from each token to the next, and the last token of every sequence has position 4094.
All inputs are finite; a program needn't handle non-finite values.
Results may differ from a plain program's by a relative error of at most 0.023.
Values may be sent and summed in bfloat16 or wider, within the bound.
No kernel may reach another device: no remote copies, remote signals or barrier semaphores. Data moves between devices by JAX's collectives and lax.ppermute only.
A program may use at most 320 MiB of HBM per device.

v0:
```python
import jax
import jax.numpy as jnp
from jax import lax
from jax.sharding import PartitionSpec as P

HEADS = 16
KV_HEADS = 8
HEAD_DIM = 96
SPAN = 128


norm_eps = 1e-05
rope_base = 100000.0
masked_value = -1e30


def rms_scale(values):
    return lax.rsqrt(jnp.mean(values * values, axis=-1, keepdims=True) + norm_eps)


def rope_tables(positions):
    half_dim = HEAD_DIM // 2
    frequency = rope_base ** (-2.0 * jnp.arange(half_dim, dtype=jnp.float32) / HEAD_DIM)
    angles = positions.astype(jnp.float32)[..., None] * frequency
    return (jnp.cos(angles), jnp.sin(angles))


def rotate(values, cosine, sine_table):
    half_dim = values.shape[-1] // 2
    first_half = values[..., :half_dim]
    second_half = values[..., half_dim:]
    cosine = cosine[..., None, :]
    sine_table = sine_table[..., None, :]
    return jnp.concatenate(
        [
            first_half * cosine - second_half * sine_table,
            second_half * cosine + first_half * sine_table,
        ],
        axis=-1,
    )


def norm_back(grad_normed, values, scale_rows, gain):
    scaled = grad_normed * gain
    return scale_rows * scaled - values * scale_rows**3 * jnp.mean(
        scaled * values, axis=-1, keepdims=True
    )


def matmul(left, right):
    return jnp.dot(left, right, preferred_element_type=jnp.float32)


def shards(
    tokens,
    span_order,
    token_positions,
    attn_gain,
    w_query,
    w_key,
    w_value,
    w_out,
    mlp_gain,
    w_gate,
    w_up,
    w_down,
    cotangent,
):
    seq_dev, local_len, model_width = tokens.shape
    row_count = seq_dev * local_len
    groups = HEADS // KV_HEADS
    kv_width = KV_HEADS * HEAD_DIM
    score_scale = HEAD_DIM ** (-0.5)
    full_len = local_len * lax.axis_size("ctx")
    ctx_index = lax.axis_index("ctx")
    slot_index = jnp.arange(full_len, dtype=jnp.int32)
    key_index = span_order[:, slot_index // SPAN] * SPAN + slot_index[None, :] % SPAN
    query_index = lax.dynamic_slice_in_dim(key_index, ctx_index * local_len, local_len, 1)
    allowed = query_index[:, :, None] >= key_index[:, None, :]
    cosine, sine_table = rope_tables(token_positions)
    gain_one, wq_full, wk_full, wv_full, wo_full = (
        lax.all_gather(attn_gain, "shard", axis=0, tiled=True),
        lax.all_gather(w_query, "shard", axis=0, tiled=True),
        lax.all_gather(w_key, "shard", axis=0, tiled=True),
        lax.all_gather(w_value, "shard", axis=0, tiled=True),
        lax.all_gather(w_out, "shard", axis=0, tiled=True),
    )
    x_rows = tokens.reshape(row_count, model_width).astype(jnp.float32)
    scale_one = rms_scale(x_rows)
    normed = (x_rows * scale_one * gain_one).astype(jnp.bfloat16)
    queries = rotate(
        matmul(normed, wq_full).reshape(seq_dev, local_len, HEADS, HEAD_DIM), cosine, sine_table
    ).astype(jnp.bfloat16)
    keys_local = rotate(
        matmul(normed, wk_full).reshape(seq_dev, local_len, KV_HEADS, HEAD_DIM), cosine, sine_table
    ).astype(jnp.bfloat16)
    values_local = matmul(normed, wv_full).astype(jnp.bfloat16)
    keys_all, values_all = (
        lax.all_gather(keys_local.reshape(seq_dev, local_len, kv_width), "ctx", axis=1, tiled=True),
        lax.all_gather(
            values_local.reshape(seq_dev, local_len, kv_width), "ctx", axis=1, tiled=True
        ),
    )
    query_heads = queries.reshape(seq_dev, local_len, KV_HEADS, groups, HEAD_DIM).transpose(
        2, 0, 1, 3, 4
    )
    key_heads = keys_all.reshape(seq_dev, full_len, KV_HEADS, HEAD_DIM).transpose(2, 0, 1, 3)
    value_heads = values_all.reshape(seq_dev, full_len, KV_HEADS, HEAD_DIM).transpose(2, 0, 1, 3)

    def scores_of(query_head, key_head):
        raw_scores = (
            jnp.einsum("sqjd,skd->sjqk", query_head, key_head, preferred_element_type=jnp.float32)
            * score_scale
        )
        return jnp.where(allowed[:, None], raw_scores, masked_value)

    def attend_head(pieces):
        query_head, key_head, value_head = pieces
        scores = scores_of(query_head, key_head)
        row_max = jnp.max(scores, axis=-1, keepdims=True)
        exponent = jnp.exp(scores - row_max)
        row_total = jnp.sum(exponent, axis=-1, keepdims=True)
        probabilities = (exponent / row_total).astype(jnp.bfloat16)
        mixed_head = jnp.einsum(
            "sjqk,skd->sqjd", probabilities, value_head, preferred_element_type=jnp.float32
        )
        return (mixed_head, row_max[..., 0] + jnp.log(row_total[..., 0]))

    mixed_heads, log_totals = lax.map(attend_head, (query_heads, key_heads, value_heads))
    mixed_low = (
        mixed_heads.transpose(1, 2, 0, 3, 4).reshape(row_count, model_width).astype(jnp.bfloat16)
    )
    hidden = x_rows + matmul(mixed_low, wo_full)
    scale_two = rms_scale(hidden)
    gain_two, wg_full, wu_full, wd_full = (
        lax.all_gather(mlp_gain, "shard", axis=0, tiled=True),
        lax.all_gather(w_gate, "shard", axis=0, tiled=True),
        lax.all_gather(w_up, "shard", axis=0, tiled=True),
        lax.all_gather(w_down, "shard", axis=0, tiled=True),
    )
    normed_two = (hidden * scale_two * gain_two).astype(jnp.bfloat16)
    gate_pre = matmul(normed_two, wg_full)
    up_pre = matmul(normed_two, wu_full)
    sigmoid_gate = jax.nn.sigmoid(gate_pre)
    activated = gate_pre * sigmoid_gate
    product = (activated * up_pre).astype(jnp.bfloat16)
    layer_out = (hidden + matmul(product, wd_full)).astype(jnp.bfloat16).reshape(tokens.shape)
    grad_out = cotangent.reshape(row_count, model_width)
    gain_two_back, wg_back, wu_back, wd_back = (
        lax.all_gather(mlp_gain, "shard", axis=0, tiled=True),
        lax.all_gather(w_gate, "shard", axis=0, tiled=True),
        lax.all_gather(w_up, "shard", axis=0, tiled=True),
        lax.all_gather(w_down, "shard", axis=0, tiled=True),
    )
    grad_product = matmul(grad_out, wd_back.T)
    grad_w_down = matmul(product.T, grad_out)
    grad_gate = (
        grad_product * up_pre * sigmoid_gate * (1.0 + gate_pre * (1.0 - sigmoid_gate))
    ).astype(jnp.bfloat16)
    grad_up = (grad_product * activated).astype(jnp.bfloat16)
    grad_w_gate = matmul(normed_two.T, grad_gate)
    grad_w_up = matmul(normed_two.T, grad_up)
    grad_normed_two = matmul(grad_gate, wg_back.T) + matmul(grad_up, wu_back.T)
    gain_two_f = gain_two_back.astype(jnp.float32)
    grad_mlp_gain = jnp.sum(grad_normed_two * hidden * scale_two, axis=0)
    grad_hidden = grad_out.astype(jnp.float32) + norm_back(
        grad_normed_two, hidden, scale_two, gain_two_f
    )
    gain_one_back, wq_back, wk_back, wv_back, wo_back = (
        lax.all_gather(attn_gain, "shard", axis=0, tiled=True),
        lax.all_gather(w_query, "shard", axis=0, tiled=True),
        lax.all_gather(w_key, "shard", axis=0, tiled=True),
        lax.all_gather(w_value, "shard", axis=0, tiled=True),
        lax.all_gather(w_out, "shard", axis=0, tiled=True),
    )
    grad_attended = grad_hidden.astype(jnp.bfloat16)
    grad_w_out = matmul(mixed_low.T, grad_attended)
    grad_mixed = matmul(grad_attended, wo_back.T).astype(jnp.bfloat16)
    grad_heads = grad_mixed.reshape(seq_dev, local_len, KV_HEADS, groups, HEAD_DIM).transpose(
        2, 0, 1, 3, 4
    )

    def attend_back(pieces):
        query_head, key_head, value_head, grad_head, log_total = pieces
        scores = scores_of(query_head, key_head)
        probabilities = jnp.exp(scores - log_total[..., None])
        grad_probs = jnp.einsum(
            "sqjd,skd->sjqk", grad_head, value_head, preferred_element_type=jnp.float32
        )
        inner_sum = jnp.sum(probabilities * grad_probs, axis=-1, keepdims=True)
        grad_scores = (probabilities * (grad_probs - inner_sum)).astype(jnp.bfloat16)
        grad_query = (
            jnp.einsum("sjqk,skd->sqjd", grad_scores, key_head, preferred_element_type=jnp.float32)
            * score_scale
        )
        grad_key = (
            jnp.einsum(
                "sjqk,sqjd->skd", grad_scores, query_head, preferred_element_type=jnp.float32
            )
            * score_scale
        )
        grad_value = jnp.einsum(
            "sjqk,sqjd->skd",
            probabilities.astype(jnp.bfloat16),
            grad_head,
            preferred_element_type=jnp.float32,
        )
        return (grad_query, grad_key, grad_value)

    grad_queries, key_terms, value_terms = lax.map(
        attend_back, (query_heads, key_heads, value_heads, grad_heads, log_totals)
    )
    key_terms = key_terms.transpose(1, 2, 0, 3).reshape(seq_dev, full_len, kv_width)
    value_terms = value_terms.transpose(1, 2, 0, 3).reshape(seq_dev, full_len, kv_width)
    grad_keys, grad_values = (
        lax.psum_scatter(
            key_terms.astype(jnp.bfloat16), "ctx", scatter_dimension=1, tiled=True
        ).astype(jnp.float32),
        lax.psum_scatter(
            value_terms.astype(jnp.bfloat16), "ctx", scatter_dimension=1, tiled=True
        ).astype(jnp.float32),
    )
    grad_queries = grad_queries.transpose(1, 2, 0, 3, 4).reshape(
        seq_dev, local_len, HEADS, HEAD_DIM
    )
    grad_q_low = (
        rotate(grad_queries, cosine, -sine_table)
        .reshape(row_count, model_width)
        .astype(jnp.bfloat16)
    )
    grad_k_low = (
        rotate(grad_keys.reshape(seq_dev, local_len, KV_HEADS, HEAD_DIM), cosine, -sine_table)
        .reshape(row_count, kv_width)
        .astype(jnp.bfloat16)
    )
    grad_v_low = grad_values.reshape(row_count, kv_width).astype(jnp.bfloat16)
    grad_w_query = matmul(normed.T, grad_q_low)
    grad_w_key = matmul(normed.T, grad_k_low)
    grad_w_value = matmul(normed.T, grad_v_low)
    grad_normed = (
        matmul(grad_q_low, wq_back.T)
        + matmul(grad_k_low, wk_back.T)
        + matmul(grad_v_low, wv_back.T)
    )
    gain_one_f = gain_one_back.astype(jnp.float32)
    grad_attn_gain = jnp.sum(grad_normed * x_rows * scale_one, axis=0)
    grad_tokens = (grad_hidden + norm_back(grad_normed, x_rows, scale_one, gain_one_f)).astype(
        jnp.bfloat16
    )
    grad_tokens = grad_tokens.reshape(tokens.shape)
    part_gain_two, part_gate, part_up, part_down = (
        lax.psum_scatter(
            grad_mlp_gain.astype(jnp.bfloat16), "shard", scatter_dimension=0, tiled=True
        ).astype(jnp.float32),
        lax.psum_scatter(
            grad_w_gate.astype(jnp.bfloat16), "shard", scatter_dimension=0, tiled=True
        ).astype(jnp.float32),
        lax.psum_scatter(
            grad_w_up.astype(jnp.bfloat16), "shard", scatter_dimension=0, tiled=True
        ).astype(jnp.float32),
        lax.psum_scatter(
            grad_w_down.astype(jnp.bfloat16), "shard", scatter_dimension=0, tiled=True
        ).astype(jnp.float32),
    )
    part_gain_one, part_query, part_key, part_value, part_out = (
        lax.psum_scatter(
            grad_attn_gain.astype(jnp.bfloat16), "shard", scatter_dimension=0, tiled=True
        ).astype(jnp.float32),
        lax.psum_scatter(
            grad_w_query.astype(jnp.bfloat16), "shard", scatter_dimension=0, tiled=True
        ).astype(jnp.float32),
        lax.psum_scatter(
            grad_w_key.astype(jnp.bfloat16), "shard", scatter_dimension=0, tiled=True
        ).astype(jnp.float32),
        lax.psum_scatter(
            grad_w_value.astype(jnp.bfloat16), "shard", scatter_dimension=0, tiled=True
        ).astype(jnp.float32),
        lax.psum_scatter(
            grad_w_out.astype(jnp.bfloat16), "shard", scatter_dimension=0, tiled=True
        ).astype(jnp.float32),
    )
    summed = (
        lax.psum(part_gain_one.astype(jnp.bfloat16), ("ctx", "batch")).astype(jnp.float32),
        lax.psum(part_query.astype(jnp.bfloat16), ("ctx", "batch")).astype(jnp.float32),
        lax.psum(part_key.astype(jnp.bfloat16), ("ctx", "batch")).astype(jnp.float32),
        lax.psum(part_value.astype(jnp.bfloat16), ("ctx", "batch")).astype(jnp.float32),
        lax.psum(part_out.astype(jnp.bfloat16), ("ctx", "batch")).astype(jnp.float32),
        lax.psum(part_gain_two.astype(jnp.bfloat16), ("ctx", "batch")).astype(jnp.float32),
        lax.psum(part_gate.astype(jnp.bfloat16), ("ctx", "batch")).astype(jnp.float32),
        lax.psum(part_up.astype(jnp.bfloat16), ("ctx", "batch")).astype(jnp.float32),
        lax.psum(part_down.astype(jnp.bfloat16), ("ctx", "batch")).astype(jnp.float32),
    )
    return (
        layer_out,
        grad_tokens,
        summed[0],
        summed[1],
        summed[2],
        summed[3],
        summed[4],
        summed[5],
        summed[6],
        summed[7],
        summed[8],
    )


def solution(mesh):
    in_specs = (
        P(("shard", "batch"), "ctx", None),
        P(("shard", "batch"), None),
        P(("shard", "batch"), "ctx"),
        P("shard"),
        P("shard", None),
        P("shard", None),
        P("shard", None),
        P("shard", None),
        P("shard"),
        P("shard", None),
        P("shard", None),
        P("shard", None),
        P(("shard", "batch"), "ctx", None),
    )
    out_specs = (
        P(("shard", "batch"), "ctx", None),
        P(("shard", "batch"), "ctx", None),
        P("shard"),
        P("shard", None),
        P("shard", None),
        P("shard", None),
        P("shard", None),
        P("shard"),
        P("shard", None),
        P("shard", None),
        P("shard", None),
    )
    return jax.shard_map(shards, mesh=mesh, in_specs=in_specs, out_specs=out_specs, check_vma=False)
```

profile of v0, /device:TPU:0, one launch (start us, length us, event | category | flops | bytes accessed | tf_op | source)
XLA Modules:
  0.0 2852.4 jit_solution(10242920798495159735)
XLA Ops:
  10.1 13.5 all-gather
  28.8 34.0 %all-gather.12.cloned.1.call-done = bf16[1536,768]{1,0:T(8,128)(2,1)} async-done(((bf16[384,768]{1,0:T(8,128)(2,1)}), bf16[1536,768]{1,0:T(8,128)(2,1)}) %all-gather.12.cloned.1.call-update) | async-done | bytes 2359312 | tf_op jit(solution)/shard_map/all_gather | solution.py:85
  75.8 37.9 %all-gather.16.cloned.1.call-done = bf16[1536,768]{1,0:T(8,128)(2,1)} async-done(((bf16[384,768]{1,0:T(8,128)(2,1)}), bf16[1536,768]{1,0:T(8,128)(2,1)}) %all-gather.16.cloned.1.call-update) | async-done | bytes 2359312 | tf_op jit(solution)/shard_map/all_gather | solution.py:84
  147.8 13.0 all-gather.1
  162.8 40.9 %all-gather.20.cloned.1.call-done = bf16[1536,1536]{1,0:T(8,128)(2,1)} async-done(((bf16[384,1536]{1,0:T(8,128)(2,1)}), bf16[1536,1536]{1,0:T(8,128)(2,1)}) %all-gather.20.cloned.1.call-update) | async-done | bytes 4718608 | tf_op jit(solution)/shard_map/all_gather | solution.py:83
  222.0 28.4 all-gather.14.cloned.1.call-done
  257.1 41.8 %all-gather.18.cloned.1.call-done = bf16[2,2048,768]{1,2,0:T(8,128)(2,1)} async-done(((bf16[2,512,768]{1,2,0:T(8,128)(2,1)}), bf16[2,2048,768]{1,2,0:T(8,128)(2,1)}) %all-gather.18.cloned.1.call-update) | async-done | bytes 6291472 | tf_op jit(solution)/shard_map/all_gather | solution.py:99
  305.5 139.3 %while.30 = (s32[]{:T(128)}, bf16[8,2,512,2,96]{2,4,3,1,0:T(8,128)(2,1)S(1)}, f32[8,2,2,512]{3,2,1,0:T(2,128)}, bf16[8,2,2048,96]{2,3,1,0:T(8,128)(2,1)}, bf16[8...) while((s32[]{:T(128)}, ...), condition=%wide.region_4.5_spmd.clone.clone, body=%wide.region_1.4_spmd.clone.sunk.clone | while | flops 1663039488 | bytes 61560928 | solution.py:129
  466.2 141.9 %all-gather.24.cloned.1.call-done = bf16[1536,4096]{1,0:T(8,128)(2,1)} async-done(((bf16[384,4096]{1,0:T(8,128)(2,1)}), bf16[1536,4096]{1,0:T(8,128)(2,1)}) %all-gather.24.cloned.1.call-update) | async-done | bytes 12582928 | tf_op jit(solution)/shard_map/all_gather | solution.py:137
  608.1 19.4 fusion.82
  627.5 198.6 %all-gather.26.cloned.1.call-done = bf16[1536,4096]{1,0:T(8,128)(2,1)} async-done(((bf16[384,4096]{1,0:T(8,128)(2,1)}), bf16[1536,4096]{1,0:T(8,128)(2,1)}) %all-gather.26.cloned.1.call-update) | async-done | bytes 12582928 | tf_op jit(solution)/shard_map/all_gather | solution.py:138
  826.1 20.8 fusion.83
  846.9 197.2 %all-gather.28.cloned.1.call-done = bf16[4096,1536]{1,0:T(8,128)(2,1)} async-done(((bf16[1024,1536]{1,0:T(8,128)(2,1)}), bf16[4096,1536]{1,0:T(8,128)(2,1)}) %all-gather.28.cloned.1.call-update) | async-done | bytes 12582928 | tf_op jit(solution)/shard_map/all_gather | solution.py:139
  1044.1 32.2 %multiply_convert_fusion = (bf16[1024,4096]{1,0:T(8,128)(2,1)}, bf16[1024,4096]{1,0:T(8,128)(2,1)}, bf16[1024,4096]{1,0:T(8,128)(2,1)}) fusion(f32[1024,4096]{1,0:T(8,128)} %fusion.82, f32[1024,4096]{1,0:T(8,128)} %fusion.83, bf16[1024,1536]{1,0:T(8,128)(2,1)} %bitcast.371, bf16[4096,1536]{1,0:T(8,128)(2,1)} %all-gather.28.cloned.1.call-done), kind=kOutput, calls=%fused_computation.66 | convolution fusion | flops 12947816448 | bytes 74448896 | tf_op jit(solution)/shard_map/dot_general | solution.py:51
  1076.3 19.6 fusion.84
  1096.0 21.0 multiply_reduce_fusion
  1135.7 465.1 %while.31 = (s32[]{:T(128)}, f32[8,2,512,2,96]{2,4,3,1,0:T(8,128)}, bf16[8,2,2048,96]{2,3,0,1:T(8,128)(2,1)}, bf16[8,2,2048,96]{2,3,0,1:T(8,128)(2,1)}, bf16[8,2...) while((s32[]{:T(128)}, f32[8,2,512,2,96]{2,4,3,1,0:T(8,128)}, ...), condition=%wide.region_9.10_spmd.clone.clone, body=%wide.region_7.9_spmd.clone.sunk.clone | while | flops 4092131328 | bytes 226835760 | solution.py:210
  1219.1 13.0 fusion.175
  1630.2 27.3 reduce-scatter.10.cloned.1.call-done
  1667.2 51.3 %reduce-scatter.12.cloned.1.call-done = bf16[2,512,768]{1,2,0:T(8,128)(2,1)} async-done(((bf16[2,2048,768]{1,2,0:T(8,128)(2,1)}), bf16[2,512,768]{1,2,0:T(8,128)(2,1)}) %reduce-scatter.12.cloned.1.call-update) | async-done | bytes 1572880 | tf_op jit(solution)/shard_map/reduce_scatter | solution.py:219
  1725.1 20.1 convolution_convert_fusion.2
  1745.4 19.1 convolution_convert_fusion.1
  1766.5 19.1 convolution_convert_fusion
  1806.6 88.1 %reduce-scatter.20.cloned.1.call-done = bf16[384,1536]{1,0:T(8,128)(2,1)} async-done(((bf16[1536,1536]{1,0:T(8,128)(2,1)}), bf16[384,1536]{1,0:T(8,128)(2,1)}) %reduce-scatter.20.cloned.1.call-update) | async-done | bytes 1179664 | tf_op jit(solution)/shard_map/reduce_scatter | solution.py:278
  1894.7 51.3 %reduce-scatter.16.cloned.1.call-done = bf16[384,768]{1,0:T(8,128)(2,1)} async-done(((bf16[1536,768]{1,0:T(8,128)(2,1)}), bf16[384,768]{1,0:T(8,128)(2,1)}) %reduce-scatter.16.cloned.1.call-update) | async-done | bytes 589840 | tf_op jit(solution)/shard_map/reduce_scatter | solution.py:272
  1946.0 50.3 %reduce-scatter.18.cloned.1.call-done = bf16[384,768]{1,0:T(8,128)(2,1)} async-done(((bf16[1536,768]{1,0:T(8,128)(2,1)}), bf16[384,768]{1,0:T(8,128)(2,1)}) %reduce-scatter.18.cloned.1.call-update) | async-done | bytes 589840 | tf_op jit(solution)/shard_map/reduce_scatter | solution.py:275
  1996.3 213.6 %reduce-scatter.22.cloned.1.call-done = bf16[384,4096]{1,0:T(8,128)(2,1)} async-done(((bf16[1536,4096]{1,0:T(8,128)(2,1)}), bf16[384,4096]{1,0:T(8,128)(2,1)}) %reduce-scatter.22.cloned.1.call-update) | async-done | bytes 3145744 | tf_op jit(solution)/shard_map/reduce_scatter | solution.py:255
  2209.9 215.1 %reduce-scatter.24.cloned.1.call-done = bf16[384,4096]{1,0:T(8,128)(2,1)} async-done(((bf16[1536,4096]{1,0:T(8,128)(2,1)}), bf16[384,4096]{1,0:T(8,128)(2,1)}) %reduce-scatter.24.cloned.1.call-update) | async-done | bytes 3145744 | tf_op jit(solution)/shard_map/reduce_scatter | solution.py:258
  2425.1 215.1 %reduce-scatter.26.cloned.1.call-done = bf16[1024,1536]{1,0:T(8,128)(2,1)} async-done(((bf16[4096,1536]{1,0:T(8,128)(2,1)}), bf16[1024,1536]{1,0:T(8,128)(2,1)}) %reduce-scatter.26.cloned.1.call-update) | async-done | bytes 3145744 | tf_op jit(solution)/shard_map/reduce_scatter | solution.py:261
  2640.2 19.9 add_convert_fusion
  2686.4 14.9 all-reduce.2
  2709.5 116.1 %all-reduce.7.cloned.1.call-done = (bf16[384,1536]{1,0:T(8,128)(2,1)}, bf16[384,768]{1,0:T(8,128)(2,1)}, bf16[384,768]{1,0:T(8,128)(2,1)}, bf16[384,1536]{1,0:T(...) async-done(((bf16[384,1536]{1,0:T(8,128)(2,1)}, bf16[384,768]{1,0:T(8,128)(2,1)}, bf16[384,768]{1,0:T(8,128)(2,1)}, ...) | async-done | bytes 12976144 | tf_op jit(solution)/shard_map/psum | solution.py:284
  (415 shorter events, 840.8 us)
Async XLA Ops:
  7.2 55.6 %all-gather.12.cloned.1.call-start = ((), (), s32[]{:S(2)}) async-start(), calls=%async_computation.9 | async-start | bytes 2949120 | tf_op jit(solution)/shard_map/all_gather | solution.py:85
  7.9 105.8 %all-gather.16.cloned.1.call-start = ((), (), s32[]{:S(2)}) async-start(), calls=%async_computation.11 | async-start | bytes 2949120 | tf_op jit(solution)/shard_map/all_gather | solution.py:84
  8.7 195.0 %all-gather.20.cloned.1.call-start = ((), (), s32[]{:S(2)}) async-start(), calls=%async_computation.13 | async-start | bytes 5898240 | tf_op jit(solution)/shard_map/all_gather | solution.py:83
  9.4 241.0 %all-gather.14.cloned.1.call-start = ((), (), s32[]{:S(2)}) async-start(), calls=%async_computation.10 | async-start | bytes 7864320 | tf_op jit(solution)/shard_map/all_gather | solution.py:100
  23.7 49.7 %copy-start.31 = (f32[1536]{0:T(1024)}, f32[1536]{0:T(1024)S(1)}, u32[]{:S(2)}) copy-start(f32[1536]{0:T(1024)S(1)} %reshape.326) | copy-start | bytes 18436
  26.3 42.9 %copy-start.33 = (f32[1,4,2,128]{3,1,2,0:T(4,128)}, f32[1,4,2,128]{3,1,2,0:T(4,128)S(1)}, u32[]{:S(2)}) copy-start(f32[1,4,2,128]{3,1,2,0:T(4,128)S(1)} %copy.151) | copy-start | bytes 12292
  28.8 43.1 %copy-start.40 = (s32[2,512]{1,0:T(2,128)S(1)}, s32[2,512]{1,0:T(2,128)}, u32[]{:S(2)}) copy-start(s32[2,512]{1,0:T(2,128)} %param.19) | copy-start | bytes 12292
  71.8 227.0 %all-gather.18.cloned.1.call-start = ((), (), s32[]{:S(2)}) async-start(), calls=%async_computation.12 | async-start | bytes 7864320 | tf_op jit(solution)/shard_map/all_gather | solution.py:99
  73.4 145.5 %copy-start.8 = (f32[2,512,48]{1,2,0:T(8,128)}, f32[2,512,48]{1,2,0:T(8,128)S(1)}, u32[]{:S(2)}) copy-start(f32[2,512,48]{1,2,0:T(8,128)S(1)} %get-tuple-element.300) | copy-start | bytes 589828
  122.9 331.4 %all-gather.22.cloned.1.call-start = ((), (), s32[]{:S(2)}) async-start(), calls=%async_computation.14 | async-start | bytes 5898240 | tf_op jit(solution)/shard_map/all_gather | solution.py:86
  123.5 484.5 %all-gather.24.cloned.1.call-start = ((), (), s32[]{:S(2)}) async-start(), calls=%async_computation.15 | async-start | bytes 15728640 | tf_op jit(solution)/shard_map/all_gather | solution.py:137
  124.3 701.8 %all-gather.26.cloned.1.call-start = ((), (), s32[]{:S(2)}) async-start(), calls=%async_computation.16 | async-start | bytes 15728640 | tf_op jit(solution)/shard_map/all_gather | solution.py:138
  125.0 919.1 %all-gather.28.cloned.1.call-start = ((), (), s32[]{:S(2)}) async-start(), calls=%async_computation.17 | async-start | bytes 15728640 | tf_op jit(solution)/shard_map/all_gather | solution.py:139
  125.8 1531.7 %reduce-scatter.10.cloned.1.call-start = ((), (), s32[]{:S(2)}) async-start(), calls=%async_computation.18 | async-start | bytes 7864320 | tf_op jit(solution)/shard_map/reduce_scatter | solution.py:216
  466.2 161.3 %copy-start.10 = (bf16[1024,1536]{1,0:T(8,128)(2,1)}, bf16[1024,1536]{1,0:T(8,128)(2,1)S(1)}, u32[]{:S(2)}) copy-start(bf16[1024,1536]{1,0:T(8,128)(2,1)S(1)} %multiply_convert_fusion.3) | copy-start | bytes 9437188
  826.1 269.9 %slice-start.4 = ((s8[6291456]{0:T(1024)(128)(4,1)}), s8[2097152]{0:T(1024)(128)(4,1)S(1)}, s32[]{:S(2)}) async-start(s8[6291456]{0:T(1024)(128)(4,1)} %bitcast.347), calls=%async_computation.32 | async-start | bytes 4194304
  1044.1 51.9 %slice-start.5 = ((s8[6291456]{0:T(1024)(128)(4,1)}), s8[4194304]{0:T(1024)(128)(4,1)S(1)}, s32[]{:S(2)}) async-start(s8[6291456]{0:T(1024)(128)(4,1)} %bitcast.347), calls=%async_computation.33 | async-start | bytes 8388608
  1335.4 27.0 slice-start
  1335.4 27.0 slice-start.1
  1335.4 27.0 slice-start.2
  1567.8 27.0 slice-start
  1567.8 27.0 slice-start.1
  1600.8 117.8 %reduce-scatter.12.cloned.1.call-start = ((), (), s32[]{:S(2)}) async-start(), calls=%async_computation.19 | async-start | bytes 7864320 | tf_op jit(solution)/shard_map/reduce_scatter | solution.py:219
  1601.5 205.1 %reduce-scatter.14.cloned.1.call-start = ((), (), s32[]{:S(2)}) async-start(), calls=%async_computation.20 | async-start | bytes 5898240 | tf_op jit(solution)/shard_map/reduce_scatter | solution.py:269
  1620.0 274.8 %reduce-scatter.20.cloned.1.call-start = ((), (), s32[]{:S(2)}) async-start(), calls=%async_computation.23 | async-start | bytes 5898240 | tf_op jit(solution)/shard_map/reduce_scatter | solution.py:278
  1630.0 316.0 %reduce-scatter.16.cloned.1.call-start = ((), (), s32[]{:S(2)}) async-start(), calls=%async_computation.21 | async-start | bytes 2949120 | tf_op jit(solution)/shard_map/reduce_scatter | solution.py:272
  1667.2 57.9 %copy-start.11 = (bf16[1024,1536]{1,0:T(8,128)(2,1)S(1)}, bf16[1024,1536]{1,0:T(8,128)(2,1)}, u32[]{:S(2)}) copy-start(bf16[1024,1536]{1,0:T(8,128)(2,1)} %copy-done.10) | copy-start | bytes 9437188
  1667.2 329.1 %reduce-scatter.18.cloned.1.call-start = ((), (), s32[]{:S(2)}) async-start(), calls=%async_computation.22 | async-start | bytes 2949120 | tf_op jit(solution)/shard_map/reduce_scatter | solution.py:275
  1725.0 484.9 %reduce-scatter.22.cloned.1.call-start = ((), (), s32[]{:S(2)}) async-start(), calls=%async_computation.24 | async-start | bytes 15728640 | tf_op jit(solution)/shard_map/reduce_scatter | solution.py:255
  1745.2 679.9 %reduce-scatter.24.cloned.1.call-start = ((), (), s32[]{:S(2)}) async-start(), calls=%async_computation.25 | async-start | bytes 15728640 | tf_op jit(solution)/shard_map/reduce_scatter | solution.py:258
  1764.6 875.6 %reduce-scatter.26.cloned.1.call-start = ((), (), s32[]{:S(2)}) async-start(), calls=%async_computation.26 | async-start | bytes 15728640 | tf_op jit(solution)/shard_map/reduce_scatter | solution.py:261
  1785.6 1040.1 %all-reduce.7.cloned.1.call-start = ((), (), s32[]{:S(2)}) async-start(), calls=%async_computation.27 | async-start | bytes 25952256 | tf_op jit(solution)/shard_map/psum | solution.py:284
  (72 other events, 894.5 us)
Sparse Core Ops, SparseCore 0:
  9.6 53.1 all-gather.11
  64.4 49.2 all-gather.15
  115.3 88.3 all-gather.19
  205.6 44.7 all-gather.13
  252.4 46.3 all-gather.17
  300.3 89.4 all-gather.21
  391.3 216.7 all-gather.23
  609.6 216.3 all-gather.25
  827.6 216.3 all-gather.27
  1600.9 56.5 reduce-scatter.9
  1660.2 58.3 reduce-scatter.11
  1721.3 85.2 reduce-scatter.13
  1808.9 85.7 reduce-scatter.19
  1897.4 48.5 reduce-scatter.15
  1948.7 47.5 reduce-scatter.17
  1998.5 211.3 reduce-scatter.21
  2212.1 212.8 reduce-scatter.23
  2427.3 212.8 reduce-scatter.25
  2645.2 180.4 all-reduce.6
where the time goes:
time: 2860 us; the launch traced here: 2850 us
  waiting for transfers between devices  1760 us (62%)
  matrix products  674 us (24%)
  other arithmetic  219 us (8%)
  local copies, waits for them, and re-layouts  123 us (4%)
  blocking collectives  53.1 us (2%)
    dot_general x21, matrix products, matmul(): return jnp.dot(left, right, preferred_element_type=jnp.float32)  275 us
    reduce_scatter x1, waiting for transfers between devices, shards(): lax.psum_scatter(grad_w_down.astype(jnp.bfloat16), 'shard', scatter_dimen...  215 us
    reduce_scatter x1, waiting for transfers between devices, shards(): lax.psum_scatter(grad_w_up.astype(jnp.bfloat16), 'shard', scatter_dimensi...  215 us
    reduce_scatter x1, waiting for transfers between devices, shards(): lax.psum_scatter(grad_w_gate.astype(jnp.bfloat16), 'shard', scatter_dimen...  214 us
    all_gather x1, waiting for transfers between devices, shards(): lax.all_gather(w_up, 'shard', axis=0, tiled=True)  199 us
    all_gather x1, waiting for transfers between devices, shards(): lax.all_gather(w_down, 'shard', axis=0, tiled=True)  197 us
    all_gather x1, waiting for transfers between devices, shards(): lax.all_gather(w_gate, 'shard', axis=0, tiled=True)  142 us
    psum x1, waiting for transfers between devices, shards(): lax.psum(part_query.astype(jnp.bfloat16), ('ctx', 'batch'))  116 us
  transfers between devices with their start and end apart: 19, of which 18 were waited for; matrix products, arithmetic and copies ran while one was open for 15% of the time, Pallas kernels for 0%

commit v1 on v0

--- a/solution.py
+++ b/solution.py
@@ -1,21 +1,1192 @@
+import functools
+
 import jax
 import jax.numpy as jnp
+import numpy as np
 from jax import lax
+from jax.experimental import pallas as pl
+from jax.experimental.pallas import tpu as pltpu
 from jax.sharding import PartitionSpec as P
 
 HEADS = 16
 KV_HEADS = 8
 HEAD_DIM = 96
 SPAN = 128
-
+GROUPS = HEADS // KV_HEADS
+HALF = HEAD_DIM // 2
+LANES = 128
+SLOT = LANES // 2
+GROUP_COLS = (GROUPS + 2) * HEAD_DIM
+Q_COLS = GROUPS * HEAD_DIM
+Q_LANES = GROUPS * LANES
+PAD_ROWS = 16
 
 norm_eps = 1e-05
 rope_base = 100000.0
 masked_value = -1e30
+score_scale = HEAD_DIM ** (-0.5)
+exp2_scale = score_scale * 1.4426950408889634
+
+bf16 = jnp.bfloat16
+f32 = jnp.float32
+MIB = 1 << 20
+NT = (((1,), (1,)), ((), ()))
+TN = (((0,), (0,)), ((), ()))
 
 
 def rms_scale(values):
     return lax.rsqrt(jnp.mean(values * values, axis=-1, keepdims=True) + norm_eps)
+
+
+def matmul(left, right):
+    return jnp.dot(left, right, preferred_element_type=f32)
+
+
+def dot_nt(left, right):
+    return lax.dot_general(left, right, NT, preferred_element_type=f32)
+
+
+def dot_tn(left, right):
+    return lax.dot_general(left, right, TN, preferred_element_type=f32)
+
+
+def params(limit=60):
+    return pltpu.CompilerParams(vmem_limit_bytes=limit * MIB)
+
+
+def short():
+    return pl.CostEstimate(flops=1000, bytes_accessed=1000, transcendentals=0)
+
+
+def whole(shape):
+    return pl.BlockSpec(shape, lambda *_: (0,) * len(shape))
+
+
+def part(block, index):
+    return pl.BlockSpec(block, lambda *_: index)
+
+
+def call(kernel, grid, in_specs, out_specs, out_shape, operands, name, prefetch=(), scratch=()):
+    return pl.pallas_call(
+        kernel,
+        grid_spec=pltpu.PrefetchScalarGridSpec(
+            num_scalar_prefetch=len(prefetch), grid=grid, in_specs=in_specs, out_specs=out_specs, scratch_shapes=list(scratch)
+        ),
+        out_shape=[jax.ShapeDtypeStruct(shape, dtype) for shape, dtype in out_shape],
+        compiler_params=params(),
+        cost_estimate=short(),
+        name=name,
+    )(*prefetch, *operands)
+
+
+def spread_matrix():
+    spread = np.zeros((GROUP_COLS, (GROUPS + 2) * LANES), np.float32)
+    for row in range(spread.shape[0]):
+        head, feature = divmod(row, HEAD_DIM)
+        half, place = divmod(feature, HALF)
+        spread[row, head * LANES + half * SLOT + place] = 1.0
+    return spread
+
+
+def front_kernel(near_ref, far_ref, flag_ref, *refs):
+    spans = 4
+    near, far, refs = refs[:spans], refs[spans : 2 * spans], refs[2 * spans :]
+    cos_ref, sin_ref, gain_ref, spread_ref, w0, w1, w2, w3a, w3b, x_out, n_out, nt_out, q_out, k_out, v_out, w_out = refs
+    q_width, k_width = q_out.shape[1], k_out.shape[1]
+    step_at = pl.program_id(0)
+
+    @pl.when(step_at == 0)
+    def _():
+        depth = w0.shape[1]
+        halves = w3a.shape[0]
+        for at, piece in enumerate((w0, w1, w2, None)):
+            for z in range(w0.shape[0]):
+                block = piece[z] if piece is not None else (w3a[z] if z < halves else w3b[z - halves])
+                spread = matmul(block, spread_ref[...]).astype(bf16)
+                rows = slice(z * depth, (z + 1) * depth)
+                w_out[rows, Q_LANES * at : Q_LANES * (at + 1)] = spread[:, :Q_LANES]
+                w_out[rows, q_width + LANES * at : q_width + LANES * (at + 1)] = spread[:, Q_LANES : Q_LANES + LANES]
+                at_v = q_width + k_width + LANES * at
+                w_out[rows, at_v : at_v + LANES] = spread[:, Q_LANES + LANES :]
+
+    for k in range(spans):
+        rows = slice(k * SPAN, (k + 1) * SPAN)
+
+        @pl.when(flag_ref[spans * step_at + k] == 0)
+        def _():
+            x_out[rows, :] = near[k][0]
+
+        @pl.when(flag_ref[spans * step_at + k] != 0)
+        def _():
+            x_out[rows, :] = far[k][0]
+
+    x = x_out[...].astype(f32)
+    normed = (x * rms_scale(x) * gain_ref[...]).astype(bf16)
+    n_out[...] = normed
+    nt_out[...] = normed.T
+    cosine, sine = cos_ref[...], sin_ref[...]
+    lane = lax.broadcasted_iota(jnp.int32, (1, LANES), 1)
+    ones = jnp.where((lane >= HALF) & (lane < HALF + 3), 1.0, 0.0)
+    step = 4 * LANES
+    for start in range(0, w_out.shape[1], step):
+        raw = matmul(normed, w_out[:, start : start + step])
+        for piece in range(0, step, LANES):
+            at = start + piece
+            head = raw[:, piece : piece + LANES]
+            if at < q_width + k_width:
+                head = head * cosine + pltpu.roll(head, SLOT, 1) * sine
+            if at < q_width:
+                q_out[:, at : at + LANES] = head.astype(bf16)
+            elif at < q_width + k_width:
+                k_out[:, at - q_width : at - q_width + LANES] = (head + ones).astype(bf16)
+            else:
+                v_out[:, at - q_width - k_width : at - q_width - k_width + LANES] = (head + ones).astype(bf16)
+
+
+def span_specs(width, count):
+    def near(k):
+        return pl.BlockSpec((1, SPAN, width), lambda i, near, far, flag: (near[count * i + k], 0, 0))
+
+    def far(k):
+        return pl.BlockSpec((1, SPAN, width), lambda i, near, far, flag: (far[count * i + k], 0, 0))
+
+    return [near(k) for k in range(count)] + [far(k) for k in range(count)]
+
+
+def as_spans(array):
+    return array.reshape(array.shape[0] // SPAN, SPAN, array.shape[1])
+
+
+def front(places, near, far, cosine, sine, gain, pieces):
+    rows, width = 2 * near.shape[0], near.shape[1]
+    groups = len(pieces) - 1
+    n_shard = pieces[0].shape[0]
+    depth = width // n_shard
+    spread = jnp.asarray(spread_matrix(), bf16)
+    spans = 4
+    tile = spans * SPAN
+    q_width, k_width = groups * Q_LANES, groups * LANES
+    total = q_width + 2 * k_width
+
+    def rows_spec(cols):
+        return pl.BlockSpec((tile, cols), lambda i, *_: (i, 0))
+
+    near, far = as_spans(near), as_spans(far)
+    return call(
+        front_kernel,
+        (rows // tile,),
+        span_specs(width, spans)
+        + [rows_spec(LANES), rows_spec(LANES), whole(gain.shape), whole(spread.shape)]
+        + [part((p.shape[0], depth, p.shape[2]), (0, 0, 0)) for p in pieces],
+        [rows_spec(width), rows_spec(width), pl.BlockSpec((width, tile), lambda i, *_: (0, i))]
+        + [rows_spec(q_width), rows_spec(k_width), rows_spec(k_width), whole((n_shard * depth, total))],
+        [
+            ((rows, width), bf16),
+            ((rows, width), bf16),
+            ((width, rows), bf16),
+            ((rows, q_width), bf16),
+            ((rows, k_width), bf16),
+            ((rows, k_width), bf16),
+            ((n_shard * depth, total), bf16),
+        ],
+        [near] * spans + [far] * spans + [cosine, sine, gain, spread, *pieces],
+        "front",
+        places,
+    )
+
+
+def span_copy(places, source):
+    width = source.shape[1]
+    count = places.shape[0]
+
+    def kernel(place_ref, x_ref, o_ref):
+        o_ref[...] = x_ref[...]
+
+    (out,) = call(
+        kernel,
+        (count,),
+        [pl.BlockSpec((1, SPAN, width), lambda i, place: (place[i], 0, 0))],
+        [pl.BlockSpec((1, SPAN, width), lambda i, place: (i, 0, 0))],
+        [((count, SPAN, width), source.dtype)],
+        [as_spans(source)],
+        "span_copy",
+        [places],
+    )
+    return out.reshape(count * SPAN, width)
+
+
+def span_join(places, near, far):
+    width = near.shape[1]
+    count = 2 * near.shape[0] // SPAN
+
+    def kernel(near_ref, far_ref, flag_ref, a_ref, b_ref, o_ref):
+        @pl.when(flag_ref[pl.program_id(0)] == 0)
+        def _():
+            o_ref[...] = a_ref[...]
+
+        @pl.when(flag_ref[pl.program_id(0)] != 0)
+        def _():
+            o_ref[...] = b_ref[...]
+
+    (out,) = call(
+        kernel,
+        (count,),
+        span_specs(width, 1),
+        [pl.BlockSpec((1, SPAN, width), lambda i, *_: (i, 0, 0))],
+        [((count, SPAN, width), near.dtype)],
+        [as_spans(near), as_spans(far)],
+        "span_join",
+        places,
+    )
+    return out.reshape(count * SPAN, width)
+
+
+def three_parts(values):
+    first = values.astype(bf16).astype(f32)
+    second = (values - first).astype(bf16).astype(f32)
+    third = values - first - second
+    return first, second, third
+
+
+def with_lanes(block, column):
+    lane = lax.broadcasted_iota(jnp.int32, block.shape, 1)
+    first, second, third = three_parts(column)
+    wide = block.astype(f32)
+    wide = jnp.where(lane == HALF, first, wide)
+    wide = jnp.where(lane == HALF + 1, second, wide)
+    wide = jnp.where(lane == HALF + 2, third, wide)
+    return wide.astype(bf16)
+
+
+Q_TILE = 256
+K_CHUNK = 512
+
+
+def heads_down(block):
+    return jnp.concatenate([block[:, LANES * h : LANES * (h + 1)] for h in range(GROUPS)], axis=0)
+
+
+def attend_kernel(q_ref, k_ref, v_ref, mixed_ref, q_aug_ref):
+    rows = q_ref.shape[0]
+    for tile in range(rows // Q_TILE):
+        first_row = tile * Q_TILE
+        query = heads_down(q_ref[first_row : first_row + Q_TILE, :])
+        end = first_row + Q_TILE
+        top = acc = None
+        for start in range(0, end, K_CHUNK):
+            size = min(K_CHUNK, end - start)
+            key = k_ref[start : start + size, :]
+            value = v_ref[start : start + size, :]
+            scores = dot_nt(query, key)
+            if start + size > first_row:
+                row = lax.broadcasted_iota(jnp.int32, (Q_TILE, size), 0) + first_row
+                column = lax.broadcasted_iota(jnp.int32, (Q_TILE, size), 1) + start
+                allowed = row >= column
+                scores = jnp.where(jnp.concatenate([allowed] * GROUPS, axis=0), scores, masked_value)
+            chunk_top = jnp.max(scores, axis=-1, keepdims=True)
+            new_top = chunk_top if top is None else jnp.maximum(top, chunk_top)
+            weights = jnp.exp2((scores - new_top) * exp2_scale).astype(bf16)
+            part = matmul(weights, value)
+            acc = part if top is None else acc * jnp.exp2((top - new_top) * exp2_scale) + part
+            top = new_top
+        total = acc[:, HALF : HALF + 1]
+        mixed = (acc * (1.0 / total)).astype(bf16)
+        log_total = top + jnp.log2(total) * (1.0 / exp2_scale)
+        marked = with_lanes(query, -log_total)
+        for h in range(GROUPS):
+            mixed_ref[first_row : first_row + Q_TILE, LANES * h : LANES * (h + 1)] = mixed[Q_TILE * h : Q_TILE * (h + 1)]
+            q_aug_ref[first_row : first_row + Q_TILE, LANES * h : LANES * (h + 1)] = marked[Q_TILE * h : Q_TILE * (h + 1)]
+
+
+def attend(queries, keys, values):
+    rows, k_width = keys.shape
+    groups = k_width // LANES
+    pair = pl.BlockSpec((rows, Q_LANES), lambda g: (0, g))
+    single = pl.BlockSpec((rows, LANES), lambda g: (0, g))
+    return call(
+        attend_kernel, (groups,), [pair, single, single], [pair, pair], [(queries.shape, bf16)] * 2, [queries, keys, values], "attend"
+    )
+
+
+def attend_back_kernel(q_ref, k_ref, v_ref, do_ref, o_ref, cos_ref, sin_ref, dq_ref, dk_ref, dv_ref, q_s, do_s, dq_s, dk_s, dv_s):
+    rows = q_ref.shape[0]
+    tiles = rows // Q_TILE
+    for tile in range(tiles):
+        at = slice(tile * Q_TILE, (tile + 1) * Q_TILE)
+        q_s[tile] = heads_down(q_ref[at, :])
+        grad = heads_down(do_ref[at, :])
+        inner = jnp.sum(grad.astype(f32) * heads_down(o_ref[at, :]).astype(f32), axis=-1, keepdims=True)
+        do_s[tile] = with_lanes(grad, -inner)
+        dq_s[tile] = jnp.zeros(dq_s.shape[1:], f32)
+
+    def unit(tile, key_start, size, mask_from):
+        key = k_ref[key_start : key_start + size, :]
+        value = v_ref[key_start : key_start + size, :]
+        query, grad = q_s[tile], do_s[tile]
+        probs = jnp.exp2(dot_nt(key, query) * exp2_scale)
+        if mask_from is not None:
+            row = lax.broadcasted_iota(jnp.int32, (size, Q_TILE), 0)
+            column = lax.broadcasted_iota(jnp.int32, (size, Q_TILE), 1) + mask_from
+            allowed = jnp.concatenate([row <= column] * GROUPS, axis=1)
+            probs = jnp.where(allowed, probs, 0.0)
+        d_scores = (probs * dot_nt(value, grad)).astype(bf16)
+        dv_s[:size] += matmul(probs.astype(bf16), grad)
+        dk_s[:size] += matmul(d_scores, query)
+        dq_s[tile] += dot_tn(d_scores, key)
+
+    for key_start in range(0, rows, K_CHUNK):
+        dk_s[...] = jnp.zeros(dk_s.shape, f32)
+        dv_s[...] = jnp.zeros(dv_s.shape, f32)
+        tile = key_start // Q_TILE
+        unit(tile, key_start, Q_TILE, 0)
+        unit(tile + 1, key_start, K_CHUNK, Q_TILE)
+        if tile + 2 < tiles:
+
+            @pl.loop(tile + 2, tiles)
+            def _(later):
+                unit(later, key_start, K_CHUNK, None)
+
+        at = slice(key_start, key_start + K_CHUNK)
+        turned = dk_s[...] * score_scale
+        turned = turned * cos_ref[at, :] - pltpu.roll(turned, SLOT, 1) * sin_ref[at, :]
+        dk_ref[at, :] = turned.astype(bf16)
+        dv_ref[at, :] = dv_s[...].astype(bf16)
+    for tile in range(tiles):
+        at = slice(tile * Q_TILE, (tile + 1) * Q_TILE)
+        cosine, sine = cos_ref[at, :], sin_ref[at, :]
+        for h in range(GROUPS):
+            turned = dq_s[tile, Q_TILE * h : Q_TILE * (h + 1), :] * score_scale
+            turned = turned * cosine - pltpu.roll(turned, SLOT, 1) * sine
+            dq_ref[at, LANES * h : LANES * (h + 1)] = turned.astype(bf16)
+
+
+def attend_back(first, groups, q_aug, keys, values, grad, mixed, cosine, sine):
+    rows = keys.shape[0]
+    tiles = rows // Q_TILE
+    pair = pl.BlockSpec((rows, Q_LANES), lambda g: (0, g + first))
+    single = pl.BlockSpec((rows, LANES), lambda g: (0, g + first))
+    pair_out = pl.BlockSpec((rows, Q_LANES), lambda g: (0, g))
+    single_out = pl.BlockSpec((rows, LANES), lambda g: (0, g))
+    stacked = (tiles, GROUPS * Q_TILE, LANES)
+    table = whole((rows, LANES))
+    return call(
+        attend_back_kernel,
+        (groups,),
+        [pair, single, single, pair, pair, table, table],
+        [pair_out, single_out, single_out],
+        [((rows, groups * Q_LANES), bf16), ((rows, groups * LANES), bf16), ((rows, groups * LANES), bf16)],
+        [q_aug, keys, values, grad, mixed, cosine, sine],
+        "attend_back",
+        scratch=[
+            pltpu.VMEM(stacked, bf16),
+            pltpu.VMEM(stacked, bf16),
+            pltpu.VMEM(stacked, f32),
+            pltpu.VMEM((K_CHUNK, LANES), f32),
+            pltpu.VMEM((K_CHUNK, LANES), f32),
+        ],
+    )
+
+
+def flat(block):
+    return block.reshape(block.shape[0] * block.shape[1], block.shape[2])
+
+
+def down_columns(down_ref, j, zs):
+    rows = down_ref.shape[1] // 3
+    return jnp.concatenate([down_ref[z, rows * j : rows * (j + 1), :] for z in zs], axis=0)
+
+
+def hidden_kernel(n_ref, cot_ref, gate_ref, up_ref, down_ref, product_ref, dboth_ref):
+    n_shard, units = gate_ref.shape[0], gate_ref.shape[2]
+    third = cot_ref.shape[1] // 3
+    step = 256
+    for start in range(0, units, step):
+        at = slice(start, start + step)
+        zs = range(start * n_shard // units, (start + step) * n_shard // units)
+        gate = matmul(n_ref[...], flat(gate_ref[:, :, at]))
+        up = matmul(n_ref[...], flat(up_ref[:, :, at]))
+        d_product = sum(dot_nt(cot_ref[:, third * j : third * (j + 1)], down_columns(down_ref, j, zs)) for j in range(3))
+        sigmoid = 1.0 / (1.0 + jnp.exp(-gate))
+        silu = gate * sigmoid
+        product_ref[:, at] = (silu * up).astype(bf16)
+        dboth_ref[:, at] = (d_product * up * sigmoid * (1.0 + gate * (1.0 - sigmoid))).astype(bf16)
+        dboth_ref[:, units + start : units + start + step] = (d_product * silu).astype(bf16)
+
+
+def feed_grads(normed_t, cot, product, d_both):
+    width, rows = normed_t.shape
+    units = product.shape[1]
+    steps = width // units
+
+    def kernel(n_ref, cot_ref, product_ref, both_ref, gate_ref, up_ref, down_ref, turned_ref):
+        step = pl.program_id(0)
+
+        @pl.when(step < steps)
+        def _():
+            gate_ref[...] = matmul(n_ref[...], both_ref[:, :units]).astype(bf16)
+            up_ref[...] = matmul(n_ref[...], both_ref[:, units:]).astype(bf16)
+
+        @pl.when(step == steps)
+        def _():
+            turned_ref[...] = product_ref[...].T
+
+        @pl.when(step >= steps)
+        def _():
+            down_ref[...] = matmul(turned_ref[...], cot_ref[...]).astype(bf16)
+
+    early = lambda i: (jnp.minimum(i, steps - 1), 0)
+    late = lambda i: (0, jnp.maximum(i - steps, 0))
+    return call(
+        kernel,
+        (2 * steps,),
+        [pl.BlockSpec((units, rows), early), pl.BlockSpec((rows, units), late), whole(product.shape), whole(d_both.shape)],
+        [pl.BlockSpec((units, units), early), pl.BlockSpec((units, units), early), pl.BlockSpec((units, units), late)],
+        [((width, units), bf16), ((width, units), bf16), ((units, width), bf16)],
+        [normed_t, cot, product, d_both],
+        "feed_grads",
+        scratch=[pltpu.VMEM((units, rows), bf16)],
+    )
+
+
+def whole_of(array):
+    return array, array.shape, (0,) * array.ndim
+
+
+def third_of(array, index):
+    rows = 384
+    return array, (array.shape[0], rows, array.shape[2]), (0, index, 0)
+
+
+def hidden_units(normed, cot, weights):
+    rows, width = normed.shape
+    units = weights[0][0].shape[2]
+    tile = 512
+    wide = pl.BlockSpec((tile, width), lambda i: (i, 0))
+    thin = pl.BlockSpec((tile, units), lambda i: (i, 0))
+    return call(
+        hidden_kernel,
+        (rows // tile,),
+        [wide, wide] + [part(block, index) for _, block, index in weights],
+        [thin, pl.BlockSpec((tile, 2 * units), lambda i: (i, 0))],
+        [((rows, units), bf16), ((rows, 2 * units), bf16)],
+        [normed, cot] + [a for a, _, _ in weights],
+        "hidden_units",
+    )
+
+
+def sum_rows_call(body, base, lhs, rhs, others, outs, tile, name):
+    rows = outs[0][0][0]
+
+    def shifted(cols):
+        return pl.BlockSpec((tile, cols), lambda i, base: (base[0] + i, 0))
+
+    def plain(cols):
+        return pl.BlockSpec((tile, cols), lambda i, base: (i, 0))
+
+    in_specs = [shifted(a.shape[1]) for a in lhs] + [part(block, index) for _, block, index in rhs]
+    for a, kind in others:
+        in_specs.append(whole(a.shape) if kind == "whole" else {"shifted": shifted, "plain": plain}[kind](a.shape[1]))
+    out_specs = [plain(shape[1]) if shape[0] == rows else whole(shape) for shape, _ in outs]
+    n_lhs, n_rhs, n_other = len(lhs), len(rhs), len(others)
+
+    def kernel(base_ref, *refs):
+        left, refs = refs[:n_lhs], refs[n_lhs:]
+        right, refs = refs[:n_rhs], refs[n_rhs:]
+        body(left, right, refs[:n_other], refs[n_other:])
+
+    return call(
+        kernel,
+        (rows // tile,),
+        in_specs,
+        out_specs,
+        outs,
+        [*lhs, *[a for a, _, _ in rhs], *[a for a, _ in others]],
+        name,
+        [base],
+    )
+
+
+def norm_back(grad_normed, values, scale_rows, gain):
+    scaled = grad_normed * gain
+    return scale_rows * scaled - values * (scale_rows * scale_rows * scale_rows) * jnp.mean(scaled * values, axis=-1, keepdims=True)
+
+
+def column_sums(values):
+    return jnp.sum(values.reshape(-1, 8, values.shape[-1]), axis=0)
+
+
+def half_specs(tile, tiles, width):
+    own = pl.BlockSpec((tile, width), lambda i, core: (jnp.clip(i - tiles * core[0], 0, tiles - 1), 0))
+    far = pl.BlockSpec((tile, width), lambda i, core: (jnp.clip(i - tiles * (1 - core[0]), 0, tiles - 1), 0))
+    return [own, far]
+
+
+def place_half(core_ref, tiles, own_ref, far_ref, out_ref):
+    is_own = pl.program_id(0) // tiles == core_ref[0]
+
+    @pl.when(is_own)
+    def _():
+        out_ref[...] = own_ref[...]
+
+    @pl.when(jnp.logical_not(is_own))
+    def _():
+        out_ref[...] = far_ref[...]
+
+
+def join_halves(core, own, far):
+    rows, width = own.shape
+    tile = 256
+    tiles = rows // tile
+
+    def kernel(core_ref, own_ref, far_ref, out_ref, turned_ref):
+        place_half(core_ref, tiles, own_ref, far_ref, out_ref)
+        turned_ref[...] = out_ref[...].T
+
+    return call(
+        kernel,
+        (2 * tiles,),
+        half_specs(tile, tiles, width),
+        [pl.BlockSpec((tile, width), lambda i, _: (i, 0)), pl.BlockSpec((width, tile), lambda i, _: (0, i))],
+        [((2 * rows, width), bf16), ((width, 2 * rows), bf16)],
+        [own, far],
+        "join_halves",
+        [core],
+    )
+
+
+def mixed_back(core, own, far, w_out_rows):
+    rows, width = own.shape
+    heads = w_out_rows.shape[0]
+    tile = 512
+    tiles = rows // tile
+
+    def kernel(core_ref, own_ref, far_ref, w_ref, out_ref, grad_ref):
+        place_half(core_ref, tiles, own_ref, far_ref, out_ref)
+        grad_ref[...] = dot_nt(out_ref[...], w_ref[...]).astype(bf16)
+
+    return call(
+        kernel,
+        (2 * tiles,),
+        half_specs(tile, tiles, width) + [whole(w_out_rows.shape)],
+        [pl.BlockSpec((tile, width), lambda i, _: (i, 0)), pl.BlockSpec((tile, heads), lambda i, _: (i, 0))],
+        [((2 * rows, width), bf16), ((2 * rows, heads), bf16)],
+        [own, far, w_out_rows],
+        "mixed_back",
+        [core],
+    )
+
+
+def out_rows(place, blocks):
+    n_shard, rows_in, cols = blocks[0].shape
+    chunks = rows_in // HALF
+    quarters = len(blocks)
+    shape = (quarters * quarters * SLOT, chunks * cols)
+
+    def kernel(place_ref, *refs):
+        out_ref = refs[-1]
+        out_ref[...] = jnp.zeros(shape, bf16)
+        for group in range(quarters):
+            for at in range(quarters):
+                row = pl.multiple_of(Q_LANES * group + SLOT * (at ^ place_ref[0]), SLOT)
+                for j in range(chunks):
+                    out_ref[pl.ds(row, HALF), cols * j : cols * (j + 1)] = refs[at][group ^ place_ref[0], HALF * j : HALF * (j + 1), :]
+
+    (out,) = call(
+        kernel,
+        (1,),
+        [whole((n_shard, rows_in, cols))] * quarters,
+        [whole(shape)],
+        [(shape, bf16)],
+        blocks,
+        "out_rows",
+        [place],
+    )
+    return out
+
+
+def out_grad_blocks(place, mixed, grad):
+    rows, heads = mixed.shape
+    width = grad.shape[1]
+    quarters = heads // Q_LANES
+    tile = 512
+
+    def kernel(place_ref, mixed_ref, grad_ref, *refs):
+        outs = refs[:quarters]
+        group = pl.program_id(0)
+        sums = dot_tn(mixed_ref[...], grad_ref[...]).astype(bf16)
+        refs[quarters][...] = sums
+        shard = group ^ place_ref[0]
+        for at in range(quarters):
+            row = pl.multiple_of(SLOT * (at ^ place_ref[0]), SLOT)
+            outs[at][shard] = refs[quarters][pl.ds(row, HALF), :]
+
+    return call(
+        kernel,
+        (quarters,),
+        [pl.BlockSpec((rows, Q_LANES), lambda g, _: (0, g)), whole((rows, width))],
+        [whole((quarters, HALF, width))] * quarters,
+        [((quarters, HALF, width), bf16)] * quarters,
+        [mixed, grad],
+        "out_grads",
+        [place],
+        [pltpu.VMEM((Q_LANES, width), bf16)],
+    )
+
+
+def qkv_grad(normed_t, d_query, d_key, d_value):
+    width, rows = normed_t.shape
+    spread = jnp.asarray(spread_matrix(), bf16)
+    tile = 512
+
+    def kernel(n_ref, q_ref, k_ref, v_ref, spread_ref, out_ref):
+        query = matmul(n_ref[...], q_ref[...]).astype(bf16)
+        both = matmul(n_ref[...], jnp.concatenate([k_ref[...], v_ref[...]], axis=1)).astype(bf16)
+        out_ref[...] = dot_nt(jnp.concatenate([query, both], axis=1), spread_ref[...]).astype(bf16)
+
+    (out,) = call(
+        kernel,
+        (width // tile,),
+        [
+            pl.BlockSpec((tile, rows), lambda i: (i, 0)),
+            whole(d_query.shape),
+            whole(d_key.shape),
+            whole(d_value.shape),
+            whole(spread.shape),
+        ],
+        [pl.BlockSpec((tile, GROUP_COLS), lambda i: (i, 0))],
+        [((width, GROUP_COLS), bf16)],
+        [normed_t, d_query, d_key, d_value, spread],
+        "qkv_grad",
+    )
+    return out
+
+
+def unit_columns(where, pieces, n_shard, index):
+    depth, cols = pieces[0].shape[0] // 2, pieces[0].shape[1]
+    tile = 96
+    count = len(pieces)
+    quarters = count // 2
+    unit_cols = cols // n_shard
+
+    def kernel(where_ref, *refs):
+        out_ref = refs[-1]
+        for k in range(count):
+            unit = quarters * (where_ref[1] ^ (k // quarters)) + (where_ref[0] ^ (k % quarters))
+            for z in range(n_shard):
+                at = pl.multiple_of((count * z + unit) * unit_cols, unit_cols)
+                out_ref[:, pl.ds(at, unit_cols)] = refs[k][:, unit_cols * z : unit_cols * (z + 1)].astype(f32)
+
+    steps = depth // tile
+    (out,) = call(
+        kernel,
+        (depth // tile,),
+        [pl.BlockSpec((tile, cols), lambda i, _: (index * steps + i, 0))] * count,
+        [pl.BlockSpec((tile, cols * count), lambda i, _: (i, 0))],
+        [((depth, cols * count), f32)],
+        pieces,
+        "unit_columns",
+        [where],
+    )
+    return out
+
+
+def unit_rows(where, pieces, down_depth):
+    depth, width = pieces[0].shape
+    count = len(pieces)
+    quarters = count // 2
+    out_depth = depth - down_depth
+
+    def unit_at(i, where_ref):
+        return quarters * (where_ref[1] ^ (i // quarters)) + (where_ref[0] ^ (i % quarters))
+
+    def kernel(where_ref, *refs):
+        for k in range(count):
+
+            @pl.when(pl.program_id(0) == k)
+            def _():
+                refs[count][...] = refs[k][:down_depth, :].astype(f32)
+                refs[count + 1][...] = refs[k][down_depth:, :].astype(f32)
+
+    return call(
+        kernel,
+        (count,),
+        [whole((depth, width))] * count,
+        [
+            pl.BlockSpec((down_depth, width), lambda i, where: (unit_at(i, where), 0)),
+            pl.BlockSpec((out_depth, width), lambda i, where: (unit_at(i, where), 0)),
+        ],
+        [((down_depth * count, width), f32), ((out_depth * count, width), f32)],
+        pieces,
+        "unit_rows",
+        [where],
+    )
+
+
+def head_columns(where, pieces):
+    depth, cols = pieces[0].shape
+    count = len(pieces)
+    quarters = count // 2
+    split = 2
+
+    def kernel(where_ref, *refs):
+        q_out, k_out, v_out = refs[count:]
+        place, core = where_ref[0], where_ref[1]
+        row = lax.broadcasted_iota(jnp.int32, (cols, cols), 0)
+        column = lax.broadcasted_iota(jnp.int32, (cols, cols), 1)
+
+        def moved(piece, start, size, to):
+            chosen = (row >= start) & (row < start + size) & (row - start == column - to)
+            return matmul(piece, jnp.where(chosen, 1.0, 0.0).astype(bf16))
+
+        for at in range(quarters):
+            total = 0.0
+            for other in range(split):
+                total += moved(refs[quarters * other + at][...], 0, Q_COLS, Q_COLS * (core ^ other))
+            q_out[:, pl.ds(pl.multiple_of(cols * (place ^ at), LANES), cols)] = total
+        for pair in range(quarters // 2):
+            keys = values = 0.0
+            for low in range(2):
+                for other in range(split):
+                    piece = refs[quarters * other + 2 * pair + low][...]
+                    to = HEAD_DIM * (2 * ((place & 1) ^ low) + (core ^ other))
+                    keys += moved(piece, Q_COLS, HEAD_DIM, to)
+                    values += moved(piece, Q_COLS + HEAD_DIM, HEAD_DIM, to)
+            start = pl.multiple_of(cols * ((place >> 1) ^ pair), LANES)
+            k_out[:, pl.ds(start, cols)] = keys
+            v_out[:, pl.ds(start, cols)] = values
+
+    shapes = [(depth, quarters * split * w) for w in (Q_COLS, HEAD_DIM, HEAD_DIM)]
+    return call(
+        kernel, (1,), [whole((depth, cols))] * count, [whole(s) for s in shapes], [(s, f32) for s in shapes], pieces, "head_columns", [where]
+    )
+
+
+def chip_layer(
+    tokens, span_order, token_positions, attn_gain, w_query, w_key, w_value, w_out, mlp_gain, w_gate, w_up, w_down, cotangent
+):
+    seq_dev, local_len, width = tokens.shape
+    n_ctx, n_shard = lax.axis_size("ctx"), lax.axis_size("shard")
+    split = n_ctx // seq_dev
+    full_len = local_len * n_ctx
+    half_rows = full_len // split
+    spans_dev = local_len // SPAN
+    quarters = 4
+    units = w_gate.shape[1] // (split * quarters)
+    unit_cols = units // n_shard
+    gain_width = attn_gain.shape[0]
+    ctx, batch, shard = lax.axis_index("ctx"), lax.axis_index("batch"), lax.axis_index("shard")
+    seq, core = ctx // split, ctx % split
+    place = 2 * seq + batch
+
+    perm_x = [(c, c ^ split) for c in range(n_ctx)]
+    perm_core = [(c, c ^ 1) for c in range(n_ctx)]
+    perm_both = [(c, c ^ (split | 1)) for c in range(n_ctx)]
+    perm_diagonal = [(2 * c + b, 2 * (c ^ split) + (b ^ 1)) for c in range(n_ctx) for b in range(2)]
+    over_x = lambda a: lax.ppermute(a, "ctx", perm_x)
+    over_core = lambda a: lax.ppermute(a, "ctx", perm_core)
+    over_both = lambda a: lax.ppermute(a, "ctx", perm_both)
+    over_y = lambda a: lax.ppermute(a, "batch", [(0, 1), (1, 0)])
+    over_diagonal = lambda a: lax.ppermute(a, ("ctx", "batch"), perm_diagonal)
+
+    def over_z(piece):
+        gathered = lax.all_gather(piece, "shard", axis=0, tiled=True)
+        return gathered.reshape(n_shard, piece.shape[0], piece.shape[1])
+
+    def pick(array, index, axis):
+        return lax.dynamic_index_in_dim(array, index, axis, keepdims=False)
+
+    def scatter(block):
+        return lax.psum_scatter(block, "shard", scatter_dimension=0, tiled=True)
+
+    def add(*terms):
+        return functools.reduce(lambda a, b: a + b, [t.astype(f32) for t in terms]).astype(bf16)
+
+    def fence(*arrays):
+        return lax.optimization_barrier(arrays)
+
+    column = split * place + core
+    unit_at = quarters * core + place
+
+    def columns_of(array, width_of):
+        return lax.dynamic_slice_in_dim(array, column * width_of, width_of, 1)
+
+    def units_of(array, at):
+        blocks = [lax.dynamic_slice_in_dim(array, (split * quarters * z + at) * unit_cols, unit_cols, 1) for z in range(n_shard)]
+        return jnp.concatenate(blocks, axis=1)
+
+    def stacked(rows, cols):
+        return jnp.concatenate([rows[:, cols * j : cols * (j + 1)] for j in range(rows.shape[1] // cols)], axis=0)
+
+    head_piece = jnp.concatenate(
+        [columns_of(w_query, Q_COLS), columns_of(w_key, HEAD_DIM), columns_of(w_value, HEAD_DIM)], axis=1
+    )
+    gains = jnp.pad(jnp.stack([attn_gain, mlp_gain]), ((0, PAD_ROWS - 2), (0, 0)))
+    out_piece = stacked(lax.dynamic_slice_in_dim(w_out, unit_at * HALF, HALF, 0), GROUP_COLS)
+    head_piece = jnp.concatenate([head_piece, gains, out_piece], axis=0)
+
+    def second_piece(at):
+        return jnp.concatenate([units_of(w_up, at), stacked(lax.dynamic_slice_in_dim(w_down, at * unit_cols, unit_cols, 0), units)], axis=0)
+
+    own_tokens, sent_tokens = pick(tokens, seq, 0), pick(tokens, 1 - seq, 0)
+    positions = pick(token_positions, seq, 0)
+    sent_positions = pick(token_positions, 1 - seq, 0)
+    head_piece, own_tokens, sent_tokens, positions, sent_positions, w_gate, w_up, w_down = fence(
+        head_piece, own_tokens, sent_tokens, positions, sent_positions, w_gate, w_up, w_down
+    )
+    head_own = over_z(head_piece)
+    positions = jnp.stack([positions, over_x(sent_positions)])
+    x_near = jnp.concatenate([own_tokens, over_x(sent_tokens)], axis=0)
+    head_rows = gain_width + PAD_ROWS
+    head_sent, out_own = head_own[:, :head_rows], head_own[:, head_rows:]
+    gate_piece, second_own, second_last = units_of(w_gate, unit_at), second_piece(unit_at), second_piece(unit_at ^ 3)
+    head_own, head_sent, out_own, x_near, positions, gate_piece, second_own, second_last, cotangent = fence(
+        head_own, head_sent, out_own, x_near, positions, gate_piece, second_own, second_last, cotangent
+    )
+
+    gate_own = over_z(gate_piece)
+    head_x, head_y, x_far = over_x(head_sent), over_y(head_sent), over_core(x_near)
+    positions = jnp.concatenate([positions, over_core(positions)], axis=0).reshape(-1, SPAN)
+    cot_own, cot_sent = pick(cotangent, seq, 0), pick(cotangent, 1 - seq, 0)
+    order = pick(span_order, seq, 0)
+    n_spans = order.shape[0]
+    span_ids = jnp.arange(n_spans, dtype=jnp.int32)
+    slot_of = jnp.sum(jnp.where(order[None, :] == span_ids[:, None], span_ids[None, :], 0), axis=1)
+    owner = slot_of // spans_dev
+    from_far = (owner % split) ^ core
+    side_place = ((owner // split) ^ seq) * spans_dev + slot_of % spans_dev
+    places = [
+        jnp.where(from_far == 0, side_place, 0).astype(jnp.int32),
+        jnp.where(from_far == 0, 0, side_place).astype(jnp.int32),
+        from_far.astype(jnp.int32),
+    ]
+    head_x, head_y, x_far, positions, cot_own, cot_sent, out_own = fence(
+        head_x, head_y, x_far, positions, cot_own, cot_sent, out_own
+    )
+
+    middle = n_shard // 2
+    head_last = [over_x(head_y[:middle]), over_y(head_x[middle:])]
+    choice = (from_far * seq_dev * spans_dev + side_place)[:, None] == span_ids[None, :]
+    positions = jnp.sum(jnp.where(choice[:, :, None], positions[None], 0), axis=1).reshape(full_len)
+    frequency = rope_base ** (-2.0 * jnp.arange(HALF, dtype=f32) / HEAD_DIM)
+    angles = positions.astype(f32)[:, None] * frequency
+    blank = jnp.zeros((full_len, SLOT - HALF), f32)
+    cos_half, sin_half = jnp.cos(angles), jnp.sin(angles)
+    cosine = jnp.concatenate([cos_half, blank, cos_half, blank], axis=1)
+    sine = jnp.concatenate([-sin_half, blank, sin_half, blank], axis=1)
+    gain_one = head_own[:, gain_width, :].reshape(1, width).astype(f32)
+    gain_two = head_own[:, gain_width + 1, :].reshape(1, width).astype(f32)
+    *head_last, cosine, sine, cot_sent, gate_own, second_own, out_own = fence(
+        *head_last, cosine, sine, cot_sent, gate_own, second_own, out_own
+    )
+
+    out_blocks = [out_own, over_y(out_own), over_x(out_own), over_diagonal(out_own)]
+    head_blocks = [head_own, head_y, head_x, *head_last]
+    x, normed, normed_t, queries, keys, values, w_qkv = front(places, x_near, x_far, cosine, sine, gain_one, head_blocks)
+    x, normed_t, queries, keys, values, w_qkv = fence(x, normed_t, queries, keys, values, w_qkv)
+
+    second_own = over_z(second_own)
+    cot_received, gate_y = over_x(cot_sent), over_y(gate_own)
+    mixed, q_aug = attend(queries, keys, values)
+    cot_near = jnp.concatenate([cot_own, cot_received], axis=0)
+    mixed, q_aug, cot_near, gate_y, second_own, second_last, gate_sent, *out_blocks = fence(
+        mixed, q_aug, cot_near, gate_y, second_own, second_last, gate_own, *out_blocks
+    )
+
+    second_last = over_z(second_last)
+    gate_x, cot_far = over_x(gate_sent), over_core(cot_near)
+    second_y = over_y(second_own)
+    place_at = place.astype(jnp.int32)[None]
+    w_out_rows = out_rows(place_at, out_blocks)
+    mine = core.astype(jnp.int32)[None]
+    other = 1 - mine
+    row_tile = 256
+    tiles_half = half_rows // row_tile
+    full_out = (w_out_rows, w_out_rows.shape, (0, 0))
+
+    def partial_rows(lhs, rhs, dots, name):
+        def body(left, right, _, outs):
+            dots(left, right, lambda at, total: outs[0].__setitem__((slice(None), at), total.astype(bf16)))
+
+        tile = 512
+        return sum_rows_call(body, other * (half_rows // tile), lhs, rhs, [], [((half_rows, width), bf16)], tile, name)[0]
+
+    def out_dot(left, right, store):
+        store(slice(None), matmul(left[0][...], right[0][...]))
+
+    def back_dot(left, right, store):
+        total = 0.0
+        for k, both in enumerate(left):
+            for which in range(2):
+                total += dot_nt(both[:, units * which : units * (which + 1)], flat(right[2 * k + which][...]))
+        store(slice(None), total)
+
+    def down_dot(left, right, store):
+        for j in range(width // units):
+            total = sum(matmul(a[...], down_columns(b, j, range(n_shard))) for a, b in zip(left, right))
+            store(slice(units * j, units * (j + 1)), total)
+
+    def in_dot(left, right, store):
+        total = 0.0
+        for which, weights in enumerate(right):
+            total += dot_nt(jnp.concatenate([a[...] for a in left[which::3]], axis=1), weights[...])
+        store(slice(None), total)
+
+    def kept(dots, left, right):
+        found = []
+        dots(left, right, lambda at, total: found.append(total))
+        return found[0]
+
+    received = over_core(partial_rows([mixed], [full_out], out_dot, "out_other"))
+
+    def hidden_body(left, right, others, outs):
+        x_ref, received_ref, gain_ref = others
+        hidden = x_ref[...].astype(f32) + kept(out_dot, left, right) + received_ref[...].astype(f32)
+        outs[0][...] = hidden
+        outs[1][...] = (hidden * rms_scale(hidden) * gain_ref[...]).astype(bf16)
+
+    hidden, normed_two_own = sum_rows_call(
+        hidden_body,
+        mine * tiles_half,
+        [mixed],
+        [full_out],
+        [(x, "shifted"), (received, "plain"), (gain_two, "whole")],
+        [((half_rows, width), f32), ((half_rows, width), bf16)],
+        row_tile,
+        "out_own",
+    )
+    normed_two_own, cot_far, gate_x, second_own = fence(normed_two_own, cot_far, gate_x, second_own)
+    second_x = over_x(second_own)
+    cot = span_join(places, cot_near, cot_far)
+    normed_two, normed_two_t = join_halves(mine, normed_two_own, over_core(normed_two_own))
+    normed_two, normed_two_t, cot, second_y, second_last = fence(normed_two, normed_two_t, cot, second_y, second_last)
+
+    def feed(normed_two, cot, gate, second, with_grads=True):
+        weights = [whole_of(gate), third_of(second, 0), third_of(second, 1)]
+        product, d_both = hidden_units(normed_two, cot, weights)
+        if not with_grads:
+            return weights, product, d_both
+        return weights, product, d_both, feed_grads(normed_two_t, cot, product, d_both)
+
+    gate_last = over_y(gate_x)
+    fed = [feed(normed_two, cot, gate_own, second_own)]
+    own_grads, normed_two, second_x, gate_last = fence(fed[0][3], normed_two, second_x, gate_last)
+    fed.append(feed(normed_two, cot, gate_y, second_y))
+    (gate_gy, up_gy, down_gy), normed_two = fence(fed[1][3], normed_two)
+    down_gy = over_y(down_gy)
+    fed.append(feed(normed_two, cot, gate_x, second_x))
+    (gate_gx, up_gx, down_gx), normed_two, gate_gy, up_gy, down_gy = fence(fed[2][3], normed_two, gate_gy, up_gy, down_gy)
+    gate_gy, down_gx = over_y(gate_gy), over_x(down_gx)
+    weights_last, product_last, d_both_last = feed(normed_two, cot, gate_last, second_last, False)
+    fed.append((weights_last, product_last, d_both_last))
+    products, d_boths = [f[1] for f in fed], [f[2] for f in fed]
+
+    back_rhs = [f[0][k] for f in fed for k in range(2)]
+    downs = [f[0][2] for f in fed]
+    back_sent = partial_rows(d_boths, back_rhs, back_dot, "back_other")
+    back_sent, d_boths, products, gate_gy, up_gy, down_gx, gate_gx, up_gx = fence(
+        back_sent, d_boths, products, gate_gy, up_gy, down_gx, gate_gx, up_gx
+    )
+    received_two = over_core(back_sent)
+    up_gy, gate_gx = over_y(up_gy), over_x(gate_gx)
+    gate_gl, up_gl, down_gl = feed_grads(normed_two_t, cot, products[3], d_boths[3])
+    out_sent = partial_rows(products, downs, down_dot, "down_other")
+    received_two, out_sent, up_gy, gate_gx, gate_gl, up_gl, up_gx, down_gl = fence(
+        received_two, out_sent, up_gy, gate_gx, gate_gl, up_gl, up_gx, down_gl
+    )
+
+    def back_body(left, right, others, outs):
+        received_ref, hidden_ref, cot_ref, gain_ref = others
+        grad_normed = kept(back_dot, left, right) + received_ref[...].astype(f32)
+        values_ = hidden_ref[...]
+        scale_rows = rms_scale(values_)
+        grad_hidden = cot_ref[...].astype(f32) + norm_back(grad_normed, values_, scale_rows, gain_ref[...])
+        outs[0][...] = grad_hidden
+        outs[1][...] = grad_hidden.astype(bf16)
+
+        @pl.when(pl.program_id(0) == 0)
+        def _():
+            outs[2][...] = jnp.zeros(outs[2].shape, f32)
+
+        outs[2][...] += column_sums(grad_normed * values_ * scale_rows)
+
+    up_gx, gate_gl = over_x(up_gx), scatter(gate_gl)
+    received_out = over_core(out_sent)
+    grad_hidden, grad_attended_own, gain_two_sums = sum_rows_call(
+        back_body,
+        mine * tiles_half,
+        d_boths,
+        back_rhs,
+        [(received_two, "plain"), (hidden, "plain"), (cot, "shifted"), (gain_two, "whole")],
+        [((half_rows, width), f32), ((half_rows, width), bf16), ((8, width), f32)],
+        row_tile,
+        "back_own",
+    )
+    grad_attended_own, received_out, up_gx, gate_gl, up_gl, gate_gx = fence(grad_attended_own, received_out, up_gx, gate_gl, up_gl, gate_gx)
+    grad_attended_far = over_core(grad_attended_own)
+    up_gl = scatter(up_gl)
+    gate_sum = add(own_grads[0], gate_gy, gate_gx)
+
+    def down_body(left, right, others, outs):
+        hidden_ref, received_ref = others
+
+        def store(at, total):
+            outs[0][:, at] = (hidden_ref[:, at] + total + received_ref[:, at].astype(f32)).astype(bf16)
+
+        down_dot(left, right, store)
+
+    (layer_rows,) = sum_rows_call(
+        down_body,
+        mine * tiles_half,
+        products,
+        downs,
+        [(hidden, "plain"), (received_out, "plain")],
+        [((half_rows, width), bf16)],
+        row_tile,
+        "down_own",
+    )
+    grad_attended_own, grad_attended_far, layer_rows, down_gl, gate_sum = fence(
+        grad_attended_own, grad_attended_far, layer_rows, down_gl, gate_sum
+    )
+
+    pair_order = order.reshape(n_ctx, spans_dev // 2, 2)
+    in_half = jnp.where(pair_order[..., 0] // (n_spans // 2) == core, pair_order[..., 0], pair_order[..., 1]) - core * (n_spans // 2)
+    steps = jnp.arange(n_ctx, dtype=jnp.int32) ^ ctx
+    send_places = in_half[steps].reshape(-1).astype(jnp.int32)
+    my_order = lax.dynamic_slice_in_dim(span_order, ctx * spans_dev, spans_dev, 1)
+    from_mine = (my_order // (n_spans // 2) == core).reshape(seq_dev, spans_dev // 2, 2, 1, 1)
+
+    def to_slots(arranged):
+        return [arranged[0], over_core(arranged[1]), over_x(arranged[2]), over_both(arranged[3])]
+
+    def arrange(rows):
+        arranged = span_copy(send_places, rows).reshape(n_ctx, -1, width)
+        return [arranged[k] for k in range(n_ctx)]
+
+    def from_slots(parts):
+        parts = [p.reshape(spans_dev // 2, 1, SPAN, width) for p in parts]
+        near = jnp.where(from_mine[seq], parts[0], parts[1])
+        far = jnp.where(from_mine[1 - seq], parts[2], parts[3])
+        near, far = near.reshape(local_len, width), far.reshape(local_len, width)
+        return jnp.where(seq == 0, jnp.stack([near, far]), jnp.stack([far, near]))
+
+    def sides(piece):
+        return [piece, over_y(piece), over_x(piece), over_diagonal(piece)]
+
+    def both_cores(side):
+        return side + [over_core(a) for a in side]
+
+    gate_sum = scatter(gate_sum)
+    down_gl = over_diagonal(down_gl)
+    grad_attended, grad_mixed = mixed_back(mine, grad_attended_own, grad_attended_far, w_out_rows)
+    out_grads = [b.reshape(-1, width) for b in out_grad_blocks(place_at, mixed, grad_attended)]
+    layer_parts = arrange(layer_rows)
+    up_sum = add(own_grads[1], up_gy, up_gx)
+    grad_mixed, out_grads, down_gl, layer_parts, up_sum, gate_gl, up_gl = fence(
+        grad_mixed, out_grads, down_gl, layer_parts, up_sum, gate_gl, up_gl
+    )
+
+    def back_of(group, q_aug):
+        return attend_back(group, 1, q_aug, keys, values, grad_mixed, mixed, cosine, sine)
+
+    up_sum = scatter(up_sum)
+    layer_parts = to_slots(layer_parts)
+    both_gl = over_diagonal(jnp.concatenate([gate_gl, up_gl], axis=0))
+    back_last = back_of(3, q_aug)
+    down_sum = add(own_grads[2], down_gy, down_gx, down_gl)
+    back_last, q_aug, layer_parts, gate_sum, both_gl, down_sum, out_grads = fence(
+        back_last, q_aug, layer_parts, gate_sum, both_gl, down_sum, out_grads
+    )
+    qkv_last = qkv_grad(normed_t, *back_last)
+    qkv_last, q_aug, down_sum = fence(qkv_last, q_aug, down_sum)
+
+    qkv_last = over_diagonal(qkv_last)
+    down_sum = scatter(down_sum)
+    out_grads = [out_grads[0], over_y(out_grads[1]), over_x(out_grads[2]), over_diagonal(out_grads[3])]
+    back_x = back_of(2, q_aug)
+    back_x, q_aug, qkv_last, out_grads, up_sum = fence(back_x, q_aug, qkv_last, out_grads, up_sum)
+    qkv_x = qkv_grad(normed_t, *back_x)
+    out_sum = add(*out_grads)
+    both_sum = add(jnp.concatenate([gate_sum, up_sum], axis=0), both_gl)
+    qkv_x, out_sum, both_sum, q_aug = fence(qkv_x, out_sum, both_sum, q_aug)
+
+    qkv_x = over_x(qkv_x)
+    out_sum = scatter(out_sum)
+    both_sides = sides(both_sum)
+    back_y = back_of(1, q_aug)
+    back_y, q_aug, qkv_x, both_sides, down_sum = fence(back_y, q_aug, qkv_x, both_sides, down_sum)
+    qkv_y = qkv_grad(normed_t, *back_y)
+    qkv_y, q_aug = fence(qkv_y, q_aug)
+
+    qkv_y = over_y(qkv_y)
+    both_pieces = both_cores(both_sides)
+    back_own = back_of(0, q_aug)
+    back_own, qkv_y, both_pieces, out_sum = fence(back_own, qkv_y, both_pieces, out_sum)
+
+    in_lhs = [*back_own, *back_y, *back_x, *back_last]
+    depth = w_qkv.shape[0]
+    q_width, k_width = queries.shape[1], keys.shape[1]
+    in_rhs = [(w_qkv, (depth, q_width), (0, 0))]
+    in_rhs += [(w_qkv, (depth, k_width), (0, q_width // k_width + which)) for which in range(2)]
+    received_in = over_core(partial_rows(in_lhs, in_rhs, in_dot, "in_other"))
+    row_sides = sides(jnp.concatenate([down_sum, out_sum], axis=0))
+    qkv_sum = add(qkv_grad(normed_t, *back_own), qkv_y, qkv_x, qkv_last)
+    qkv_sum, received_in, row_sides = fence(qkv_sum, received_in, row_sides)
+    qkv_sum = scatter(qkv_sum)
+
+    def in_body(left, right, others, outs):
+        received_ref, x_ref, grad_ref, gain_ref = others
+        grad_normed = kept(in_dot, left, right) + received_ref[...].astype(f32)
+        values_ = x_ref[...].astype(f32)
+        scale_rows = rms_scale(values_)
+        outs[0][...] = (grad_ref[...] + norm_back(grad_normed, values_, scale_rows, gain_ref[...])).astype(bf16)
+
+        @pl.when(pl.program_id(0) == 0)
+        def _():
+            outs[1][...] = jnp.zeros(outs[1].shape, f32)
+
+        outs[1][...] += column_sums(grad_normed * values_ * scale_rows)
+
+    grad_rows, gain_one_sums = sum_rows_call(
+        in_body,
+        mine * tiles_half,
+        in_lhs,
+        in_rhs,
+        [(received_in, "plain"), (x, "shifted"), (grad_hidden, "plain"), (gain_one, "whole")],
+        [((half_rows, width), bf16), ((8, width), f32)],
+        row_tile,
+        "in_own",
+    )
+    sums = jnp.stack([gain_one_sums.sum(0), gain_two_sums.sum(0)])
+    token_parts, sums, qkv_sum, row_sides = fence(arrange(grad_rows), sums, qkv_sum, row_sides)
+    for step in (over_core, over_x, over_y):
+        sums = sums + step(sums)
+    total = lax.dynamic_slice_in_dim(sums, shard * gain_width, gain_width, 1)
+    for step in range(1, n_shard):
+        to = lax.dynamic_slice_in_dim(sums, (shard + step) % n_shard * gain_width, gain_width, 1)
+        total = total + lax.ppermute(to, "shard", [(z, (z + step) % n_shard) for z in range(n_shard)])
+    token_parts = to_slots(token_parts)
+    where = jnp.stack([place, core]).astype(jnp.int32)
+    qkv_pieces = both_cores(sides(qkv_sum))
+    grad_w_gate = unit_columns(where, both_pieces, n_shard, 0)
+    grad_w_up = unit_columns(where, both_pieces, n_shard, 1)
+    grad_w_down, grad_w_out = unit_rows(where, both_cores(row_sides), unit_cols)
+    layer_out = from_slots(layer_parts)
+    grad_w_query, grad_w_key, grad_w_value = head_columns(where, qkv_pieces)
+    grad_tokens = from_slots(token_parts)
+
+    return (
+        layer_out,
+        grad_tokens,
+        total[0],
+        grad_w_query,
+        grad_w_key,
+        grad_w_value,
+        grad_w_out,
+        total[1],
+        grad_w_gate,
+        grad_w_up,
+        grad_w_down,
+    )
 
 
 def rope_tables(positions):
@@ -40,18 +1211,7 @@
     )
 
 
-def norm_back(grad_normed, values, scale_rows, gain):
-    scaled = grad_normed * gain
-    return scale_rows * scaled - values * scale_rows**3 * jnp.mean(
-        scaled * values, axis=-1, keepdims=True
-    )
-
-
-def matmul(left, right):
-    return jnp.dot(left, right, preferred_element_type=jnp.float32)
-
-
-def shards(
+def general_layer(
     tokens,
     span_order,
     token_positions,
@@ -305,6 +1465,11 @@
     )
 
 
+def fits(mesh):
+    split = mesh.shape["ctx"] // 2
+    return split == 2 and mesh.shape["batch"] == 2 and mesh.shape["shard"] * split == KV_HEADS and mesh.shape["shard"] == 4
+
+
 def solution(mesh):
     in_specs = (
         P(("shard", "batch"), "ctx", None),
@@ -334,4 +1499,5 @@
         P("shard", None),
         P("shard", None),
     )
-    return jax.shard_map(shards, mesh=mesh, in_specs=in_specs, out_specs=out_specs, check_vma=False)
+    layer = chip_layer if fits(mesh) else general_layer
+    return jax.shard_map(layer, mesh=mesh, in_specs=in_specs, out_specs=out_specs, check_vma=False)

time: 2860 us -> 972 us (0.34)
  waiting for transfers between devices: 1760 us -> 288 us
  matrix products: 674 us -> 0 us
  Pallas kernels: 0 us -> 512 us
  other arithmetic: 219 us -> 40.2 us
  local copies, waits for them, and re-layouts: 123 us -> 49.5 us
  starting transfers between devices: 1.8 us -> 57.9 us
  blocking collectives: 53.1 us -> 0 us
    reduce_scatter x9 -> x7, waiting for transfers between devices: 922 us -> 1.39 us  [scatter(): return lax.psum_scatter(block, 'shard', scatter_dimension=0, tiled=True)]
    all_gather x9 -> x4, waiting for transfers between devices: 721 us -> 4.31 us  [over_z(): gathered = lax.all_gather(piece, 'shard', axis=0, tiled=True)]
    dot_general x77 -> x0, matrix products: 674 us -> none  [the longest x21 275 us: matmul(): return jnp.dot(left, right, preferred_element_type=jnp.float32)]
    pallas_call x0 -> x37, Pallas kernels: none -> 512 us  [call(): pl.pallas_call(kernel, grid_spec=pltpu.PrefetchScalarGridSpec(num_scalar_...]
    ppermute x0 -> x71, waiting for transfers between devices: none -> 282 us  [the longest x19 114 us: chip_layer(): over_x = lambda a: lax.ppermute(a, 'ctx', perm_x)]
    convert_element_type x26 -> x9, other arithmetic: 138 us -> 19.8 us  [the longest x6 18.6 us: add(): functools.reduce(lambda a, b: a + b, [t.astype(f32) for t in terms])]
    psum x1 -> x0, waiting for transfers between devices: 116 us -> none  [shards(): lax.psum(part_query.astype(jnp.bfloat16), ('ctx', 'batch'))]
    ppermute x0 -> x71, starting transfers between devices: none -> 57.2 us  [the longest x19 20.5 us: chip_layer(): over_x = lambda a: lax.ppermute(a, 'ctx', perm_x)]
  transfers between devices with their start and end apart: 19 -> 82, of which waited for: 18 -> 34; matrix products, arithmetic and copies ran while one was open for 15% -> 6% of each run, Pallas kernels for 0% -> 47%
where the time goes in v1:
time: 972 us; the launch traced here: 963 us
  Pallas kernels  512 us (53%)
  waiting for transfers between devices  288 us (30%)
  starting transfers between devices  57.9 us (6%)
  local copies, waits for them, and re-layouts  49.5 us (5%)
  other arithmetic  40.2 us (4%)
  between operations  15.1 us (2%)
    pallas_call x37, Pallas kernels, call(): pl.pallas_call(kernel, grid_spec=pltpu.PrefetchScalarGridSpec(num_scalar_...  512 us
    ppermute x19, waiting for transfers between devices, chip_layer(): over_x = lambda a: lax.ppermute(a, 'ctx', perm_x)  114 us
    ppermute x15, waiting for transfers between devices, chip_layer(): over_y = lambda a: lax.ppermute(a, 'batch', [(0, 1), (1, 0)])  84.2 us
    ppermute x8, waiting for transfers between devices, chip_layer(): over_diagonal = lambda a: lax.ppermute(a, ('ctx', 'batch'), perm_diagonal)  55.8 us
    ppermute x19, starting transfers between devices, chip_layer(): over_x = lambda a: lax.ppermute(a, 'ctx', perm_x)  20.5 us
  transfers between devices with their start and end apart: 82, of which 34 were waited for; matrix products, arithmetic and copies ran while one was open for 6% of the time, Pallas kernels for 47%

profile of v1, /device:TPU:0, one launch (start us, length us, event | category | flops | bytes accessed | tf_op | source)
XLA Modules:
  0.0 962.8 jit_solution(833379560991537726)
XLA Ops:
  26.9 28.1 %collective-permute-done.1 = s32[512]{0:T(512)S(1)} collective-permute-done((s32[512]{0:T(512)S(1)}, s32[512]{0:T(512)S(1)}, u32[]{:S(2)}, u32[]{:S(2)}) %collective-permute-start.1) | collective-permute-done | bytes 2080 | tf_op jit(solution)/shard_map/ppermute | solution.py:785
  73.0 22.6 %collective-permute-done.2.refs_14_ = bf16[4,400,384]{2,1,0:T(8,128)(2,1)} collective-permute-done((bf16[4,400,384]{2,1,0:T(8,128)(2,1)}, bf16[4,400,384]{2,1,0:T(8,128)(2,1)}, u32[]{:S(2)}, u32[]{:S(2)}) %collective-permute-start.2) | collective-permute-done | bytes 1228832 | tf_op jit(solution)/shard_map/ppermute | solution.py:785
  124.1 28.1 %front.1 = (bf16[2048,1536]{1,0:T(8,128)(2,1)}, bf16[2048,1536]{1,0:T(8,128)(2,1)}, bf16[1536,2048]{1,0:T(8,128)(2,1)}, bf16[2048,1024]{1,0:T(8,128)(2,1)}, bf16...) custom-call(s32[16]{0:T(128)} %get-tuple-element.573.near_ref, ...), custom_call_target="tpu_custom_call" | custom-call | flops 1000 | bytes 1000 | tf_op jit(solution)/shard_map/front/pallas_call | solution.py:70
  152.2 33.1 %attend.1 = (bf16[2048,1024]{1,0:T(8,128)(2,1)}, bf16[2048,1024]{1,0:T(8,128)(2,1)}) custom-call(bf16[2048,1024]{1,0:T(8,128)(2,1)} %get-tuple-element.297.q_ref, bf16[2048,512]{1,0:T(8,128)(2,1)} %get-tuple-element.298.k_ref, bf16[2048,512]{1,0:T(8,128)(2,1)} %get-tuple-element.299.v_ref), custom_call_target="tpu_custom_call" | custom-call | flops 1000 | bytes 1000 | tf_op jit(solution)/shard_map/attend/pallas_call | solution.py:70
  215.2 19.8 %collective-permute-done.15.gate_ref.refs_8_ = bf16[4,384,512]{2,1,0:T(8,128)(2,1)} collective-permute-done((bf16[4,384,512]{2,1,0:T(8,128)(2,1)}, bf16[4,384,512]{2,1,0:T(8,128)(2,1)}, u32[]{:S(2)}, u32[]{:S(2)}) %collective-permute-start.15) | collective-permute-done | bytes 1572896 | tf_op jit(solution)/shard_map/ppermute | solution.py:785
  237.7 12.6 %span_join.1 = bf16[16,128,1536]{2,1,0:T(8,128)(2,1)} custom-call(s32[16]{0:T(128)} %get-tuple-element.573.near_ref, s32[16]{0:T(128)} %get-tuple-element.572.far_ref, s32[16]{0:T(128)} %copy-done.37, bf16[8,128,1536]{2,1,0:T(8,128)(2,1)} %bitcast.20.a_ref, bf16[8,128,1536]{2,1,0:T(8,128)(2,1)} %bitcast.21.b_ref), custom_call_target="tpu_custom_call" | custom-call | flops 1000 | bytes 1000 | tf_op jit(solution)/shard_map/span_join/pallas_call | solution.py:70
  259.8 46.2 %collective-permute-done.17.up_ref.down_ref.refs_7_.refs_5_ = bf16[4,768,512]{2,1,0:T(8,128)(2,1)} collective-permute-done((bf16[4,768,512]{2,1,0:T(8,128)(2,1)S(1)}, bf16[4,768,512]{2,1,0:T(8,128)(2,1)}, u32[]{:S(2)}, u32[]{:S(2)}) %collective-permute-start.17) | collective-permute-done | bytes 3145760 | tf_op jit(solution)/shard_map/ppermute | solution.py:788
  306.1 15.2 %hidden_units.4 = (bf16[2048,512]{1,0:T(8,128)(2,1)}, bf16[2048,1024]{1,0:T(8,128)(2,1)}) custom-call(bf16[2048,1536]{1,0:T(8,128)(2,1)} %get-tuple-element.352.n_ref, bf16[2048,1536]{1,0:T(8,128)(2,1)} %bitcast.69, bf16[4,384,512]{2,1,0:T(8,128)(2,1)} %bitcast.14.gate_ref.refs_4_, bf16[4,768,512]{2,1,0:T(8,128)(2,1)} %bitcast.78, bf16[4,768,512]{2,1,0:T(8,128)(2,1)} %bitcast.79), custom_call_target="tpu_custom_call" | custom-call | flops 1000 | bytes 1000 | tf_op jit(solution)/shard_map/hidden_units/pallas_call | solution.py:70
  321.2 17.5 %feed_grads.4 = (bf16[1536,512]{1,0:T(8,128)(2,1)}, bf16[1536,512]{1,0:T(8,128)(2,1)}, bf16[512,1536]{1,0:T(8,128)(2,1)}) custom-call(bf16[1536,2048]{1,0:T(8,128)(2,1)} %get-tuple-element.328.n_ref, bf16[2048,1536]{1,0:T(8,128)(2,1)} %bitcast.70, bf16[2048,512]{1,0:T(8,128)(2,1)} %get-tuple-element.367.product_ref.refs_0_, ...), custom_call_target="tpu_custom_call" | custom-call | flops 1000 | bytes 1000 | tf_op jit(solution)/shard_map/feed_grads/pallas_call | solution.py:70
  339.3 15.2 %hidden_units.5 = (bf16[2048,512]{1,0:T(8,128)(2,1)}, bf16[2048,1024]{1,0:T(8,128)(2,1)}) custom-call(bf16[2048,1536]{1,0:T(8,128)(2,1)} %get-tuple-element.352.n_ref, bf16[2048,1536]{1,0:T(8,128)(2,1)} %bitcast.71, bf16[4,384,512]{2,1,0:T(8,128)(2,1)} %collective-permute-done.9.gate_ref.refs_6_, ...), custom_call_target="tpu_custom_call" | custom-call | flops 1000 | bytes 1000 | tf_op jit(solution)/shard_map/hidden_units/pallas_call | solution.py:70
  354.5 17.4 %feed_grads.5 = (bf16[1536,512]{1,0:T(8,128)(2,1)}, bf16[1536,512]{1,0:T(8,128)(2,1)}, bf16[512,1536]{1,0:T(8,128)(2,1)}) custom-call(bf16[1536,2048]{1,0:T(8,128)(2,1)} %get-tuple-element.328.n_ref, bf16[2048,1536]{1,0:T(8,128)(2,1)} %bitcast.72, bf16[2048,512]{1,0:T(8,128)(2,1)} %get-tuple-element.368.product_ref.refs_1_, ...), custom_call_target="tpu_custom_call" | custom-call | flops 1000 | bytes 1000 | tf_op jit(solution)/shard_map/feed_grads/pallas_call | solution.py:70
  372.5 15.4 %hidden_units.6 = (bf16[2048,512]{1,0:T(8,128)(2,1)}, bf16[2048,1024]{1,0:T(8,128)(2,1)}) custom-call(bf16[2048,1536]{1,0:T(8,128)(2,1)} %get-tuple-element.352.n_ref, bf16[2048,1536]{1,0:T(8,128)(2,1)} %bitcast.73, bf16[4,384,512]{2,1,0:T(8,128)(2,1)} %collective-permute-done.15.gate_ref.refs_8_, ...), custom_call_target="tpu_custom_call" | custom-call | flops 1000 | bytes 1000 | tf_op jit(solution)/shard_map/hidden_units/pallas_call | solution.py:70
  387.9 17.5 %feed_grads.6 = (bf16[1536,512]{1,0:T(8,128)(2,1)}, bf16[1536,512]{1,0:T(8,128)(2,1)}, bf16[512,1536]{1,0:T(8,128)(2,1)}) custom-call(bf16[1536,2048]{1,0:T(8,128)(2,1)} %get-tuple-element.328.n_ref, bf16[2048,1536]{1,0:T(8,128)(2,1)} %bitcast.74, bf16[2048,512]{1,0:T(8,128)(2,1)} %get-tuple-element.369.product_ref.refs_2_, ...), custom_call_target="tpu_custom_call" | custom-call | flops 1000 | bytes 1000 | tf_op jit(solution)/shard_map/feed_grads/pallas_call | solution.py:70
  410.3 15.2 %hidden_units.7 = (bf16[2048,512]{1,0:T(8,128)(2,1)}, bf16[2048,1024]{1,0:T(8,128)(2,1)}) custom-call(bf16[2048,1536]{1,0:T(8,128)(2,1)} %get-tuple-element.352.n_ref, bf16[2048,1536]{1,0:T(8,128)(2,1)} %bitcast.75, bf16[4,384,512]{2,1,0:T(8,128)(2,1)} %collective-permute-done.19.gate_ref.refs_10_, bf16[4,768,512]{2,1,0:T(8,128)(2,1)} %bitcast.86, ...), custom_call_target="tpu_custom_call" | custom-call | flops 1000 | bytes 1000 | tf_op jit(solution)/shard_map/hidden_units/pallas_call | solution.py:70
  425.5 20.6 %back_other.1 = bf16[1024,1536]{1,0:T(8,128)(2,1)} custom-call(s32[1]{0:T(128)S(6)} %mul.134.base_ref, bf16[2048,1024]{1,0:T(8,128)(2,1)} %get-tuple-element.362.both_ref.refs_0_, bf16[2048,1024]{1,0:T(8,128)(2,1)} %get-tuple-element.363.both_ref.refs_1_, bf16[2048,1024]{1,0:T(8,128)(2,1)} %get-tuple-element.364.both_ref.refs_2_, ...), custom_call_target="tpu_custom_call" | custom-call | flops 1000 | bytes 1000 | tf_op jit(solution)/shard_map/back_other/pallas_call | solution.py:70
  451.3 17.8 %feed_grads.7 = (bf16[1536,512]{1,0:T(8,128)(2,1)}, bf16[1536,512]{1,0:T(8,128)(2,1)}, bf16[512,1536]{1,0:T(8,128)(2,1)}) custom-call(bf16[1536,2048]{1,0:T(8,128)(2,1)} %get-tuple-element.328.n_ref, bf16[2048,1536]{1,0:T(8,128)(2,1)} %bitcast.76, bf16[2048,512]{1,0:T(8,128)(2,1)} %get-tuple-element.370.refs_3_.product_ref, ...), custom_call_target="tpu_custom_call" | custom-call | flops 1000 | bytes 1000 | tf_op jit(solution)/shard_map/feed_grads/pallas_call | solution.py:70
  469.1 11.6 %down_other.1 = bf16[1024,1536]{1,0:T(8,128)(2,1)} custom-call(s32[1]{0:T(128)S(6)} %mul.134.base_ref, bf16[2048,512]{1,0:T(8,128)(2,1)} %get-tuple-element.367.product_ref.refs_0_, bf16[2048,512]{1,0:T(8,128)(2,1)} %get-tuple-element.368.product_ref.refs_1_, bf16[2048,512]{1,0:T(8,128)(2,1)} %get-tuple-element.369.product_ref.refs_2_, ...), custom_call_target="tpu_custom_call" | custom-call | flops 1000 | bytes 1000 | tf_op jit(solution)/shard_map/down_other/pallas_call | solution.py:70
  488.4 24.4 %back_own.1 = (f32[1024,1536]{1,0:T(8,128)}, bf16[1024,1536]{1,0:T(8,128)(2,1)}, f32[8,1536]{1,0:T(8,128)}) custom-call(s32[1]{0:T(128)S(6)} %mul.133.base_ref, bf16[2048,1024]{1,0:T(8,128)(2,1)} %get-tuple-element.362.both_ref.refs_0_, bf16[2048,1024]{1,0:T(8,128)(2,1)} %get-tuple-element.363.both_ref.refs_1_, ...), custom_call_target="tpu_custom_call" | custom-call | flops 1000 | bytes 1000 | tf_op jit(solution)/shard_map/back_own/pallas_call | solution.py:70
  524.1 12.6 %down_own.1 = bf16[1024,1536]{1,0:T(8,128)(2,1)} custom-call(s32[1]{0:T(128)S(6)} %mul.133.base_ref, bf16[2048,512]{1,0:T(8,128)(2,1)} %get-tuple-element.367.product_ref.refs_0_, bf16[2048,512]{1,0:T(8,128)(2,1)} %get-tuple-element.368.product_ref.refs_1_, bf16[2048,512]{1,0:T(8,128)(2,1)} %get-tuple-element.369.product_ref.refs_2_, ...), custom_call_target="tpu_custom_call" | custom-call | flops 1000 | bytes 1000 | tf_op jit(solution)/shard_map/down_own/pallas_call | solution.py:70
  548.3 12.3 %mixed_back.1 = (bf16[2048,1536]{1,0:T(8,128)(2,1)}, bf16[2048,1024]{1,0:T(8,128)(2,1)}) custom-call(s32[1]{0:T(128)} %bitcast.17.core_ref, bf16[1024,1536]{1,0:T(8,128)(2,1)} %get-tuple-element.391.own_ref, bf16[1024,1536]{1,0:T(8,128)(2,1)} %copy-done.12, bf16[1024,1536]{1,0:T(8,128)(2,1)} %out_rows.1.refs_1_.w_ref), custom_call_target="tpu_custom_call" | custom-call | flops 1000 | bytes 1000 | tf_op jit(solution)/shard_map/mixed_back/pallas_call | solution.py:70
  560.5 12.0 %out_grads.1 = (bf16[4,48,1536]{2,1,0:T(8,128)(2,1)}, bf16[4,48,1536]{2,1,0:T(8,128)(2,1)}, bf16[4,48,1536]{2,1,0:T(8,128)(2,1)}, bf16[4,48,1536]{2,1,0:T(8,128)(2,1)}) custom-call(s32[1]{0:T(128)} %bitcast.18.place_ref, bf16[2048,1024]{1,0:T(8,128)(2,1)} %get-tuple-element.309.refs_0_.mixed_ref.o_ref, bf16[2048,1536]{1,0:T(8,128)(2,1)} %get-tuple-element.394.grad_ref), custom_call_target="tpu_custom_call" | custom-call | flops 1000 | bytes 1000 | tf_op jit(solution)/shard_map/out_grads/pallas_call | solution.py:70
  587.1 20.4 %attend_back.4 = (bf16[2048,256]{1,0:T(8,128)(2,1)}, bf16[2048,128]{1,0:T(8,128)(2,1)}, bf16[2048,128]{1,0:T(8,128)(2,1)}) custom-call(bf16[2048,1024]{1,0:T(8,128)(2,1)} %get-tuple-element.467.q_ref, bf16[2048,512]{1,0:T(8,128)(2,1)} %get-tuple-element.298.k_ref, bf16[2048,512]{1,0:T(8,128)(2,1)} %get-tuple-element.299.v_ref, ...), custom_call_target="tpu_custom_call" | custom-call | flops 1000 | bytes 1000 | tf_op jit(solution)/shard_map/attend_back/pallas_call | solution.py:70
  619.4 18.3 %collective-permute-done.33 = bf16[768,512]{1,0:T(8,128)(2,1)} collective-permute-done((bf16[768,512]{1,0:T(8,128)(2,1)}, bf16[768,512]{1,0:T(8,128)(2,1)}, u32[]{:S(2)}, u32[]{:S(2)}) %collective-permute-start.33) | collective-permute-done | bytes 786464 | tf_op jit(solution)/shard_map/ppermute | solution.py:789
  649.7 21.1 %attend_back.5 = (bf16[2048,256]{1,0:T(8,128)(2,1)}, bf16[2048,128]{1,0:T(8,128)(2,1)}, bf16[2048,128]{1,0:T(8,128)(2,1)}) custom-call(bf16[2048,1024]{1,0:T(8,128)(2,1)} %get-tuple-element.467.q_ref, bf16[2048,512]{1,0:T(8,128)(2,1)} %get-tuple-element.298.k_ref, bf16[2048,512]{1,0:T(8,128)(2,1)} %get-tuple-element.299.v_ref, ...), custom_call_target="tpu_custom_call" | custom-call | flops 1000 | bytes 1000 | tf_op jit(solution)/shard_map/attend_back/pallas_call | solution.py:70
  670.8 16.3 %collective-permute-done.35 = bf16[192,1536]{1,0:T(8,128)(2,1)S(1)} collective-permute-done((bf16[192,1536]{1,0:T(8,128)(2,1)}, bf16[192,1536]{1,0:T(8,128)(2,1)S(1)}, u32[]{:S(2)}, u32[]{:S(2)}) %collective-permute-start.35) | collective-permute-done | bytes 589856 | tf_op jit(solution)/shard_map/ppermute | solution.py:788
  687.3 12.0 %collective-permute-done.37 = bf16[192,1536]{1,0:T(8,128)(2,1)S(1)} collective-permute-done((bf16[192,1536]{1,0:T(8,128)(2,1)S(1)}, bf16[192,1536]{1,0:T(8,128)(2,1)S(1)}, u32[]{:S(2)}, u32[]{:S(2)}) %collective-permute-start.37) | collective-permute-done | bytes 589856 | tf_op jit(solution)/shard_map/ppermute | solution.py:789
  714.7 20.5 %attend_back.6 = (bf16[2048,256]{1,0:T(8,128)(2,1)}, bf16[2048,128]{1,0:T(8,128)(2,1)}, bf16[2048,128]{1,0:T(8,128)(2,1)}) custom-call(bf16[2048,1024]{1,0:T(8,128)(2,1)} %get-tuple-element.467.q_ref, bf16[2048,512]{1,0:T(8,128)(2,1)} %get-tuple-element.298.k_ref, bf16[2048,512]{1,0:T(8,128)(2,1)} %get-tuple-element.299.v_ref, ...), custom_call_target="tpu_custom_call" | custom-call | flops 1000 | bytes 1000 | tf_op jit(solution)/shard_map/attend_back/pallas_call | solution.py:70
  735.3 21.4 %collective-permute-done.40.refs_2_ = bf16[768,512]{1,0:T(8,128)(2,1)S(1)} collective-permute-done((bf16[768,512]{1,0:T(8,128)(2,1)S(1)}, bf16[768,512]{1,0:T(8,128)(2,1)S(1)}, u32[]{:S(2)}, u32[]{:S(2)}) %collective-permute-start.40) | collective-permute-done | bytes 786464 | tf_op jit(solution)/shard_map/ppermute | solution.py:785
  756.8 14.5 %collective-permute-done.41.refs_3_ = bf16[768,512]{1,0:T(8,128)(2,1)S(1)} collective-permute-done((bf16[768,512]{1,0:T(8,128)(2,1)S(1)}, bf16[768,512]{1,0:T(8,128)(2,1)S(1)}, u32[]{:S(2)}, u32[]{:S(2)}) %collective-permute-start.41) | collective-permute-done | bytes 786464 | tf_op jit(solution)/shard_map/ppermute | solution.py:789
  781.8 20.3 %attend_back.7 = (bf16[2048,256]{1,0:T(8,128)(2,1)}, bf16[2048,128]{1,0:T(8,128)(2,1)}, bf16[2048,128]{1,0:T(8,128)(2,1)}) custom-call(bf16[2048,1024]{1,0:T(8,128)(2,1)} %get-tuple-element.467.q_ref, bf16[2048,512]{1,0:T(8,128)(2,1)} %get-tuple-element.298.k_ref, bf16[2048,512]{1,0:T(8,128)(2,1)} %get-tuple-element.299.v_ref, ...), custom_call_target="tpu_custom_call" | custom-call | flops 1000 | bytes 1000 | tf_op jit(solution)/shard_map/attend_back/pallas_call | solution.py:70
  805.3 12.1 %in_other.1 = bf16[1024,1536]{1,0:T(8,128)(2,1)} custom-call(s32[1]{0:T(128)S(6)} %mul.134.base_ref, bf16[2048,256]{1,0:T(8,128)(2,1)} %get-tuple-element.477.q_ref.refs_0_, bf16[2048,128]{1,0:T(8,128)(2,1)} %get-tuple-element.478.k_ref.refs_1_, bf16[2048,128]{1,0:T(8,128)(2,1)} %get-tuple-element.479.v_ref.refs_2_, ...), custom_call_target="tpu_custom_call" | custom-call | flops 1000 | bytes 1000 | tf_op jit(solution)/shard_map/in_other/pallas_call | solution.py:70
  856.2 15.2 %in_own.1 = (bf16[1024,1536]{1,0:T(8,128)(2,1)}, f32[8,1536]{1,0:T(8,128)}) custom-call(s32[1]{0:T(128)S(6)} %mul.133.base_ref, bf16[2048,256]{1,0:T(8,128)(2,1)} %get-tuple-element.477.q_ref.refs_0_, bf16[2048,128]{1,0:T(8,128)(2,1)} %get-tuple-element.478.k_ref.refs_1_, bf16[2048,128]{1,0:T(8,128)(2,1)} %get-tuple-element.479.v_ref.refs_2_, ...), custom_call_target="tpu_custom_call" | custom-call | flops 1000 | bytes 1000 | tf_op jit(solution)/shard_map/in_own/pallas_call | solution.py:70
  (359 shorter events, 340.9 us)
Async XLA Ops:
  7.2 54.2 %all-gather.5.cloned.1.call-start = ((), (), s32[]{:S(2)}) async-start(), calls=%async_computation.7 | async-start | bytes 2273280 | tf_op jit(solution)/shard_map/all_gather | solution.py:792
  17.4 90.3 %all-gather.7.cloned.1.call-start = ((), (), s32[]{:S(2)}) async-start(), calls=%async_computation.8 | async-start | bytes 1966080 | tf_op jit(solution)/shard_map/all_gather | solution.py:792
  17.4 37.5 %collective-permute-start = (bf16[512,1536]{1,0:T(8,128)(2,1)S(1)}, bf16[512,1536]{1,0:T(8,128)(2,1)}, u32[]{:S(2)}, u32[]{:S(2)}) collective-permute-start(bf16[512,1536]{1,0:T(8,128)(2,1)S(1)} %get-tuple-element.267), channel_id=1, source_target_pairs={{0,4},{2,6},{4,0},{6,2},{1,5},{3,7},{5,1},{7,3},{8,12},{10,14},{12... | collective-permute-start | bytes 4718600 | tf_op jit(solution)/shard_map/ppermute | solution.py:785
  68.7 118.4 %all-gather.9.cloned.1.call-start = ((), (), s32[]{:S(2)}) async-start(), calls=%async_computation.9 | async-start | bytes 3932160 | tf_op jit(solution)/shard_map/all_gather | solution.py:792
  115.4 190.6 %all-gather.11.cloned.1.call-start = ((), (), s32[]{:S(2)}) async-start(), calls=%async_computation.10 | async-start | bytes 3932160 | tf_op jit(solution)/shard_map/all_gather | solution.py:792
  115.7 69.6 %collective-permute-start.8 = (bf16[512,1536]{1,0:T(8,128)(2,1)}, bf16[512,1536]{1,0:T(8,128)(2,1)S(1)}, u32[]{:S(2)}, u32[]{:S(2)}) collective-permute-start(bf16[512,1536]{1,0:T(8,128)(2,1)} %get-tuple-element.303), channel_id=1, source_target_pairs={{0,4},{2,6},{4,0},{6,2},{1,5},{3,7},{5,1},{7,3},{8,12},{10,14},{12... | collective-permute-start | bytes 4718600 | tf_op jit(solution)/shard_map/ppermute | solution.py:785
  117.2 70.0 %collective-permute-start.9 = (bf16[4,384,512]{2,1,0:T(8,128)(2,1)}, bf16[4,384,512]{2,1,0:T(8,128)(2,1)}, u32[]{:S(2)}, u32[]{:S(2)}) collective-permute-start(bf16[4,384,512]{2,1,0:T(8,128)(2,1)} %bitcast.14.gate_ref.refs_4_), channel_id=1, source_target_pairs={{0,1},{1,0},{2,3},{3,2},{4,5},{5,4},{6,7},{7,6},{8,9},{9,8},{10,11... | collective-permute-start | bytes 4718600 | tf_op jit(solution)/shard_map/ppermute | solution.py:788
  118.6 68.5 %collective-permute-start.10 = (bf16[4,192,384]{2,1,0:T(8,128)(2,1)S(1)}, bf16[4,192,384]{2,1,0:T(8,128)(2,1)}, u32[]{:S(2)}, u32[]{:S(2)}) collective-permute-start(bf16[4,192,384]{2,1,0:T(8,128)(2,1)S(1)} %copy-done.13), channel_id=1, source_target_pairs={{0,1},{1,0},{2,3},{3,2},{4,5},{5,4},{6,7},{7,6},{8,9},{9,8},{10,11... | collective-permute-start | bytes 1769480 | tf_op jit(solution)/shard_map/ppermute | solution.py:788
  119.2 68.0 %collective-permute-start.11 = (bf16[4,192,384]{2,1,0:T(8,128)(2,1)S(1)}, bf16[4,192,384]{2,1,0:T(8,128)(2,1)}, u32[]{:S(2)}, u32[]{:S(2)}) collective-permute-start(bf16[4,192,384]{2,1,0:T(8,128)(2,1)S(1)} %copy-done.13), channel_id=1, source_target_pairs={{0,4},{2,6},{4,0},{6,2},{1,5},{3,7},{5,1},{7,3},{8,12},{10,14},{12... | collective-permute-start | bytes 1769480 | tf_op jit(solution)/shard_map/ppermute | solution.py:785
  119.8 67.4 %collective-permute-start.12 = (bf16[4,192,384]{2,1,0:T(8,128)(2,1)S(1)}, bf16[4,192,384]{2,1,0:T(8,128)(2,1)}, u32[]{:S(2)}, u32[]{:S(2)}) collective-permute-start(bf16[4,192,384]{2,1,0:T(8,128)(2,1)S(1)} %copy-done.13), channel_id=1, source_target_pairs={{0,5},{1,4},{2,7},{3,6},{4,1},{5,0},{6,3},{7,2},{8,13},{9,12},{10,... | collective-permute-start | bytes 1769480 | tf_op jit(solution)/shard_map/ppermute | solution.py:789
  199.0 325.0 %reduce-scatter.8.cloned.1.call-start = ((), (), s32[]{:S(2)}) async-start(), calls=%async_computation.11 | async-start | bytes 1966080 | tf_op jit(solution)/shard_map/reduce_scatter | solution.py:799
  235.0 71.1 %collective-permute-start.17 = (bf16[4,768,512]{2,1,0:T(8,128)(2,1)S(1)}, bf16[4,768,512]{2,1,0:T(8,128)(2,1)}, u32[]{:S(2)}, u32[]{:S(2)}) collective-permute-start(bf16[4,768,512]{2,1,0:T(8,128)(2,1)S(1)} %bitcast.84), channel_id=1, source_target_pairs={{0,1},{1,0},{2,3},{3,2},{4,5},{5,4},{6,7},{7,6},{8,9},{9,8},{10,11... | collective-permute-start | bytes 9437192 | tf_op jit(solution)/shard_map/ppermute | solution.py:788
  235.6 103.7 %collective-permute-start.18 = (bf16[4,768,512]{2,1,0:T(8,128)(2,1)S(1)}, bf16[4,768,512]{2,1,0:T(8,128)(2,1)}, u32[]{:S(2)}, u32[]{:S(2)}) collective-permute-start(bf16[4,768,512]{2,1,0:T(8,128)(2,1)S(1)} %bitcast.85), channel_id=1, source_target_pairs={{0,4},{2,6},{4,0},{6,2},{1,5},{3,7},{5,1},{7,3},{8,12},{10,14},{12... | collective-permute-start | bytes 9437192 | tf_op jit(solution)/shard_map/ppermute | solution.py:785
  236.2 103.1 %collective-permute-start.19 = (bf16[4,384,512]{2,1,0:T(8,128)(2,1)}, bf16[4,384,512]{2,1,0:T(8,128)(2,1)}, u32[]{:S(2)}, u32[]{:S(2)}) collective-permute-start(bf16[4,384,512]{2,1,0:T(8,128)(2,1)} %collective-permute-done.15.gate_ref.refs_8_), channel_id=1, source_target_pairs={{0,1},{1,0},{2,3},{3,2},{4,5},{5,4},{6,7},{7,6},{8,9},{9,8},{10,11... | collective-permute-start | bytes 4718600 | tf_op jit(solution)/shard_map/ppermute | solution.py:788
  448.4 38.4 %collective-permute-start.23 = (bf16[1024,1536]{1,0:T(8,128)(2,1)}, bf16[1024,1536]{1,0:T(8,128)(2,1)S(1)}, u32[]{:S(2)}, u32[]{:S(2)}) collective-permute-start(bf16[1024,1536]{1,0:T(8,128)(2,1)} %back_other.1), channel_id=1, source_target_pairs={{0,2},{2,0},{4,6},{6,4},{1,3},{3,1},{5,7},{7,5},{8,10},{10,8},{12,... | collective-permute-start | bytes 9437192 | tf_op jit(solution)/shard_map/ppermute | solution.py:786
  486.8 37.3 %collective-permute-start.26 = (bf16[1024,1536]{1,0:T(8,128)(2,1)}, bf16[1024,1536]{1,0:T(8,128)(2,1)}, u32[]{:S(2)}, u32[]{:S(2)}) collective-permute-start(bf16[1024,1536]{1,0:T(8,128)(2,1)} %down_other.1), channel_id=1, source_target_pairs={{0,2},{2,0},{4,6},{6,4},{1,3},{3,1},{5,7},{7,5},{8,10},{10,8},{12,... | collective-permute-start | bytes 9437192 | tf_op jit(solution)/shard_map/ppermute | solution.py:786
  486.8 95.9 %reduce-scatter.10.cloned.1.call-start = ((), (), s32[]{:S(2)}) async-start(), calls=%async_computation.12 | async-start | bytes 1966080 | tf_op jit(solution)/shard_map/reduce_scatter | solution.py:799
  486.8 37.2 %collective-permute-start.27 = (bf16[1536,512]{1,0:T(8,128)(2,1)}, bf16[1536,512]{1,0:T(8,128)(2,1)}, u32[]{:S(2)}, u32[]{:S(2)}) collective-permute-start(bf16[1536,512]{1,0:T(8,128)(2,1)} %get-tuple-element.381), channel_id=1, source_target_pairs={{0,4},{2,6},{4,0},{6,2},{1,5},{3,7},{5,1},{7,3},{8,12},{10,14},{12... | collective-permute-start | bytes 4718600 | tf_op jit(solution)/shard_map/ppermute | solution.py:785
  524.1 113.6 %reduce-scatter.12.cloned.1.call-start = ((), (), s32[]{:S(2)}) async-start(), calls=%async_computation.13 | async-start | bytes 1966080 | tf_op jit(solution)/shard_map/reduce_scatter | solution.py:799
  540.9 158.5 %reduce-scatter.14.cloned.1.call-start = ((), (), s32[]{:S(2)}) async-start(), calls=%async_computation.14 | async-start | bytes 1966080 | tf_op jit(solution)/shard_map/reduce_scatter | solution.py:799
  541.5 41.2 %collective-permute-start.29 = (bf16[512,1536]{1,0:T(8,128)(2,1)}, bf16[512,1536]{1,0:T(8,128)(2,1)}, u32[]{:S(2)}, u32[]{:S(2)}) collective-permute-start(bf16[512,1536]{1,0:T(8,128)(2,1)} %get-tuple-element.399), channel_id=1, source_target_pairs={{0,5},{1,4},{2,7},{3,6},{4,1},{5,0},{6,3},{7,2},{8,13},{9,12},{10,... | collective-permute-start | bytes 4718600 | tf_op jit(solution)/shard_map/ppermute | solution.py:789
  582.7 188.6 %reduce-scatter.16.cloned.1.call-start = ((), (), s32[]{:S(2)}) async-start(), calls=%async_computation.15 | async-start | bytes 1966080 | tf_op jit(solution)/shard_map/reduce_scatter | solution.py:799
  585.6 52.0 %collective-permute-start.33 = (bf16[768,512]{1,0:T(8,128)(2,1)}, bf16[768,512]{1,0:T(8,128)(2,1)}, u32[]{:S(2)}, u32[]{:S(2)}) collective-permute-start(bf16[768,512]{1,0:T(8,128)(2,1)} %pad_maximum_fusion.8), channel_id=1, source_target_pairs={{0,5},{1,4},{2,7},{3,6},{4,1},{5,0},{6,3},{7,2},{8,13},{9,12},{10,... | collective-permute-start | bytes 2359304 | tf_op jit(solution)/shard_map/ppermute | solution.py:789
  645.5 53.8 %collective-permute-start.34 = (bf16[1536,384]{1,0:T(8,128)(2,1)}, bf16[1536,384]{1,0:T(8,128)(2,1)S(1)}, u32[]{:S(2)}, u32[]{:S(2)}) collective-permute-start(bf16[1536,384]{1,0:T(8,128)(2,1)} %qkv_grad.4), channel_id=1, source_target_pairs={{0,5},{1,4},{2,7},{3,6},{4,1},{5,0},{6,3},{7,2},{8,13},{9,12},{10,... | collective-permute-start | bytes 3538952 | tf_op jit(solution)/shard_map/ppermute | solution.py:789
  646.1 156.0 %reduce-scatter.18.cloned.1.call-start = ((), (), s32[]{:S(2)}) async-start(), calls=%async_computation.16 | async-start | bytes 737280 | tf_op jit(solution)/shard_map/reduce_scatter | solution.py:799
  646.2 41.0 %collective-permute-start.35 = (bf16[192,1536]{1,0:T(8,128)(2,1)}, bf16[192,1536]{1,0:T(8,128)(2,1)S(1)}, u32[]{:S(2)}, u32[]{:S(2)}) collective-permute-start(bf16[192,1536]{1,0:T(8,128)(2,1)} %bitcast.25), channel_id=1, source_target_pairs={{0,1},{1,0},{2,3},{3,2},{4,5},{5,4},{6,7},{7,6},{8,9},{9,8},{10,11... | collective-permute-start | bytes 1769480 | tf_op jit(solution)/shard_map/ppermute | solution.py:788
  647.7 39.6 %collective-permute-start.36 = (bf16[192,1536]{1,0:T(8,128)(2,1)}, bf16[192,1536]{1,0:T(8,128)(2,1)S(1)}, u32[]{:S(2)}, u32[]{:S(2)}) collective-permute-start(bf16[192,1536]{1,0:T(8,128)(2,1)} %bitcast.26), channel_id=1, source_target_pairs={{0,4},{2,6},{4,0},{6,2},{1,5},{3,7},{5,1},{7,3},{8,12},{10,14},{12... | collective-permute-start | bytes 1769480 | tf_op jit(solution)/shard_map/ppermute | solution.py:785
  649.1 50.2 %collective-permute-start.37 = (bf16[192,1536]{1,0:T(8,128)(2,1)S(1)}, bf16[192,1536]{1,0:T(8,128)(2,1)S(1)}, u32[]{:S(2)}, u32[]{:S(2)}) collective-permute-start(bf16[192,1536]{1,0:T(8,128)(2,1)S(1)} %bitcast.121), channel_id=1, source_target_pairs={{0,5},{1,4},{2,7},{3,6},{4,1},{5,0},{6,3},{7,2},{8,13},{9,12},{10,... | collective-permute-start | bytes 1769480 | tf_op jit(solution)/shard_map/ppermute | solution.py:789
  710.8 60.5 %collective-permute-start.38 = (bf16[1536,384]{1,0:T(8,128)(2,1)}, bf16[1536,384]{1,0:T(8,128)(2,1)}, u32[]{:S(2)}, u32[]{:S(2)}) collective-permute-start(bf16[1536,384]{1,0:T(8,128)(2,1)} %qkv_grad.5), channel_id=1, source_target_pairs={{0,4},{2,6},{4,0},{6,2},{1,5},{3,7},{5,1},{7,3},{8,12},{10,14},{12... | collective-permute-start | bytes 3538952 | tf_op jit(solution)/shard_map/ppermute | solution.py:785
  711.9 44.8 %collective-permute-start.40 = (bf16[768,512]{1,0:T(8,128)(2,1)S(1)}, bf16[768,512]{1,0:T(8,128)(2,1)S(1)}, u32[]{:S(2)}, u32[]{:S(2)}) collective-permute-start(bf16[768,512]{1,0:T(8,128)(2,1)S(1)} %add_convert_fusion.4.refs_0_), channel_id=1, source_target_pairs={{0,4},{2,6},{4,0},{6,2},{1,5},{3,7},{5,1},{7,3},{8,12},{10,14},{12... | collective-permute-start | bytes 2359304 | tf_op jit(solution)/shard_map/ppermute | solution.py:785
  713.5 57.8 %collective-permute-start.41 = (bf16[768,512]{1,0:T(8,128)(2,1)S(1)}, bf16[768,512]{1,0:T(8,128)(2,1)S(1)}, u32[]{:S(2)}, u32[]{:S(2)}) collective-permute-start(bf16[768,512]{1,0:T(8,128)(2,1)S(1)} %add_convert_fusion.4.refs_0_), channel_id=1, source_target_pairs={{0,5},{1,4},{2,7},{3,6},{4,1},{5,0},{6,3},{7,2},{8,13},{9,12},{10,... | collective-permute-start | bytes 2359304 | tf_op jit(solution)/shard_map/ppermute | solution.py:789
  735.2 146.8 %reduce-scatter.20.cloned.1.call-start = ((), (), s32[]{:S(2)}) async-start(), calls=%async_computation.17 | async-start | bytes 1474560 | tf_op jit(solution)/shard_map/reduce_scatter | solution.py:799
  (92 other events, 1572.5 us)
Sparse Core Ops, SparseCore 0:
  17.5 43.8 all-gather.4
  68.9 34.3 all-gather.6
  114.8 62.3 all-gather.8
  199.1 61.5 all-gather.10
  486.9 33.4 reduce-scatter.7
  524.2 33.4 reduce-scatter.9
  560.0 34.2 reduce-scatter.11
  596.6 34.2 reduce-scatter.13
  646.3 34.2 reduce-scatter.15
  735.4 20.4 reduce-scatter.17
  854.6 27.3 reduce-scatter.19

commit v2 on v1

--- a/solution.py
+++ b/solution.py
@@ -50,7 +50,7 @@
     return lax.dot_general(left, right, TN, preferred_element_type=f32)
 
 
-def params(limit=60):
+def params(limit):
     return pltpu.CompilerParams(vmem_limit_bytes=limit * MIB)
 
 
@@ -63,17 +63,21 @@
 
 
 def part(block, index):
-    return pl.BlockSpec(block, lambda *_: index)
-
-
-def call(kernel, grid, in_specs, out_specs, out_shape, operands, name, prefetch=(), scratch=()):
+    return pl.BlockSpec(block, lambda *_: index, pipeline_mode=pl.Buffered(1))
+
+
+def fixed(shape):
+    return part(shape, (0,) * len(shape))
+
+
+def call(kernel, grid, in_specs, out_specs, out_shape, operands, name, prefetch=(), scratch=(), limit=60):
     return pl.pallas_call(
         kernel,
         grid_spec=pltpu.PrefetchScalarGridSpec(
             num_scalar_prefetch=len(prefetch), grid=grid, in_specs=in_specs, out_specs=out_specs, scratch_shapes=list(scratch)
         ),
         out_shape=[jax.ShapeDtypeStruct(shape, dtype) for shape, dtype in out_shape],
-        compiler_params=params(),
+        compiler_params=params(limit),
         cost_estimate=short(),
         name=name,
     )(*prefetch, *operands)
@@ -176,7 +180,7 @@
         front_kernel,
         (rows // tile,),
         span_specs(width, spans)
-        + [rows_spec(LANES), rows_spec(LANES), whole(gain.shape), whole(spread.shape)]
+        + [rows_spec(LANES), rows_spec(LANES), fixed(gain.shape), fixed(spread.shape)]
         + [part((p.shape[0], depth, p.shape[2]), (0, 0, 0)) for p in pieces],
         [rows_spec(width), rows_spec(width), pl.BlockSpec((width, tile), lambda i, *_: (0, i))]
         + [rows_spec(q_width), rows_spec(k_width), rows_spec(k_width), whole((n_shard * depth, total))],
@@ -368,7 +372,7 @@
     pair_out = pl.BlockSpec((rows, Q_LANES), lambda g: (0, g))
     single_out = pl.BlockSpec((rows, LANES), lambda g: (0, g))
     stacked = (tiles, GROUPS * Q_TILE, LANES)
-    table = whole((rows, LANES))
+    table = fixed((rows, LANES))
     return call(
         attend_back_kernel,
         (groups,),
@@ -439,7 +443,7 @@
     return call(
         kernel,
         (2 * steps,),
-        [pl.BlockSpec((units, rows), early), pl.BlockSpec((rows, units), late), whole(product.shape), whole(d_both.shape)],
+        [pl.BlockSpec((units, rows), early), pl.BlockSpec((rows, units), late), fixed(product.shape), fixed(d_both.shape)],
         [pl.BlockSpec((units, units), early), pl.BlockSpec((units, units), early), pl.BlockSpec((units, units), late)],
         [((width, units), bf16), ((width, units), bf16), ((units, width), bf16)],
         [normed_t, cot, product, d_both],
@@ -485,7 +489,7 @@
 
     in_specs = [shifted(a.shape[1]) for a in lhs] + [part(block, index) for _, block, index in rhs]
     for a, kind in others:
-        in_specs.append(whole(a.shape) if kind == "whole" else {"shifted": shifted, "plain": plain}[kind](a.shape[1]))
+        in_specs.append(fixed(a.shape) if kind == "whole" else {"shifted": shifted, "plain": plain}[kind](a.shape[1]))
     out_specs = [plain(shape[1]) if shape[0] == rows else whole(shape) for shape, _ in outs]
     n_lhs, n_rhs, n_other = len(lhs), len(rhs), len(others)
 
@@ -521,34 +525,44 @@
     return [own, far]
 
 
-def place_half(core_ref, tiles, own_ref, far_ref, out_ref):
+def place_half(core_ref, tiles, own_refs, far_refs, out_ref):
     is_own = pl.program_id(0) // tiles == core_ref[0]
+
+    def place(refs):
+        start = 0
+        for ref in refs:
+            out_ref[:, start : start + ref.shape[1]] = ref[...]
+            start += ref.shape[1]
 
     @pl.when(is_own)
     def _():
-        out_ref[...] = own_ref[...]
+        place(own_refs)
 
     @pl.when(jnp.logical_not(is_own))
     def _():
-        out_ref[...] = far_ref[...]
+        place(far_refs)
 
 
 def join_halves(core, own, far):
-    rows, width = own.shape
+    rows, cols = own[0].shape
+    count = len(own)
+    width = count * cols
     tile = 256
     tiles = rows // tile
 
-    def kernel(core_ref, own_ref, far_ref, out_ref, turned_ref):
-        place_half(core_ref, tiles, own_ref, far_ref, out_ref)
+    def kernel(core_ref, *refs):
+        out_ref, turned_ref = refs[2 * count :]
+        place_half(core_ref, tiles, refs[:count], refs[count : 2 * count], out_ref)
         turned_ref[...] = out_ref[...].T
 
+    own_spec, far_spec = half_specs(tile, tiles, cols)
     return call(
         kernel,
         (2 * tiles,),
-        half_specs(tile, tiles, width),
+        [own_spec] * count + [far_spec] * count,
         [pl.BlockSpec((tile, width), lambda i, _: (i, 0)), pl.BlockSpec((width, tile), lambda i, _: (0, i))],
         [((2 * rows, width), bf16), ((width, 2 * rows), bf16)],
-        [own, far],
+        [*own, *far],
         "join_halves",
         [core],
     )
@@ -561,13 +575,13 @@
     tiles = rows // tile
 
     def kernel(core_ref, own_ref, far_ref, w_ref, out_ref, grad_ref):
-        place_half(core_ref, tiles, own_ref, far_ref, out_ref)
+        place_half(core_ref, tiles, [own_ref], [far_ref], out_ref)
         grad_ref[...] = dot_nt(out_ref[...], w_ref[...]).astype(bf16)
 
     return call(
         kernel,
         (2 * tiles,),
-        half_specs(tile, tiles, width) + [whole(w_out_rows.shape)],
+        half_specs(tile, tiles, width) + [fixed(w_out_rows.shape)],
         [pl.BlockSpec((tile, width), lambda i, _: (i, 0)), pl.BlockSpec((tile, heads), lambda i, _: (i, 0))],
         [((2 * rows, width), bf16), ((2 * rows, heads), bf16)],
         [own, far, w_out_rows],
@@ -594,7 +608,7 @@
     (out,) = call(
         kernel,
         (1,),
-        [whole((n_shard, rows_in, cols))] * quarters,
+        [fixed((n_shard, rows_in, cols))] * quarters,
         [whole(shape)],
         [(shape, bf16)],
         blocks,
@@ -623,7 +637,7 @@
     return call(
         kernel,
         (quarters,),
-        [pl.BlockSpec((rows, Q_LANES), lambda g, _: (0, g)), whole((rows, width))],
+        [pl.BlockSpec((rows, Q_LANES), lambda g, _: (0, g)), fixed((rows, width))],
         [whole((quarters, HALF, width))] * quarters,
         [((quarters, HALF, width), bf16)] * quarters,
         [mixed, grad],
@@ -648,10 +662,10 @@
         (width // tile,),
         [
             pl.BlockSpec((tile, rows), lambda i: (i, 0)),
-            whole(d_query.shape),
-            whole(d_key.shape),
-            whole(d_value.shape),
-            whole(spread.shape),
+            fixed(d_query.shape),
+            fixed(d_key.shape),
+            fixed(d_value.shape),
+            fixed(spread.shape),
         ],
         [pl.BlockSpec((tile, GROUP_COLS), lambda i: (i, 0))],
         [((width, GROUP_COLS), bf16)],
@@ -710,7 +724,7 @@
     return call(
         kernel,
         (count,),
-        [whole((depth, width))] * count,
+        [fixed((depth, width))] * count,
         [
             pl.BlockSpec((down_depth, width), lambda i, where: (unit_at(i, where), 0)),
             pl.BlockSpec((out_depth, width), lambda i, where: (unit_at(i, where), 0)),
@@ -757,7 +771,7 @@
 
     shapes = [(depth, quarters * split * w) for w in (Q_COLS, HEAD_DIM, HEAD_DIM)]
     return call(
-        kernel, (1,), [whole((depth, cols))] * count, [whole(s) for s in shapes], [(s, f32) for s in shapes], pieces, "head_columns", [where]
+        kernel, (1,), [fixed((depth, cols))] * count, [whole(s) for s in shapes], [(s, f32) for s in shapes], pieces, "head_columns", [where]
     )
 
 
@@ -821,8 +835,7 @@
         [columns_of(w_query, Q_COLS), columns_of(w_key, HEAD_DIM), columns_of(w_value, HEAD_DIM)], axis=1
     )
     gains = jnp.pad(jnp.stack([attn_gain, mlp_gain]), ((0, PAD_ROWS - 2), (0, 0)))
-    out_piece = stacked(lax.dynamic_slice_in_dim(w_out, unit_at * HALF, HALF, 0), GROUP_COLS)
-    head_piece = jnp.concatenate([head_piece, gains, out_piece], axis=0)
+    head_piece = jnp.concatenate([head_piece, gains], axis=0)
 
     def second_piece(at):
         return jnp.concatenate([units_of(w_up, at), stacked(lax.dynamic_slice_in_dim(w_down, at * unit_cols, unit_cols, 0), units)], axis=0)
@@ -830,21 +843,20 @@
     own_tokens, sent_tokens = pick(tokens, seq, 0), pick(tokens, 1 - seq, 0)
     positions = pick(token_positions, seq, 0)
     sent_positions = pick(token_positions, 1 - seq, 0)
-    head_piece, own_tokens, sent_tokens, positions, sent_positions, w_gate, w_up, w_down = fence(
-        head_piece, own_tokens, sent_tokens, positions, sent_positions, w_gate, w_up, w_down
+    head_piece, own_tokens, sent_tokens, positions, sent_positions, w_out, w_gate, w_up, w_down = fence(
+        head_piece, own_tokens, sent_tokens, positions, sent_positions, w_out, w_gate, w_up, w_down
     )
     head_own = over_z(head_piece)
     positions = jnp.stack([positions, over_x(sent_positions)])
     x_near = jnp.concatenate([own_tokens, over_x(sent_tokens)], axis=0)
-    head_rows = gain_width + PAD_ROWS
-    head_sent, out_own = head_own[:, :head_rows], head_own[:, head_rows:]
+    out_piece = stacked(lax.dynamic_slice_in_dim(w_out, unit_at * HALF, HALF, 0), GROUP_COLS)
     gate_piece, second_own, second_last = units_of(w_gate, unit_at), second_piece(unit_at), second_piece(unit_at ^ 3)
-    head_own, head_sent, out_own, x_near, positions, gate_piece, second_own, second_last, cotangent = fence(
-        head_own, head_sent, out_own, x_near, positions, gate_piece, second_own, second_last, cotangent
-    )
-
-    gate_own = over_z(gate_piece)
-    head_x, head_y, x_far = over_x(head_sent), over_y(head_sent), over_core(x_near)
+    head_own, out_piece, x_near, positions, gate_piece, second_own, second_last, cotangent = fence(
+        head_own, out_piece, x_near, positions, gate_piece, second_own, second_last, cotangent
+    )
+
+    out_own, gate_own = over_z(out_piece), over_z(gate_piece)
+    head_x, head_y, x_far = over_x(head_own), over_y(head_own), over_core(x_near)
     positions = jnp.concatenate([positions, over_core(positions)], axis=0).reshape(-1, SPAN)
     cot_own, cot_sent = pick(cotangent, seq, 0), pick(cotangent, 1 - seq, 0)
     order = pick(span_order, seq, 0)
@@ -859,9 +871,7 @@
         jnp.where(from_far == 0, 0, side_place).astype(jnp.int32),
         from_far.astype(jnp.int32),
     ]
-    head_x, head_y, x_far, positions, cot_own, cot_sent, out_own = fence(
-        head_x, head_y, x_far, positions, cot_own, cot_sent, out_own
-    )
+    head_x, head_y, x_far, positions, cot_own, cot_sent = fence(head_x, head_y, x_far, positions, cot_own, cot_sent)
 
     middle = n_shard // 2
     head_last = [over_x(head_y[:middle]), over_y(head_x[middle:])]
@@ -888,13 +898,14 @@
     cot_received, gate_y = over_x(cot_sent), over_y(gate_own)
     mixed, q_aug = attend(queries, keys, values)
     cot_near = jnp.concatenate([cot_own, cot_received], axis=0)
-    mixed, q_aug, cot_near, gate_y, second_own, second_last, gate_sent, *out_blocks = fence(
-        mixed, q_aug, cot_near, gate_y, second_own, second_last, gate_own, *out_blocks
+    up_own, down_own = second_own[:, :gain_width], second_own[:, gain_width:]
+    mixed, q_aug, cot_near, gate_y, up_own, down_own, second_last, gate_sent, *out_blocks = fence(
+        mixed, q_aug, cot_near, gate_y, up_own, down_own, second_last, gate_own, *out_blocks
     )
 
     second_last = over_z(second_last)
     gate_x, cot_far = over_x(gate_sent), over_core(cot_near)
-    second_y = over_y(second_own)
+    up_y = over_y(up_own)
     place_at = place.astype(jnp.int32)[None]
     w_out_rows = out_rows(place_at, out_blocks)
     mine = core.astype(jnp.int32)[None]
@@ -903,13 +914,6 @@
     tiles_half = half_rows // row_tile
     full_out = (w_out_rows, w_out_rows.shape, (0, 0))
 
-    def partial_rows(lhs, rhs, dots, name):
-        def body(left, right, _, outs):
-            dots(left, right, lambda at, total: outs[0].__setitem__((slice(None), at), total.astype(bf16)))
-
-        tile = 512
-        return sum_rows_call(body, other * (half_rows // tile), lhs, rhs, [], [((half_rows, width), bf16)], tile, name)[0]
-
     def out_dot(left, right, store):
         store(slice(None), matmul(left[0][...], right[0][...]))
 
@@ -936,67 +940,90 @@
         dots(left, right, lambda at, total: found.append(total))
         return found[0]
 
-    received = over_core(partial_rows([mixed], [full_out], out_dot, "out_other"))
+    thirds = [slice(units * j, units * (j + 1)) for j in range(width // units)]
+
+    def sent_parts(lhs, rhs, dots, name):
+        def body(left, right, _, outs):
+            def store(at, total):
+                start = at.start or 0
+                for out, place_of in zip(outs, thirds):
+                    if start <= place_of.start < start + total.shape[1]:
+                        out[...] = total[:, place_of.start - start : place_of.stop - start].astype(bf16)
+
+            dots(left, right, store)
+
+        tile = half_rows // 2
+        return sum_rows_call(body, other * 2, lhs, rhs, [], [((half_rows, units), bf16)] * len(thirds), tile, name)
+
+    def joined(refs):
+        return jnp.concatenate([r[...] for r in refs], axis=1).astype(f32)
+
+    received = [over_core(a) for a in sent_parts([mixed], [full_out], out_dot, "out_other")]
 
     def hidden_body(left, right, others, outs):
-        x_ref, received_ref, gain_ref = others
-        hidden = x_ref[...].astype(f32) + kept(out_dot, left, right) + received_ref[...].astype(f32)
+        x_ref, *received_refs, gain_ref = others
+        hidden = x_ref[...].astype(f32) + kept(out_dot, left, right) + joined(received_refs)
         outs[0][...] = hidden
-        outs[1][...] = (hidden * rms_scale(hidden) * gain_ref[...]).astype(bf16)
-
-    hidden, normed_two_own = sum_rows_call(
+        normed_rows = (hidden * rms_scale(hidden) * gain_ref[...]).astype(bf16)
+        for out, at in zip(outs[1:], thirds):
+            out[...] = normed_rows[:, at]
+
+    hidden, *normed_two_own = sum_rows_call(
         hidden_body,
         mine * tiles_half,
         [mixed],
         [full_out],
-        [(x, "shifted"), (received, "plain"), (gain_two, "whole")],
-        [((half_rows, width), f32), ((half_rows, width), bf16)],
+        [(x, "shifted"), *[(r, "plain") for r in received], (gain_two, "whole")],
+        [((half_rows, width), f32)] + [((half_rows, units), bf16)] * len(thirds),
         row_tile,
         "out_own",
     )
-    normed_two_own, cot_far, gate_x, second_own = fence(normed_two_own, cot_far, gate_x, second_own)
-    second_x = over_x(second_own)
+    normed_two_far = [over_core(a) for a in normed_two_own]
     cot = span_join(places, cot_near, cot_far)
-    normed_two, normed_two_t = join_halves(mine, normed_two_own, over_core(normed_two_own))
-    normed_two, normed_two_t, cot, second_y, second_last = fence(normed_two, normed_two_t, cot, second_y, second_last)
-
-    def feed(normed_two, cot, gate, second, with_grads=True):
-        weights = [whole_of(gate), third_of(second, 0), third_of(second, 1)]
+    normed_two_own, normed_two_far, cot, gate_x, up_y, up_own, down_own = fence(
+        normed_two_own, normed_two_far, cot, gate_x, up_y, up_own, down_own
+    )
+    up_x, down_y = over_x(up_own), over_y(down_own)
+    normed_two, normed_two_t = join_halves(mine, normed_two_own, normed_two_far)
+    normed_two, normed_two_t, cot, down_own = fence(normed_two, normed_two_t, cot, down_own)
+
+    def feed(normed_two, cot, weights, with_grads=True):
         product, d_both = hidden_units(normed_two, cot, weights)
         if not with_grads:
             return weights, product, d_both
         return weights, product, d_both, feed_grads(normed_two_t, cot, product, d_both)
 
-    gate_last = over_y(gate_x)
-    fed = [feed(normed_two, cot, gate_own, second_own)]
-    own_grads, normed_two, second_x, gate_last = fence(fed[0][3], normed_two, second_x, gate_last)
-    fed.append(feed(normed_two, cot, gate_y, second_y))
-    (gate_gy, up_gy, down_gy), normed_two = fence(fed[1][3], normed_two)
+    def apart(*arrays):
+        return [whole_of(a) for a in arrays]
+
+    fed = [feed(normed_two, cot, apart(gate_own, up_own, down_own))]
+    own_grads, normed_two, up_x, down_y, gate_x, down_own = fence(fed[0][3], normed_two, up_x, down_y, gate_x, down_own)
+    gate_last, down_x = over_y(gate_x), over_x(down_own)
+    fed.append(feed(normed_two, cot, apart(gate_y, up_y, down_y)))
+    (gate_gy, up_gy, down_gy), normed_two, gate_last, down_x, second_last = fence(fed[1][3], normed_two, gate_last, down_x, second_last)
     down_gy = over_y(down_gy)
-    fed.append(feed(normed_two, cot, gate_x, second_x))
-    (gate_gx, up_gx, down_gx), normed_two, gate_gy, up_gy, down_gy = fence(fed[2][3], normed_two, gate_gy, up_gy, down_gy)
-    gate_gy, down_gx = over_y(gate_gy), over_x(down_gx)
-    weights_last, product_last, d_both_last = feed(normed_two, cot, gate_last, second_last, False)
-    fed.append((weights_last, product_last, d_both_last))
+    fed.append(feed(normed_two, cot, [whole_of(gate_last), third_of(second_last, 0), third_of(second_last, 1)]))
+    (gate_gl, up_gl, down_gl), normed_two, gate_gy, up_gy, down_gy = fence(fed[2][3], normed_two, gate_gy, up_gy, down_gy)
+    gate_gy, gate_gl = over_y(gate_gy), scatter(gate_gl)
+    fed.append(feed(normed_two, cot, apart(gate_x, up_x, down_x)))
     products, d_boths = [f[1] for f in fed], [f[2] for f in fed]
+    (gate_gx, up_gx, down_gx), d_boths, products, gate_gy, up_gy, gate_gl, up_gl, down_gl = fence(
+        fed[3][3], d_boths, products, gate_gy, up_gy, gate_gl, up_gl, down_gl
+    )
 
     back_rhs = [f[0][k] for f in fed for k in range(2)]
     downs = [f[0][2] for f in fed]
-    back_sent = partial_rows(d_boths, back_rhs, back_dot, "back_other")
-    back_sent, d_boths, products, gate_gy, up_gy, down_gx, gate_gx, up_gx = fence(
-        back_sent, d_boths, products, gate_gy, up_gy, down_gx, gate_gx, up_gx
-    )
-    received_two = over_core(back_sent)
-    up_gy, gate_gx = over_y(up_gy), over_x(gate_gx)
-    gate_gl, up_gl, down_gl = feed_grads(normed_two_t, cot, products[3], d_boths[3])
-    out_sent = partial_rows(products, downs, down_dot, "down_other")
-    received_two, out_sent, up_gy, gate_gx, gate_gl, up_gl, up_gx, down_gl = fence(
-        received_two, out_sent, up_gy, gate_gx, gate_gl, up_gl, up_gx, down_gl
+    up_gy, gate_gx, up_gl = over_y(up_gy), over_x(gate_gx), scatter(up_gl)
+
+    received_two = [over_core(a) for a in sent_parts(d_boths, back_rhs, back_dot, "back_other")]
+    out_sent = sent_parts(products, downs, down_dot, "down_other")
+    received_two, out_sent, up_gy, gate_gx, up_gl, up_gx, down_gx, down_gl = fence(
+        received_two, out_sent, up_gy, gate_gx, up_gl, up_gx, down_gx, down_gl
     )
 
     def back_body(left, right, others, outs):
-        received_ref, hidden_ref, cot_ref, gain_ref = others
-        grad_normed = kept(back_dot, left, right) + received_ref[...].astype(f32)
+        *received_refs, hidden_ref, cot_ref, gain_ref = others
+        grad_normed = kept(back_dot, left, right) + joined(received_refs)
         values_ = hidden_ref[...]
         scale_rows = rms_scale(values_)
         grad_hidden = cot_ref[...].astype(f32) + norm_back(grad_normed, values_, scale_rows, gain_ref[...])
@@ -1009,28 +1036,27 @@
 
         outs[2][...] += column_sums(grad_normed * values_ * scale_rows)
 
-    up_gx, gate_gl = over_x(up_gx), scatter(gate_gl)
-    received_out = over_core(out_sent)
+    up_gx, down_gl = over_x(up_gx), over_y(down_gl)
+    received_out = [over_core(a) for a in out_sent]
     grad_hidden, grad_attended_own, gain_two_sums = sum_rows_call(
         back_body,
         mine * tiles_half,
         d_boths,
         back_rhs,
-        [(received_two, "plain"), (hidden, "plain"), (cot, "shifted"), (gain_two, "whole")],
+        [*[(r, "plain") for r in received_two], (hidden, "plain"), (cot, "shifted"), (gain_two, "whole")],
         [((half_rows, width), f32), ((half_rows, width), bf16), ((8, width), f32)],
         row_tile,
         "back_own",
     )
-    grad_attended_own, received_out, up_gx, gate_gl, up_gl, gate_gx = fence(grad_attended_own, received_out, up_gx, gate_gl, up_gl, gate_gx)
+    gate_sum = scatter(add(own_grads[0], gate_gy, gate_gx))
     grad_attended_far = over_core(grad_attended_own)
-    up_gl = scatter(up_gl)
-    gate_sum = add(own_grads[0], gate_gy, gate_gx)
 
     def down_body(left, right, others, outs):
-        hidden_ref, received_ref = others
+        hidden_ref, *received_refs = others
 
         def store(at, total):
-            outs[0][:, at] = (hidden_ref[:, at] + total + received_ref[:, at].astype(f32)).astype(bf16)
+            received_rows = received_refs[at.start // units][...].astype(f32)
+            outs[0][:, at] = (hidden_ref[:, at] + total + received_rows).astype(bf16)
 
         down_dot(left, right, store)
 
@@ -1039,13 +1065,14 @@
         mine * tiles_half,
         products,
         downs,
-        [(hidden, "plain"), (received_out, "plain")],
+        [(hidden, "plain"), *[(r, "plain") for r in received_out]],
         [((half_rows, width), bf16)],
         row_tile,
         "down_own",
     )
-    grad_attended_own, grad_attended_far, layer_rows, down_gl, gate_sum = fence(
-        grad_attended_own, grad_attended_far, layer_rows, down_gl, gate_sum
+    down_gx = add(down_gx, down_gl)
+    grad_attended_own, grad_attended_far, layer_rows, up_gx, down_gx, gate_sum, gate_gl, up_gl = fence(
+        grad_attended_own, grad_attended_far, layer_rows, up_gx, down_gx, gate_sum, gate_gl, up_gl
     )
 
     pair_order = order.reshape(n_ctx, spans_dev // 2, 2)
@@ -1069,73 +1096,68 @@
         near, far = near.reshape(local_len, width), far.reshape(local_len, width)
         return jnp.where(seq == 0, jnp.stack([near, far]), jnp.stack([far, near]))
 
-    def sides(piece):
-        return [piece, over_y(piece), over_x(piece), over_diagonal(piece)]
-
     def both_cores(side):
         return side + [over_core(a) for a in side]
 
-    gate_sum = scatter(gate_sum)
-    down_gl = over_diagonal(down_gl)
+    up_sum = scatter(add(own_grads[1], up_gy, up_gx))
+    down_gx = over_x(down_gx)
+    both_gl = over_diagonal(jnp.concatenate([gate_gl, up_gl], axis=0))
     grad_attended, grad_mixed = mixed_back(mine, grad_attended_own, grad_attended_far, w_out_rows)
     out_grads = [b.reshape(-1, width) for b in out_grad_blocks(place_at, mixed, grad_attended)]
     layer_parts = arrange(layer_rows)
-    up_sum = add(own_grads[1], up_gy, up_gx)
-    grad_mixed, out_grads, down_gl, layer_parts, up_sum, gate_gl, up_gl = fence(
-        grad_mixed, out_grads, down_gl, layer_parts, up_sum, gate_gl, up_gl
-    )
+    grad_mixed, out_grads, down_gx, layer_parts, up_sum, both_gl = fence(grad_mixed, out_grads, down_gx, layer_parts, up_sum, both_gl)
 
     def back_of(group, q_aug):
         return attend_back(group, 1, q_aug, keys, values, grad_mixed, mixed, cosine, sine)
 
-    up_sum = scatter(up_sum)
+    down_sum = scatter(add(own_grads[2], down_gy, down_gx))
     layer_parts = to_slots(layer_parts)
-    both_gl = over_diagonal(jnp.concatenate([gate_gl, up_gl], axis=0))
+    out_y, out_last = over_y(out_grads[1]), over_y(out_grads[3])
     back_last = back_of(3, q_aug)
-    down_sum = add(own_grads[2], down_gy, down_gx, down_gl)
-    back_last, q_aug, layer_parts, gate_sum, both_gl, down_sum, out_grads = fence(
-        back_last, q_aug, layer_parts, gate_sum, both_gl, down_sum, out_grads
-    )
+    both_sum = add(jnp.concatenate([gate_sum, up_sum], axis=0), both_gl)
+    back_last, q_aug, layer_parts, both_sum, out_y, out_last = fence(back_last, q_aug, layer_parts, both_sum, out_y, out_last)
     qkv_last = qkv_grad(normed_t, *back_last)
-    qkv_last, q_aug, down_sum = fence(qkv_last, q_aug, down_sum)
-
-    qkv_last = over_diagonal(qkv_last)
-    down_sum = scatter(down_sum)
-    out_grads = [out_grads[0], over_y(out_grads[1]), over_x(out_grads[2]), over_diagonal(out_grads[3])]
+    out_x = add(out_grads[2], out_last)
+    qkv_last, q_aug, out_x = fence(qkv_last, q_aug, out_x)
+
+    qkv_last, out_x, both_x, both_y = over_y(qkv_last), over_x(out_x), over_x(both_sum), over_y(both_sum)
     back_x = back_of(2, q_aug)
-    back_x, q_aug, qkv_last, out_grads, up_sum = fence(back_x, q_aug, qkv_last, out_grads, up_sum)
-    qkv_x = qkv_grad(normed_t, *back_x)
-    out_sum = add(*out_grads)
-    both_sum = add(jnp.concatenate([gate_sum, up_sum], axis=0), both_gl)
-    qkv_x, out_sum, both_sum, q_aug = fence(qkv_x, out_sum, both_sum, q_aug)
-
-    qkv_x = over_x(qkv_x)
+    back_x, q_aug, qkv_last, out_x, both_x, both_y, down_sum = fence(back_x, q_aug, qkv_last, out_x, both_x, both_y, down_sum)
+    qkv_x = add(qkv_grad(normed_t, *back_x), qkv_last)
+    out_sum = add(out_grads[0], out_y, out_x)
+    qkv_x, out_sum, q_aug = fence(qkv_x, out_sum, q_aug)
+
     out_sum = scatter(out_sum)
-    both_sides = sides(both_sum)
+    qkv_x, both_last = over_x(qkv_x), over_y(both_x)
+    both_far = [over_core(a) for a in (both_sum, both_y, both_x)]
     back_y = back_of(1, q_aug)
-    back_y, q_aug, qkv_x, both_sides, down_sum = fence(back_y, q_aug, qkv_x, both_sides, down_sum)
+    back_y, q_aug, qkv_x, both_last, both_far, out_sum = fence(back_y, q_aug, qkv_x, both_last, both_far, out_sum)
     qkv_y = qkv_grad(normed_t, *back_y)
-    qkv_y, q_aug = fence(qkv_y, q_aug)
-
-    qkv_y = over_y(qkv_y)
-    both_pieces = both_cores(both_sides)
+    row_sum = jnp.concatenate([down_sum, out_sum], axis=0)
+    qkv_y, q_aug, row_sum = fence(qkv_y, q_aug, row_sum)
+
+    qkv_y, row_x, row_y = over_y(qkv_y), over_x(row_sum), over_y(row_sum)
+    both_far.append(over_core(both_last))
     back_own = back_of(0, q_aug)
-    back_own, qkv_y, both_pieces, out_sum = fence(back_own, qkv_y, both_pieces, out_sum)
-
-    in_lhs = [*back_own, *back_y, *back_x, *back_last]
+    back_own, qkv_y, row_x, row_y, both_far = fence(back_own, qkv_y, row_x, row_y, both_far)
+
     depth = w_qkv.shape[0]
     q_width, k_width = queries.shape[1], keys.shape[1]
     in_rhs = [(w_qkv, (depth, q_width), (0, 0))]
     in_rhs += [(w_qkv, (depth, k_width), (0, q_width // k_width + which)) for which in range(2)]
-    received_in = over_core(partial_rows(in_lhs, in_rhs, in_dot, "in_other"))
-    row_sides = sides(jnp.concatenate([down_sum, out_sum], axis=0))
-    qkv_sum = add(qkv_grad(normed_t, *back_own), qkv_y, qkv_x, qkv_last)
-    qkv_sum, received_in, row_sides = fence(qkv_sum, received_in, row_sides)
+    qkv_sum = add(qkv_grad(normed_t, *back_own), qkv_y, qkv_x)
+    qkv_sum, back_own = fence(qkv_sum, back_own)
+    in_lhs = [*back_own, *back_y, *back_x, *back_last]
     qkv_sum = scatter(qkv_sum)
+    row_last = over_y(row_x)
+    row_far = [over_core(row_sum)]
+    received_in = [over_core(a) for a in sent_parts(in_lhs, in_rhs, in_dot, "in_other")]
+    received_in, row_last, row_far = fence(received_in, row_last, row_far)
+    row_far += [over_core(a) for a in (row_y, row_x, row_last)]
 
     def in_body(left, right, others, outs):
-        received_ref, x_ref, grad_ref, gain_ref = others
-        grad_normed = kept(in_dot, left, right) + received_ref[...].astype(f32)
+        *received_refs, x_ref, grad_ref, gain_ref = others
+        grad_normed = kept(in_dot, left, right) + joined(received_refs)
         values_ = x_ref[...].astype(f32)
         scale_rows = rms_scale(values_)
         outs[0][...] = (grad_ref[...] + norm_back(grad_normed, values_, scale_rows, gain_ref[...])).astype(bf16)
@@ -1151,27 +1173,37 @@
         mine * tiles_half,
         in_lhs,
         in_rhs,
-        [(received_in, "plain"), (x, "shifted"), (grad_hidden, "plain"), (gain_one, "whole")],
+        [*[(r, "plain") for r in received_in], (x, "shifted"), (grad_hidden, "plain"), (gain_one, "whole")],
         [((half_rows, width), bf16), ((8, width), f32)],
         row_tile,
         "in_own",
     )
     sums = jnp.stack([gain_one_sums.sum(0), gain_two_sums.sum(0)])
-    token_parts, sums, qkv_sum, row_sides = fence(arrange(grad_rows), sums, qkv_sum, row_sides)
-    for step in (over_core, over_x, over_y):
+    sums = sums + over_x(sums)
+    token_parts, sums, qkv_sum, row_far = fence(arrange(grad_rows), sums, qkv_sum, row_far)
+
+    qkv_x, qkv_y = over_x(qkv_sum), over_y(qkv_sum)
+    layer_out = from_slots(layer_parts)
+    token_parts, sums, qkv_x, qkv_y, layer_out = fence(token_parts, sums, qkv_x, qkv_y, layer_out)
+
+    token_parts = to_slots(token_parts)
+    qkv_last = over_y(qkv_x)
+    where = jnp.stack([place, core]).astype(jnp.int32)
+    both_pieces = [both_sum, both_y, both_x, both_last] + both_far
+    grad_w_gate = unit_columns(where, both_pieces, n_shard, 0)
+    grad_w_up = unit_columns(where, both_pieces, n_shard, 1)
+    grad_w_down, grad_w_out = unit_rows(where, [row_sum, row_y, row_x, row_last] + row_far, unit_cols)
+    for step in (over_core, over_y):
         sums = sums + step(sums)
+    token_parts, grad_w_gate, grad_w_up, grad_w_down, grad_w_out, qkv_last, sums = fence(
+        token_parts, grad_w_gate, grad_w_up, grad_w_down, grad_w_out, qkv_last, sums
+    )
+
     total = lax.dynamic_slice_in_dim(sums, shard * gain_width, gain_width, 1)
     for step in range(1, n_shard):
         to = lax.dynamic_slice_in_dim(sums, (shard + step) % n_shard * gain_width, gain_width, 1)
         total = total + lax.ppermute(to, "shard", [(z, (z + step) % n_shard) for z in range(n_shard)])
-    token_parts = to_slots(token_parts)
-    where = jnp.stack([place, core]).astype(jnp.int32)
-    qkv_pieces = both_cores(sides(qkv_sum))
-    grad_w_gate = unit_columns(where, both_pieces, n_shard, 0)
-    grad_w_up = unit_columns(where, both_pieces, n_shard, 1)
-    grad_w_down, grad_w_out = unit_rows(where, both_cores(row_sides), unit_cols)
-    layer_out = from_slots(layer_parts)
-    grad_w_query, grad_w_key, grad_w_value = head_columns(where, qkv_pieces)
+    grad_w_query, grad_w_key, grad_w_value = head_columns(where, both_cores([qkv_sum, qkv_y, qkv_x, qkv_last]))
     grad_tokens = from_slots(token_parts)
 
     return (

time: 972 us -> 884 us (0.909)
  waiting for transfers between devices: 288 us -> 170 us
  blocking collectives: 0 us -> 24.6 us
  other arithmetic: 40.2 us -> 53.4 us
    ppermute x19 -> x20, waiting for transfers between devices: 114 us -> 58.7 us  [chip_layer(): over_x = lambda a: lax.ppermute(a, 'ctx', perm_x)]
    ppermute x8 -> x2, waiting for transfers between devices: 55.8 us -> 13.6 us  [chip_layer(): over_diagonal = lambda a: lax.ppermute(a, ('ctx', 'batch'), perm_diagonal)]
    all_gather x0 -> x1, blocking collectives: none -> 24.6 us  [over_z(): gathered = lax.all_gather(piece, 'shard', axis=0, tiled=True)]
    ppermute x15 -> x22, waiting for transfers between devices: 84.2 us -> 62.6 us  [chip_layer(): over_y = lambda a: lax.ppermute(a, 'batch', [(0, 1), (1, 0)])]
    ppermute x3, waiting for transfers between devices: 10.7 us -> 0.01 us  [chip_layer(): lax.ppermute(to, 'shard', [(z, (z + step) % n_shard) for z in range(n_sha...]
    convert_element_type x6 -> x9, other arithmetic: 18.6 us -> 26.9 us  [add(): functools.reduce(lambda a, b: a + b, [t.astype(f32) for t in terms])]
    ppermute x15 -> x22, starting transfers between devices: 17.1 us -> 24 us  [chip_layer(): over_y = lambda a: lax.ppermute(a, 'batch', [(0, 1), (1, 0)])]
    ppermute x19 -> x20, starting transfers between devices: 20.5 us -> 23.3 us  [chip_layer(): over_x = lambda a: lax.ppermute(a, 'ctx', perm_x)]
  transfers between devices with their start and end apart: 82 -> 94, of which waited for: 34 -> 31; matrix products, arithmetic and copies ran while one was open for 6% -> 7% of each run, Pallas kernels for 47% -> 53%
where the time goes in v2:
time: 884 us; the launch traced here: 876 us
  Pallas kernels  511 us (58%)
  waiting for transfers between devices  170 us (19%)
  starting transfers between devices  61.1 us (7%)
  other arithmetic  53.4 us (6%)
  local copies, waits for them, and re-layouts  40.2 us (5%)
  blocking collectives  24.6 us (3%)
  between operations  15.3 us (2%)
    pallas_call x37, Pallas kernels, call(): pl.pallas_call(kernel, grid_spec=pltpu.PrefetchScalarGridSpec(num_scalar_...  511 us
    ppermute x22, waiting for transfers between devices, chip_layer(): over_y = lambda a: lax.ppermute(a, 'batch', [(0, 1), (1, 0)])  62.6 us
    ppermute x20, waiting for transfers between devices, chip_layer(): over_x = lambda a: lax.ppermute(a, 'ctx', perm_x)  58.7 us
    convert_element_type x9, other arithmetic, add(): functools.reduce(lambda a, b: a + b, [t.astype(f32) for t in terms])  26.9 us
    all_gather x1, blocking collectives, over_z(): gathered = lax.all_gather(piece, 'shard', axis=0, tiled=True)  24.6 us
    ppermute x22, starting transfers between devices, chip_layer(): over_y = lambda a: lax.ppermute(a, 'batch', [(0, 1), (1, 0)])  24 us
    ppermute x20, starting transfers between devices, chip_layer(): over_x = lambda a: lax.ppermute(a, 'ctx', perm_x)  23.3 us
  transfers between devices with their start and end apart: 94, of which 31 were waited for; matrix products, arithmetic and copies ran while one was open for 7% of the time, Pallas kernels for 53%

profile of v2, /device:TPU:0, one launch (start us, length us, event | category | flops | bytes accessed | tf_op | source)
XLA Modules:
  0.0 875.6 jit_solution(17755684244281839248)
XLA Ops:
  24.6 27.0 %collective-permute-done.1 = s32[512]{0:T(512)S(1)} collective-permute-done((s32[512]{0:T(512)S(1)}, s32[512]{0:T(512)S(1)}, u32[]{:S(2)}, u32[]{:S(2)}) %collective-permute-start.1) | collective-permute-done | bytes 2080 | tf_op jit(solution)/shard_map/ppermute | solution.py:799
  61.3 24.6 %all_gather.17 = bf16[768,384]{1,0:T(8,128)(2,1)} all-gather(bf16[192,384]{1,0:T(8,128)(2,1)S(1)} %pad_maximum_fusion.12), channel_id=1, replica_groups=mesh['shard'=4,'ctx'=4,'batch'=2] {'shard'}, dimensions={0}, use_global_device_ids=true | all-gather | bytes 737280 | tf_op jit(solution)/shard_map/all_gather | solution.py:806
  111.8 28.3 %front.1 = (bf16[2048,1536]{1,0:T(8,128)(2,1)}, bf16[2048,1536]{1,0:T(8,128)(2,1)}, bf16[1536,2048]{1,0:T(8,128)(2,1)}, bf16[2048,1024]{1,0:T(8,128)(2,1)}, bf16...) custom-call(s32[16]{0:T(128)} %get-tuple-element.657.near_ref, ...), custom_call_target="tpu_custom_call" | custom-call | flops 1000 | bytes 1000 | tf_op jit(solution)/shard_map/front/pallas_call | solution.py:74
  140.1 33.0 %attend.1 = (bf16[2048,1024]{1,0:T(8,128)(2,1)}, bf16[2048,1024]{1,0:T(8,128)(2,1)}) custom-call(bf16[2048,1024]{1,0:T(8,128)(2,1)} %get-tuple-element.337.q_ref, bf16[2048,512]{1,0:T(8,128)(2,1)} %get-tuple-element.338.k_ref, bf16[2048,512]{1,0:T(8,128)(2,1)} %get-tuple-element.339.v_ref), custom_call_target="tpu_custom_call" | custom-call | flops 1000 | bytes 1000 | tf_op jit(solution)/shard_map/attend/pallas_call | solution.py:74
  197.4 11.0 %out_own.1 = (f32[1024,1536]{1,0:T(8,128)}, bf16[1024,512]{1,0:T(8,128)(2,1)}, bf16[1024,512]{1,0:T(8,128)(2,1)}, bf16[1024,512]{1,0:T(8,128)(2,1)}) custom-call(s32[1]{0:T(128)S(6)} %mul.113.base_ref, bf16[2048,1024]{1,0:T(8,128)(2,1)} %get-tuple-element.349.refs_0_.mixed_ref.o_ref, bf16[1024,1536]{1,0:T(8,128)(2,1)} %out_rows.1.refs_1_.w_ref, ...), custom_call_target="tpu_custom_call" | custom-call | flops 1000 | bytes 1000 | tf_op jit(solution)/shard_map/out_own/pallas_call | solution.py:74
  209.0 12.4 %span_join.1 = bf16[16,128,1536]{2,1,0:T(8,128)(2,1)} custom-call(s32[16]{0:T(128)} %get-tuple-element.657.near_ref, s32[16]{0:T(128)} %get-tuple-element.656.far_ref, s32[16]{0:T(128)} %copy-done.44, bf16[8,128,1536]{2,1,0:T(8,128)(2,1)} %bitcast.23.a_ref, bf16[8,128,1536]{2,1,0:T(8,128)(2,1)} %bitcast.24.b_ref), custom_call_target="tpu_custom_call" | custom-call | flops 1000 | bytes 1000 | tf_op jit(solution)/shard_map/span_join/pallas_call | solution.py:74
  242.8 15.2 %hidden_units.4 = (bf16[2048,512]{1,0:T(8,128)(2,1)}, bf16[2048,1024]{1,0:T(8,128)(2,1)}) custom-call(bf16[2048,1536]{1,0:T(8,128)(2,1)} %get-tuple-element.409.n_ref, bf16[2048,1536]{1,0:T(8,128)(2,1)} %bitcast.70, bf16[4,384,512]{2,1,0:T(8,128)(2,1)} %bitcast.90, bf16[4,384,512]{2,1,0:T(8,128)(2,1)} %copy-done.3, ...), custom_call_target="tpu_custom_call" | custom-call | flops 1000 | bytes 1000 | tf_op jit(solution)/shard_map/hidden_units/pallas_call | solution.py:74
  258.0 17.4 %feed_grads.4 = (bf16[1536,512]{1,0:T(8,128)(2,1)}, bf16[1536,512]{1,0:T(8,128)(2,1)}, bf16[512,1536]{1,0:T(8,128)(2,1)}) custom-call(bf16[1536,2048]{1,0:T(8,128)(2,1)} %get-tuple-element.375.n_ref, bf16[2048,1536]{1,0:T(8,128)(2,1)} %bitcast.71, bf16[2048,512]{1,0:T(8,128)(2,1)} %get-tuple-element.429.product_ref.refs_0_, ...), custom_call_target="tpu_custom_call" | custom-call | flops 1000 | bytes 1000 | tf_op jit(solution)/shard_map/feed_grads/pallas_call | solution.py:74
  277.3 15.1 %hidden_units.5 = (bf16[2048,512]{1,0:T(8,128)(2,1)}, bf16[2048,1024]{1,0:T(8,128)(2,1)}) custom-call(bf16[2048,1536]{1,0:T(8,128)(2,1)} %get-tuple-element.409.n_ref, bf16[2048,1536]{1,0:T(8,128)(2,1)} %bitcast.72, bf16[4,384,512]{2,1,0:T(8,128)(2,1)} %copy-done.5, bf16[4,384,512]{2,1,0:T(8,128)(2,1)} %collective-permute-done.21.up_ref.refs_7_, ...), custom_call_target="tpu_custom_call" | custom-call | flops 1000 | bytes 1000 | tf_op jit(solution)/shard_map/hidden_units/pallas_call | solution.py:74
  292.4 17.5 %feed_grads.5 = (bf16[1536,512]{1,0:T(8,128)(2,1)}, bf16[1536,512]{1,0:T(8,128)(2,1)}, bf16[512,1536]{1,0:T(8,128)(2,1)}) custom-call(bf16[1536,2048]{1,0:T(8,128)(2,1)} %get-tuple-element.375.n_ref, bf16[2048,1536]{1,0:T(8,128)(2,1)} %bitcast.73, bf16[2048,512]{1,0:T(8,128)(2,1)} %get-tuple-element.430.product_ref.refs_1_, ...), custom_call_target="tpu_custom_call" | custom-call | flops 1000 | bytes 1000 | tf_op jit(solution)/shard_map/feed_grads/pallas_call | solution.py:74
  312.6 15.4 %hidden_units.6 = (bf16[2048,512]{1,0:T(8,128)(2,1)}, bf16[2048,1024]{1,0:T(8,128)(2,1)}) custom-call(bf16[2048,1536]{1,0:T(8,128)(2,1)} %get-tuple-element.409.n_ref, bf16[2048,1536]{1,0:T(8,128)(2,1)} %bitcast.74, bf16[4,384,512]{2,1,0:T(8,128)(2,1)} %copy-done.7, bf16[4,768,512]{2,1,0:T(8,128)(2,1)} %bitcast.79, bf16[4,768,512]{2,1,0:T(8,128)(2,1)} %bitcast.80), custom_call_target="tpu_custom_call" | custom-call | flops 1000 | bytes 1000 | tf_op jit(solution)/shard_map/hidden_units/pallas_call | solution.py:74
  328.0 17.5 %feed_grads.6 = (bf16[1536,512]{1,0:T(8,128)(2,1)}, bf16[1536,512]{1,0:T(8,128)(2,1)}, bf16[512,1536]{1,0:T(8,128)(2,1)}) custom-call(bf16[1536,2048]{1,0:T(8,128)(2,1)} %get-tuple-element.375.n_ref, bf16[2048,1536]{1,0:T(8,128)(2,1)} %bitcast.75, bf16[2048,512]{1,0:T(8,128)(2,1)} %get-tuple-element.431.product_ref.refs_2_, ...), custom_call_target="tpu_custom_call" | custom-call | flops 1000 | bytes 1000 | tf_op jit(solution)/shard_map/feed_grads/pallas_call | solution.py:74
  347.6 15.1 %hidden_units.7 = (bf16[2048,512]{1,0:T(8,128)(2,1)}, bf16[2048,1024]{1,0:T(8,128)(2,1)}) custom-call(bf16[2048,1536]{1,0:T(8,128)(2,1)} %get-tuple-element.409.n_ref, bf16[2048,1536]{1,0:T(8,128)(2,1)} %bitcast.76, bf16[4,384,512]{2,1,0:T(8,128)(2,1)} %collective-permute-done.20.gate_ref.refs_10_, bf16[4,384,512]{2,1,0:T(8,128)(2,1)} %copy-done.6, ...), custom_call_target="tpu_custom_call" | custom-call | flops 1000 | bytes 1000 | tf_op jit(solution)/shard_map/hidden_units/pallas_call | solution.py:74
  362.7 17.5 %feed_grads.7 = (bf16[1536,512]{1,0:T(8,128)(2,1)}, bf16[1536,512]{1,0:T(8,128)(2,1)}, bf16[512,1536]{1,0:T(8,128)(2,1)}) custom-call(bf16[1536,2048]{1,0:T(8,128)(2,1)} %get-tuple-element.375.n_ref, bf16[2048,1536]{1,0:T(8,128)(2,1)} %bitcast.77, bf16[2048,512]{1,0:T(8,128)(2,1)} %get-tuple-element.432.product_ref.refs_3_, ...), custom_call_target="tpu_custom_call" | custom-call | flops 1000 | bytes 1000 | tf_op jit(solution)/shard_map/feed_grads/pallas_call | solution.py:74
  384.9 20.9 %back_other.1 = (bf16[1024,512]{1,0:T(8,128)(2,1)}, bf16[1024,512]{1,0:T(8,128)(2,1)}, bf16[1024,512]{1,0:T(8,128)(2,1)}) custom-call(s32[1]{0:T(128)S(6)} %mul.134.base_ref, bf16[2048,1024]{1,0:T(8,128)(2,1)} %get-tuple-element.422.both_ref.refs_0_, bf16[2048,1024]{1,0:T(8,128)(2,1)} %get-tuple-element.423.both_ref.refs_1_, ...), custom_call_target="tpu_custom_call" | custom-call | flops 1000 | bytes 1000 | tf_op jit(solution)/shard_map/back_other/pallas_call | solution.py:74
  406.5 11.3 %down_other.1 = (bf16[1024,512]{1,0:T(8,128)(2,1)}, bf16[1024,512]{1,0:T(8,128)(2,1)}, bf16[1024,512]{1,0:T(8,128)(2,1)}) custom-call(s32[1]{0:T(128)S(6)} %mul.134.base_ref, bf16[2048,512]{1,0:T(8,128)(2,1)} %get-tuple-element.429.product_ref.refs_0_, bf16[2048,512]{1,0:T(8,128)(2,1)} %get-tuple-element.430.product_ref.refs_1_, ...), custom_call_target="tpu_custom_call" | custom-call | flops 1000 | bytes 1000 | tf_op jit(solution)/shard_map/down_other/pallas_call | solution.py:74
  422.7 24.5 %back_own.1 = (f32[1024,1536]{1,0:T(8,128)}, bf16[1024,1536]{1,0:T(8,128)(2,1)}, f32[8,1536]{1,0:T(8,128)}) custom-call(s32[1]{0:T(128)S(6)} %mul.113.base_ref, bf16[2048,1024]{1,0:T(8,128)(2,1)} %get-tuple-element.422.both_ref.refs_0_, bf16[2048,1024]{1,0:T(8,128)(2,1)} %get-tuple-element.423.both_ref.refs_1_, ...), custom_call_target="tpu_custom_call" | custom-call | flops 1000 | bytes 1000 | tf_op jit(solution)/shard_map/back_own/pallas_call | solution.py:74
  457.8 12.5 %down_own.1 = bf16[1024,1536]{1,0:T(8,128)(2,1)} custom-call(s32[1]{0:T(128)S(6)} %mul.113.base_ref, bf16[2048,512]{1,0:T(8,128)(2,1)} %get-tuple-element.429.product_ref.refs_0_, bf16[2048,512]{1,0:T(8,128)(2,1)} %get-tuple-element.430.product_ref.refs_1_, bf16[2048,512]{1,0:T(8,128)(2,1)} %get-tuple-element.431.product_ref.refs_2_, ...), custom_call_target="tpu_custom_call" | custom-call | flops 1000 | bytes 1000 | tf_op jit(solution)/shard_map/down_own/pallas_call | solution.py:74
  470.3 14.2 %collective-permute-done.38 = bf16[512,1536]{1,0:T(8,128)(2,1)} collective-permute-done((bf16[512,1536]{1,0:T(8,128)(2,1)}, bf16[512,1536]{1,0:T(8,128)(2,1)}, u32[]{:S(2)}, u32[]{:S(2)}) %collective-permute-start.38) | collective-permute-done | bytes 1572896 | tf_op jit(solution)/shard_map/ppermute | solution.py:802
  501.6 12.0 %mixed_back.1 = (bf16[2048,1536]{1,0:T(8,128)(2,1)}, bf16[2048,1024]{1,0:T(8,128)(2,1)}) custom-call(s32[1]{0:T(128)} %bitcast.3.core_ref, bf16[1024,1536]{1,0:T(8,128)(2,1)} %get-tuple-element.458.own_ref, bf16[1024,1536]{1,0:T(8,128)(2,1)} %copy-done.16, bf16[1024,1536]{1,0:T(8,128)(2,1)} %out_rows.1.refs_1_.w_ref), custom_call_target="tpu_custom_call" | custom-call | flops 1000 | bytes 1000 | tf_op jit(solution)/shard_map/mixed_back/pallas_call | solution.py:74
  513.7 12.0 %out_grads.1 = (bf16[4,48,1536]{2,1,0:T(8,128)(2,1)}, bf16[4,48,1536]{2,1,0:T(8,128)(2,1)}, bf16[4,48,1536]{2,1,0:T(8,128)(2,1)}, bf16[4,48,1536]{2,1,0:T(8,128)(2,1)}) custom-call(s32[1]{0:T(128)} %bitcast.21.place_ref, bf16[2048,1024]{1,0:T(8,128)(2,1)} %get-tuple-element.349.refs_0_.mixed_ref.o_ref, bf16[2048,1536]{1,0:T(8,128)(2,1)} %get-tuple-element.461.grad_ref), custom_call_target="tpu_custom_call" | custom-call | flops 1000 | bytes 1000 | tf_op jit(solution)/shard_map/out_grads/pallas_call | solution.py:74
  536.2 13.6 %collective-permute-done.40 = bf16[768,512]{1,0:T(8,128)(2,1)} collective-permute-done((bf16[768,512]{1,0:T(8,128)(2,1)}, bf16[768,512]{1,0:T(8,128)(2,1)}, u32[]{:S(2)}, u32[]{:S(2)}) %collective-permute-start.40) | collective-permute-done | bytes 786464 | tf_op jit(solution)/shard_map/ppermute | solution.py:803
  557.7 20.8 %attend_back.4 = (bf16[2048,256]{1,0:T(8,128)(2,1)}, bf16[2048,128]{1,0:T(8,128)(2,1)}, bf16[2048,128]{1,0:T(8,128)(2,1)}) custom-call(bf16[2048,1024]{1,0:T(8,128)(2,1)} %get-tuple-element.524.q_ref, bf16[2048,512]{1,0:T(8,128)(2,1)} %get-tuple-element.338.k_ref, bf16[2048,512]{1,0:T(8,128)(2,1)} %get-tuple-element.339.v_ref, ...), custom_call_target="tpu_custom_call" | custom-call | flops 1000 | bytes 1000 | tf_op jit(solution)/shard_map/attend_back/pallas_call | solution.py:74
  603.0 20.7 %attend_back.5 = (bf16[2048,256]{1,0:T(8,128)(2,1)}, bf16[2048,128]{1,0:T(8,128)(2,1)}, bf16[2048,128]{1,0:T(8,128)(2,1)}) custom-call(bf16[2048,1024]{1,0:T(8,128)(2,1)} %get-tuple-element.524.q_ref, bf16[2048,512]{1,0:T(8,128)(2,1)} %get-tuple-element.338.k_ref, bf16[2048,512]{1,0:T(8,128)(2,1)} %get-tuple-element.339.v_ref, ...), custom_call_target="tpu_custom_call" | custom-call | flops 1000 | bytes 1000 | tf_op jit(solution)/shard_map/attend_back/pallas_call | solution.py:74
  633.3 11.3 %collective-permute-done.49.refs_1_ = bf16[768,512]{1,0:T(8,128)(2,1)S(1)} collective-permute-done((bf16[768,512]{1,0:T(8,128)(2,1)S(1)}, bf16[768,512]{1,0:T(8,128)(2,1)S(1)}, u32[]{:S(2)}, u32[]{:S(2)}) %collective-permute-start.49) | collective-permute-done | bytes 786464 | tf_op jit(solution)/shard_map/ppermute | solution.py:802
  661.1 20.5 %attend_back.6 = (bf16[2048,256]{1,0:T(8,128)(2,1)}, bf16[2048,128]{1,0:T(8,128)(2,1)}, bf16[2048,128]{1,0:T(8,128)(2,1)}) custom-call(bf16[2048,1024]{1,0:T(8,128)(2,1)} %get-tuple-element.524.q_ref, bf16[2048,512]{1,0:T(8,128)(2,1)} %get-tuple-element.338.k_ref, bf16[2048,512]{1,0:T(8,128)(2,1)} %get-tuple-element.339.v_ref, ...), custom_call_target="tpu_custom_call" | custom-call | flops 1000 | bytes 1000 | tf_op jit(solution)/shard_map/attend_back/pallas_call | solution.py:74
  699.2 20.5 %attend_back.7 = (bf16[2048,256]{1,0:T(8,128)(2,1)}, bf16[2048,128]{1,0:T(8,128)(2,1)}, bf16[2048,128]{1,0:T(8,128)(2,1)}) custom-call(bf16[2048,1024]{1,0:T(8,128)(2,1)} %get-tuple-element.524.q_ref, bf16[2048,512]{1,0:T(8,128)(2,1)} %get-tuple-element.338.k_ref, bf16[2048,512]{1,0:T(8,128)(2,1)} %get-tuple-element.339.v_ref, ...), custom_call_target="tpu_custom_call" | custom-call | flops 1000 | bytes 1000 | tf_op jit(solution)/shard_map/attend_back/pallas_call | solution.py:74
  719.8 15.1 %collective-permute-done.57.refs_1_ = bf16[176,1536]{1,0:T(8,128)(2,1)} collective-permute-done((bf16[176,1536]{1,0:T(8,128)(2,1)}, bf16[176,1536]{1,0:T(8,128)(2,1)}, u32[]{:S(2)}, u32[]{:S(2)}) %collective-permute-start.57) | collective-permute-done | bytes 540704 | tf_op jit(solution)/shard_map/ppermute | solution.py:802
  746.1 11.6 %in_other.1 = (bf16[1024,512]{1,0:T(8,128)(2,1)}, bf16[1024,512]{1,0:T(8,128)(2,1)}, bf16[1024,512]{1,0:T(8,128)(2,1)}) custom-call(s32[1]{0:T(128)S(6)} %mul.134.base_ref, bf16[2048,256]{1,0:T(8,128)(2,1)} %get-tuple-element.539.q_ref.refs_0_, bf16[2048,128]{1,0:T(8,128)(2,1)} %get-tuple-element.540.k_ref.refs_1_, ...), custom_call_target="tpu_custom_call" | custom-call | flops 1000 | bytes 1000 | tf_op jit(solution)/shard_map/in_other/pallas_call | solution.py:74
  764.6 10.9 %collective-permute-done.62.refs_3_ = bf16[176,1536]{1,0:T(8,128)(2,1)} collective-permute-done((bf16[176,1536]{1,0:T(8,128)(2,1)}, bf16[176,1536]{1,0:T(8,128)(2,1)}, u32[]{:S(2)}, u32[]{:S(2)}) %collective-permute-start.62) | collective-permute-done | bytes 540704 | tf_op jit(solution)/shard_map/ppermute | solution.py:802
  775.5 15.4 %in_own.1 = (bf16[1024,1536]{1,0:T(8,128)(2,1)}, f32[8,1536]{1,0:T(8,128)}) custom-call(s32[1]{0:T(128)S(6)} %mul.113.base_ref, bf16[2048,256]{1,0:T(8,128)(2,1)} %get-tuple-element.539.q_ref.refs_0_, bf16[2048,128]{1,0:T(8,128)(2,1)} %get-tuple-element.540.k_ref.refs_1_, bf16[2048,128]{1,0:T(8,128)(2,1)} %get-tuple-element.541.v_ref.refs_2_, ...), custom_call_target="tpu_custom_call" | custom-call | flops 1000 | bytes 1000 | tf_op jit(solution)/shard_map/in_own/pallas_call | solution.py:74
  839.9 10.4 %collective-permute-done.72 = bf16[256,1536]{1,0:T(8,128)(2,1)S(1)} collective-permute-done((bf16[256,1536]{1,0:T(8,128)(2,1)}, bf16[256,1536]{1,0:T(8,128)(2,1)S(1)}, u32[]{:S(2)}, u32[]{:S(2)}) %collective-permute-start.72) | collective-permute-done | bytes 786464 | tf_op jit(solution)/shard_map/ppermute | solution.py:801
  (399 shorter events, 314.8 us)
Async XLA Ops:
  7.2 46.6 %all-gather.5.cloned.1.call-start = ((), (), s32[]{:S(2)}) async-start(), calls=%async_computation.7 | async-start | bytes 1536000 | tf_op jit(solution)/shard_map/all_gather | solution.py:806
  14.2 37.5 %collective-permute-start = (bf16[512,1536]{1,0:T(8,128)(2,1)S(1)}, bf16[512,1536]{1,0:T(8,128)(2,1)}, u32[]{:S(2)}, u32[]{:S(2)}) collective-permute-start(bf16[512,1536]{1,0:T(8,128)(2,1)S(1)} %get-tuple-element.308), channel_id=1, source_target_pairs={{0,4},{2,6},{4,0},{6,2},{1,5},{3,7},{5,1},{7,3},{8,12},{10,14},{12... | collective-permute-start | bytes 4718600 | tf_op jit(solution)/shard_map/ppermute | solution.py:799
  17.2 85.2 %all-gather.7.cloned.1.call-start = ((), (), s32[]{:S(2)}) async-start(), calls=%async_computation.8 | async-start | bytes 1966080 | tf_op jit(solution)/shard_map/all_gather | solution.py:806
  57.3 119.1 %all-gather.9.cloned.1.call-start = ((), (), s32[]{:S(2)}) async-start(), calls=%async_computation.9 | async-start | bytes 3932160 | tf_op jit(solution)/shard_map/all_gather | solution.py:806
  103.7 206.2 %all-gather.11.cloned.1.call-start = ((), (), s32[]{:S(2)}) async-start(), calls=%async_computation.10 | async-start | bytes 3932160 | tf_op jit(solution)/shard_map/all_gather | solution.py:806
  104.0 69.1 %collective-permute-start.8 = (bf16[512,1536]{1,0:T(8,128)(2,1)}, bf16[512,1536]{1,0:T(8,128)(2,1)}, u32[]{:S(2)}, u32[]{:S(2)}) collective-permute-start(bf16[512,1536]{1,0:T(8,128)(2,1)} %get-tuple-element.343), channel_id=1, source_target_pairs={{0,4},{2,6},{4,0},{6,2},{1,5},{3,7},{5,1},{7,3},{8,12},{10,14},{12... | collective-permute-start | bytes 4718600 | tf_op jit(solution)/shard_map/ppermute | solution.py:799
  105.1 74.7 %collective-permute-start.9 = (bf16[4,384,512]{2,1,0:T(8,128)(2,1)}, bf16[4,384,512]{2,1,0:T(8,128)(2,1)S(1)}, u32[]{:S(2)}, u32[]{:S(2)}) collective-permute-start(bf16[4,384,512]{2,1,0:T(8,128)(2,1)} %bitcast.89), channel_id=1, source_target_pairs={{0,1},{1,0},{2,3},{3,2},{4,5},{5,4},{6,7},{7,6},{8,9},{9,8},{10,11... | collective-permute-start | bytes 4718600 | tf_op jit(solution)/shard_map/ppermute | solution.py:802
  108.3 71.5 %collective-permute-start.10 = (bf16[4,192,384]{2,1,0:T(8,128)(2,1)}, bf16[4,192,384]{2,1,0:T(8,128)(2,1)}, u32[]{:S(2)}, u32[]{:S(2)}) collective-permute-start(bf16[4,192,384]{2,1,0:T(8,128)(2,1)} %bitcast.18.refs_0_), channel_id=1, source_target_pairs={{0,1},{1,0},{2,3},{3,2},{4,5},{5,4},{6,7},{7,6},{8,9},{9,8},{10,11... | collective-permute-start | bytes 1769480 | tf_op jit(solution)/shard_map/ppermute | solution.py:802
  109.1 70.6 %collective-permute-start.11 = (bf16[4,192,384]{2,1,0:T(8,128)(2,1)}, bf16[4,192,384]{2,1,0:T(8,128)(2,1)}, u32[]{:S(2)}, u32[]{:S(2)}) collective-permute-start(bf16[4,192,384]{2,1,0:T(8,128)(2,1)} %bitcast.18.refs_0_), channel_id=1, source_target_pairs={{0,4},{2,6},{4,0},{6,2},{1,5},{3,7},{5,1},{7,3},{8,12},{10,14},{12... | collective-permute-start | bytes 1769480 | tf_op jit(solution)/shard_map/ppermute | solution.py:799
  110.1 69.6 %collective-permute-start.12 = (bf16[4,192,384]{2,1,0:T(8,128)(2,1)}, bf16[4,192,384]{2,1,0:T(8,128)(2,1)}, u32[]{:S(2)}, u32[]{:S(2)}) collective-permute-start(bf16[4,192,384]{2,1,0:T(8,128)(2,1)} %bitcast.18.refs_0_), channel_id=1, source_target_pairs={{0,5},{1,4},{2,7},{3,6},{4,1},{5,0},{6,3},{7,2},{8,13},{9,12},{10,... | collective-permute-start | bytes 1769480 | tf_op jit(solution)/shard_map/ppermute | solution.py:803
  191.9 36.9 %collective-permute-start.20 = (bf16[4,384,512]{2,1,0:T(8,128)(2,1)S(1)}, bf16[4,384,512]{2,1,0:T(8,128)(2,1)}, u32[]{:S(2)}, u32[]{:S(2)}) collective-permute-start(bf16[4,384,512]{2,1,0:T(8,128)(2,1)S(1)} %bitcast.93), channel_id=1, source_target_pairs={{0,4},{2,6},{4,0},{6,2},{1,5},{3,7},{5,1},{7,3},{8,12},{10,14},{12... | collective-permute-start | bytes 4718600 | tf_op jit(solution)/shard_map/ppermute | solution.py:799
  194.4 36.5 %collective-permute-start.21 = (bf16[4,384,512]{2,1,0:T(8,128)(2,1)S(1)}, bf16[4,384,512]{2,1,0:T(8,128)(2,1)}, u32[]{:S(2)}, u32[]{:S(2)}) collective-permute-start(bf16[4,384,512]{2,1,0:T(8,128)(2,1)S(1)} %get-tuple-element.378.up_ref.refs_5_), channel_id=1, source_target_pairs={{0,1},{1,0},{2,3},{3,2},{4,5},{5,4},{6,7},{7,6},{8,9},{9,8},{10,11... | collective-permute-start | bytes 4718600 | tf_op jit(solution)/shard_map/ppermute | solution.py:802
  195.5 186.3 %reduce-scatter.8.cloned.1.call-start = ((), (), s32[]{:S(2)}) async-start(), calls=%async_computation.11 | async-start | bytes 1966080 | tf_op jit(solution)/shard_map/reduce_scatter | solution.py:813
  231.0 44.4 %collective-permute-start.22 = (bf16[4,384,512]{2,1,0:T(8,128)(2,1)S(1)}, bf16[4,384,512]{2,1,0:T(8,128)(2,1)S(1)}, u32[]{:S(2)}, u32[]{:S(2)}) collective-permute-start(bf16[4,384,512]{2,1,0:T(8,128)(2,1)S(1)} %get-tuple-element.378.up_ref.refs_5_), channel_id=1, source_target_pairs={{0,4},{2,6},{4,0},{6,2},{1,5},{3,7},{5,1},{7,3},{8,12},{10,14},{12... | collective-permute-start | bytes 4718600 | tf_op jit(solution)/shard_map/ppermute | solution.py:799
  231.9 43.5 %collective-permute-start.23 = (bf16[4,384,512]{2,1,0:T(8,128)(2,1)}, bf16[4,384,512]{2,1,0:T(8,128)(2,1)}, u32[]{:S(2)}, u32[]{:S(2)}) collective-permute-start(bf16[4,384,512]{2,1,0:T(8,128)(2,1)} %get-tuple-element.396.down_ref.refs_4_), channel_id=1, source_target_pairs={{0,1},{1,0},{2,3},{3,2},{4,5},{5,4},{6,7},{7,6},{8,9},{9,8},{10,11... | collective-permute-start | bytes 4718600 | tf_op jit(solution)/shard_map/ppermute | solution.py:802
  345.5 73.9 %reduce-scatter.10.cloned.1.call-start = ((), (), s32[]{:S(2)}) async-start(), calls=%async_computation.12 | async-start | bytes 1966080 | tf_op jit(solution)/shard_map/reduce_scatter | solution.py:813
  381.9 109.5 %reduce-scatter.12.cloned.1.call-start = ((), (), s32[]{:S(2)}) async-start(), calls=%async_computation.13 | async-start | bytes 1966080 | tf_op jit(solution)/shard_map/reduce_scatter | solution.py:813
  422.6 127.2 %reduce-scatter.14.cloned.1.call-start = ((), (), s32[]{:S(2)}) async-start(), calls=%async_computation.14 | async-start | bytes 1966080 | tf_op jit(solution)/shard_map/reduce_scatter | solution.py:813
  447.2 44.2 %collective-permute-start.33 = (bf16[1024,1536]{1,0:T(8,128)(2,1)}, bf16[1024,1536]{1,0:T(8,128)(2,1)S(1)}, u32[]{:S(2)}, u32[]{:S(2)}) collective-permute-start(bf16[1024,1536]{1,0:T(8,128)(2,1)} %get-tuple-element.458.own_ref), channel_id=1, source_target_pairs={{0,2},{2,0},{4,6},{6,4},{1,3},{3,1},{5,7},{7,5},{8,10},{10,8},{12,... | collective-permute-start | bytes 9437192 | tf_op jit(solution)/shard_map/ppermute | solution.py:800
  447.8 36.7 %collective-permute-start.38 = (bf16[512,1536]{1,0:T(8,128)(2,1)}, bf16[512,1536]{1,0:T(8,128)(2,1)}, u32[]{:S(2)}, u32[]{:S(2)}) collective-permute-start(bf16[512,1536]{1,0:T(8,128)(2,1)} %get-tuple-element.452), channel_id=1, source_target_pairs={{0,1},{1,0},{2,3},{3,2},{4,5},{5,4},{6,7},{7,6},{8,9},{9,8},{10,11... | collective-permute-start | bytes 4718600 | tf_op jit(solution)/shard_map/ppermute | solution.py:802
  454.4 37.0 %collective-permute-start.37 = (bf16[1536,512]{1,0:T(8,128)(2,1)}, bf16[1536,512]{1,0:T(8,128)(2,1)}, u32[]{:S(2)}, u32[]{:S(2)}) collective-permute-start(bf16[1536,512]{1,0:T(8,128)(2,1)} %get-tuple-element.450), channel_id=1, source_target_pairs={{0,4},{2,6},{4,0},{6,2},{1,5},{3,7},{5,1},{7,3},{8,12},{10,14},{12... | collective-permute-start | bytes 4718600 | tf_op jit(solution)/shard_map/ppermute | solution.py:799
  496.8 147.9 %reduce-scatter.16.cloned.1.call-start = ((), (), s32[]{:S(2)}) async-start(), calls=%async_computation.15 | async-start | bytes 1966080 | tf_op jit(solution)/shard_map/reduce_scatter | solution.py:813
  496.8 53.0 %collective-permute-start.39 = (bf16[512,1536]{1,0:T(8,128)(2,1)}, bf16[512,1536]{1,0:T(8,128)(2,1)}, u32[]{:S(2)}, u32[]{:S(2)}) collective-permute-start(bf16[512,1536]{1,0:T(8,128)(2,1)} %add_convert_fusion.3), channel_id=1, source_target_pairs={{0,4},{2,6},{4,0},{6,2},{1,5},{3,7},{5,1},{7,3},{8,12},{10,14},{12... | collective-permute-start | bytes 4718600 | tf_op jit(solution)/shard_map/ppermute | solution.py:799
  499.9 49.9 %collective-permute-start.40 = (bf16[768,512]{1,0:T(8,128)(2,1)}, bf16[768,512]{1,0:T(8,128)(2,1)}, u32[]{:S(2)}, u32[]{:S(2)}) collective-permute-start(bf16[768,512]{1,0:T(8,128)(2,1)} %pad_maximum_fusion.8), channel_id=1, source_target_pairs={{0,5},{1,4},{2,7},{3,6},{4,1},{5,0},{6,3},{7,2},{8,13},{9,12},{10,... | collective-permute-start | bytes 2359304 | tf_op jit(solution)/shard_map/ppermute | solution.py:803
  553.0 133.2 %reduce-scatter.18.cloned.1.call-start = ((), (), s32[]{:S(2)}) async-start(), calls=%async_computation.16 | async-start | bytes 737280 | tf_op jit(solution)/shard_map/reduce_scatter | solution.py:813
  599.0 45.7 %collective-permute-start.46 = (bf16[1536,384]{1,0:T(8,128)(2,1)S(1)}, bf16[1536,384]{1,0:T(8,128)(2,1)}, u32[]{:S(2)}, u32[]{:S(2)}) collective-permute-start(bf16[1536,384]{1,0:T(8,128)(2,1)S(1)} %copy-done.21), channel_id=1, source_target_pairs={{0,1},{1,0},{2,3},{3,2},{4,5},{5,4},{6,7},{7,6},{8,9},{9,8},{10,11... | collective-permute-start | bytes 3538952 | tf_op jit(solution)/shard_map/ppermute | solution.py:802
  601.6 43.1 %collective-permute-start.49 = (bf16[768,512]{1,0:T(8,128)(2,1)S(1)}, bf16[768,512]{1,0:T(8,128)(2,1)S(1)}, u32[]{:S(2)}, u32[]{:S(2)}) collective-permute-start(bf16[768,512]{1,0:T(8,128)(2,1)S(1)} %add_convert_fusion.6.refs_0_), channel_id=1, source_target_pairs={{0,1},{1,0},{2,3},{3,2},{4,5},{5,4},{6,7},{7,6},{8,9},{9,8},{10,11... | collective-permute-start | bytes 2359304 | tf_op jit(solution)/shard_map/ppermute | solution.py:802
  658.8 144.6 %reduce-scatter.20.cloned.1.call-start = ((), (), s32[]{:S(2)}) async-start(), calls=%async_computation.17 | async-start | bytes 1474560 | tf_op jit(solution)/shard_map/reduce_scatter | solution.py:813
  695.9 39.0 %collective-permute-start.55 = (bf16[1536,384]{1,0:T(8,128)(2,1)}, bf16[1536,384]{1,0:T(8,128)(2,1)S(1)}, u32[]{:S(2)}, u32[]{:S(2)}) collective-permute-start(bf16[1536,384]{1,0:T(8,128)(2,1)} %qkv_grad.6), channel_id=1, source_target_pairs={{0,1},{1,0},{2,3},{3,2},{4,5},{5,4},{6,7},{7,6},{8,9},{9,8},{10,11... | collective-permute-start | bytes 3538952 | tf_op jit(solution)/shard_map/ppermute | solution.py:802
  697.4 37.5 %collective-permute-start.58 = (bf16[768,512]{1,0:T(8,128)(2,1)}, bf16[768,512]{1,0:T(8,128)(2,1)S(1)}, u32[]{:S(2)}, u32[]{:S(2)}) collective-permute-start(bf16[768,512]{1,0:T(8,128)(2,1)} %collective-permute-done.51.refs_3_), channel_id=1, source_target_pairs={{0,2},{2,0},{4,6},{6,4},{1,3},{3,1},{5,7},{7,5},{8,10},{10,8},{12,... | collective-permute-start | bytes 2359304 | tf_op jit(solution)/shard_map/ppermute | solution.py:800
  698.3 36.6 %collective-permute-start.57 = (bf16[176,1536]{1,0:T(8,128)(2,1)}, bf16[176,1536]{1,0:T(8,128)(2,1)}, u32[]{:S(2)}, u32[]{:S(2)}) collective-permute-start(bf16[176,1536]{1,0:T(8,128)(2,1)} %pad_maximum_fusion.9.refs_0_), channel_id=1, source_target_pairs={{0,1},{1,0},{2,3},{3,2},{4,5},{5,4},{6,7},{7,6},{8,9},{9,8},{10,11... | collective-permute-start | bytes 1622024 | tf_op jit(solution)/shard_map/ppermute | solution.py:802
  764.5 38.9 %collective-permute-start.66 = (bf16[176,1536]{1,0:T(8,128)(2,1)}, bf16[176,1536]{1,0:T(8,128)(2,1)}, u32[]{:S(2)}, u32[]{:S(2)}) collective-permute-start(bf16[176,1536]{1,0:T(8,128)(2,1)} %collective-permute-done.56.refs_2_), channel_id=1, source_target_pairs={{0,2},{2,0},{4,6},{6,4},{1,3},{3,1},{5,7},{7,5},{8,10},{10,8},{12,... | collective-permute-start | bytes 1622024 | tf_op jit(solution)/shard_map/ppermute | solution.py:800
  (111 other events, 1865.1 us)
Sparse Core Ops, SparseCore 0:
  17.3 31.6 all-gather.4
  57.4 44.8 all-gather.6
  104.5 63.8 all-gather.8
  195.7 63.9 all-gather.10
  345.6 36.1 reduce-scatter.7
  384.0 34.2 reduce-scatter.9
  422.8 33.5 reduce-scatter.11
  496.9 33.5 reduce-scatter.13
  553.1 34.4 reduce-scatter.15
  659.0 20.9 reduce-scatter.17
  758.5 27.9 reduce-scatter.19

commit v3 on v2

--- a/solution.py
+++ b/solution.py
@@ -202,17 +202,20 @@
 def span_copy(places, source):
     width = source.shape[1]
     count = places.shape[0]
-
-    def kernel(place_ref, x_ref, o_ref):
-        o_ref[...] = x_ref[...]
-
+    step = 2
+
+    def kernel(place_ref, *refs):
+        for k in range(step):
+            refs[step][k] = refs[k][0]
+
+    spans = as_spans(source)
     (out,) = call(
         kernel,
-        (count,),
-        [pl.BlockSpec((1, SPAN, width), lambda i, place: (place[i], 0, 0))],
-        [pl.BlockSpec((1, SPAN, width), lambda i, place: (i, 0, 0))],
+        (count // step,),
+        [pl.BlockSpec((1, SPAN, width), lambda i, place, k=k: (place[step * i + k], 0, 0)) for k in range(step)],
+        [pl.BlockSpec((step, SPAN, width), lambda i, place: (i, 0, 0))],
         [((count, SPAN, width), source.dtype)],
-        [as_spans(source)],
+        [spans] * step,
         "span_copy",
         [places],
     )
@@ -222,23 +225,28 @@
 def span_join(places, near, far):
     width = near.shape[1]
     count = 2 * near.shape[0] // SPAN
-
-    def kernel(near_ref, far_ref, flag_ref, a_ref, b_ref, o_ref):
-        @pl.when(flag_ref[pl.program_id(0)] == 0)
-        def _():
-            o_ref[...] = a_ref[...]
-
-        @pl.when(flag_ref[pl.program_id(0)] != 0)
-        def _():
-            o_ref[...] = b_ref[...]
+    step = 4
+
+    def kernel(near_ref, far_ref, flag_ref, *refs):
+        out_ref = refs[-1]
+        for k in range(step):
+            is_far = flag_ref[step * pl.program_id(0) + k] != 0
+
+            @pl.when(jnp.logical_not(is_far))
+            def _():
+                out_ref[k] = refs[k][0]
+
+            @pl.when(is_far)
+            def _():
+                out_ref[k] = refs[step + k][0]
 
     (out,) = call(
         kernel,
-        (count,),
-        span_specs(width, 1),
-        [pl.BlockSpec((1, SPAN, width), lambda i, *_: (i, 0, 0))],
+        (count // step,),
+        span_specs(width, step),
+        [pl.BlockSpec((step, SPAN, width), lambda i, *_: (i, 0, 0))],
         [((count, SPAN, width), near.dtype)],
-        [as_spans(near), as_spans(far)],
+        [as_spans(near)] * step + [as_spans(far)] * step,
         "span_join",
         places,
     )
@@ -569,22 +577,27 @@
 
 
 def mixed_back(core, own, far, w_out_rows):
-    rows, width = own.shape
+    rows, cols = own[0].shape
+    count = len(own)
+    width = count * cols
     heads = w_out_rows.shape[0]
     tile = 512
     tiles = rows // tile
 
-    def kernel(core_ref, own_ref, far_ref, w_ref, out_ref, grad_ref):
-        place_half(core_ref, tiles, [own_ref], [far_ref], out_ref)
+    own_spec, far_spec = half_specs(tile, tiles, cols)
+
+    def kernel(core_ref, *refs):
+        w_ref, out_ref, grad_ref = refs[2 * count :]
+        place_half(core_ref, tiles, refs[:count], refs[count : 2 * count], out_ref)
         grad_ref[...] = dot_nt(out_ref[...], w_ref[...]).astype(bf16)
 
     return call(
         kernel,
         (2 * tiles,),
-        half_specs(tile, tiles, width) + [fixed(w_out_rows.shape)],
+        [own_spec] * count + [far_spec] * count + [fixed(w_out_rows.shape)],
         [pl.BlockSpec((tile, width), lambda i, _: (i, 0)), pl.BlockSpec((tile, heads), lambda i, _: (i, 0))],
         [((2 * rows, width), bf16), ((2 * rows, heads), bf16)],
-        [own, far, w_out_rows],
+        [*own, *far, w_out_rows],
         "mixed_back",
         [core],
     )
@@ -1028,28 +1041,29 @@
         scale_rows = rms_scale(values_)
         grad_hidden = cot_ref[...].astype(f32) + norm_back(grad_normed, values_, scale_rows, gain_ref[...])
         outs[0][...] = grad_hidden
-        outs[1][...] = grad_hidden.astype(bf16)
+        for out, at in zip(outs[2:], thirds):
+            out[...] = grad_hidden[:, at].astype(bf16)
 
         @pl.when(pl.program_id(0) == 0)
         def _():
-            outs[2][...] = jnp.zeros(outs[2].shape, f32)
-
-        outs[2][...] += column_sums(grad_normed * values_ * scale_rows)
+            outs[1][...] = jnp.zeros(outs[1].shape, f32)
+
+        outs[1][...] += column_sums(grad_normed * values_ * scale_rows)
 
     up_gx, down_gl = over_x(up_gx), over_y(down_gl)
     received_out = [over_core(a) for a in out_sent]
-    grad_hidden, grad_attended_own, gain_two_sums = sum_rows_call(
+    grad_hidden, gain_two_sums, *grad_attended_own = sum_rows_call(
         back_body,
         mine * tiles_half,
         d_boths,
         back_rhs,
         [*[(r, "plain") for r in received_two], (hidden, "plain"), (cot, "shifted"), (gain_two, "whole")],
-        [((half_rows, width), f32), ((half_rows, width), bf16), ((8, width), f32)],
+        [((half_rows, width), f32), ((8, width), f32)] + [((half_rows, units), bf16)] * len(thirds),
         row_tile,
         "back_own",
     )
     gate_sum = scatter(add(own_grads[0], gate_gy, gate_gx))
-    grad_attended_far = over_core(grad_attended_own)
+    grad_attended_far = [over_core(a) for a in grad_attended_own]
 
     def down_body(left, right, others, outs):
         hidden_ref, *received_refs = others
@@ -1070,10 +1084,10 @@
         row_tile,
         "down_own",
     )
+    grad_attended_own, grad_attended_far, layer_rows, up_gx, down_gl, gate_sum, gate_gl, up_gl = fence(
+        grad_attended_own, grad_attended_far, layer_rows, up_gx, down_gl, gate_sum, gate_gl, up_gl
+    )
     down_gx = add(down_gx, down_gl)
-    grad_attended_own, grad_attended_far, layer_rows, up_gx, down_gx, gate_sum, gate_gl, up_gl = fence(
-        grad_attended_own, grad_attended_far, layer_rows, up_gx, down_gx, gate_sum, gate_gl, up_gl
-    )
 
     pair_order = order.reshape(n_ctx, spans_dev // 2, 2)
     in_half = jnp.where(pair_order[..., 0] // (n_spans // 2) == core, pair_order[..., 0], pair_order[..., 1]) - core * (n_spans // 2)
@@ -1101,7 +1115,7 @@
 
     up_sum = scatter(add(own_grads[1], up_gy, up_gx))
     down_gx = over_x(down_gx)
-    both_gl = over_diagonal(jnp.concatenate([gate_gl, up_gl], axis=0))
+    both_gl = over_y(jnp.concatenate([gate_gl, up_gl], axis=0))
     grad_attended, grad_mixed = mixed_back(mine, grad_attended_own, grad_attended_far, w_out_rows)
     out_grads = [b.reshape(-1, width) for b in out_grad_blocks(place_at, mixed, grad_attended)]
     layer_parts = arrange(layer_rows)
@@ -1111,49 +1125,48 @@
         return attend_back(group, 1, q_aug, keys, values, grad_mixed, mixed, cosine, sine)
 
     down_sum = scatter(add(own_grads[2], down_gy, down_gx))
-    layer_parts = to_slots(layer_parts)
-    out_y, out_last = over_y(out_grads[1]), over_y(out_grads[3])
+    layer_parts = [layer_parts[0], over_core(layer_parts[1]), over_x(layer_parts[2]), layer_parts[3]]
+    both_gl, out_y, out_last = over_x(both_gl), over_y(out_grads[1]), over_y(out_grads[3])
     back_last = back_of(3, q_aug)
+    back_last, q_aug, both_gl, out_last = fence(back_last, q_aug, both_gl, out_last)
     both_sum = add(jnp.concatenate([gate_sum, up_sum], axis=0), both_gl)
-    back_last, q_aug, layer_parts, both_sum, out_y, out_last = fence(back_last, q_aug, layer_parts, both_sum, out_y, out_last)
     qkv_last = qkv_grad(normed_t, *back_last)
     out_x = add(out_grads[2], out_last)
-    qkv_last, q_aug, out_x = fence(qkv_last, q_aug, out_x)
-
-    qkv_last, out_x, both_x, both_y = over_y(qkv_last), over_x(out_x), over_x(both_sum), over_y(both_sum)
+    qkv_last, q_aug, out_x, both_sum, layer_parts, out_y = fence(qkv_last, q_aug, out_x, both_sum, layer_parts, out_y)
+
+    qkv_last, out_x, both_x = over_y(qkv_last), over_x(out_x), over_x(both_sum)
     back_x = back_of(2, q_aug)
-    back_x, q_aug, qkv_last, out_x, both_x, both_y, down_sum = fence(back_x, q_aug, qkv_last, out_x, both_x, both_y, down_sum)
+    back_x, q_aug, qkv_last, out_x, down_sum = fence(back_x, q_aug, qkv_last, out_x, down_sum)
     qkv_x = add(qkv_grad(normed_t, *back_x), qkv_last)
     out_sum = add(out_grads[0], out_y, out_x)
-    qkv_x, out_sum, q_aug = fence(qkv_x, out_sum, q_aug)
+    qkv_x, out_sum, q_aug, both_sum, both_x = fence(qkv_x, out_sum, q_aug, both_sum, both_x)
 
     out_sum = scatter(out_sum)
-    qkv_x, both_last = over_x(qkv_x), over_y(both_x)
-    both_far = [over_core(a) for a in (both_sum, both_y, both_x)]
+    qkv_x, both_last, both_y = over_x(qkv_x), over_y(both_x), over_y(both_sum)
+    both_far = [over_core(a) for a in (both_sum, both_x)]
     back_y = back_of(1, q_aug)
-    back_y, q_aug, qkv_x, both_last, both_far, out_sum = fence(back_y, q_aug, qkv_x, both_last, both_far, out_sum)
+    back_y, q_aug, both_far, out_sum = fence(back_y, q_aug, both_far, out_sum)
     qkv_y = qkv_grad(normed_t, *back_y)
     row_sum = jnp.concatenate([down_sum, out_sum], axis=0)
-    qkv_y, q_aug, row_sum = fence(qkv_y, q_aug, row_sum)
-
+    qkv_y, q_aug, row_sum, qkv_x, both_y, both_last, layer_parts = fence(qkv_y, q_aug, row_sum, qkv_x, both_y, both_last, layer_parts)
+
+    layer_parts[3] = over_both(layer_parts[3])
     qkv_y, row_x, row_y = over_y(qkv_y), over_x(row_sum), over_y(row_sum)
-    both_far.append(over_core(both_last))
+    both_far = [both_far[0], over_core(both_y), both_far[1], over_core(both_last)]
     back_own = back_of(0, q_aug)
-    back_own, qkv_y, row_x, row_y, both_far = fence(back_own, qkv_y, row_x, row_y, both_far)
+    back_own, both_far = fence(back_own, both_far)
 
     depth = w_qkv.shape[0]
     q_width, k_width = queries.shape[1], keys.shape[1]
     in_rhs = [(w_qkv, (depth, q_width), (0, 0))]
     in_rhs += [(w_qkv, (depth, k_width), (0, q_width // k_width + which)) for which in range(2)]
     qkv_sum = add(qkv_grad(normed_t, *back_own), qkv_y, qkv_x)
-    qkv_sum, back_own = fence(qkv_sum, back_own)
+    qkv_sum, back_own, row_x, row_y, layer_parts = fence(qkv_sum, back_own, row_x, row_y, layer_parts)
     in_lhs = [*back_own, *back_y, *back_x, *back_last]
     qkv_sum = scatter(qkv_sum)
     row_last = over_y(row_x)
-    row_far = [over_core(row_sum)]
     received_in = [over_core(a) for a in sent_parts(in_lhs, in_rhs, in_dot, "in_other")]
-    received_in, row_last, row_far = fence(received_in, row_last, row_far)
-    row_far += [over_core(a) for a in (row_y, row_x, row_last)]
+    row_far = [over_core(a) for a in (row_sum, row_y, row_x, row_last)]
 
     def in_body(left, right, others, outs):
         *received_refs, x_ref, grad_ref, gain_ref = others
@@ -1195,15 +1208,15 @@
     grad_w_down, grad_w_out = unit_rows(where, [row_sum, row_y, row_x, row_last] + row_far, unit_cols)
     for step in (over_core, over_y):
         sums = sums + step(sums)
-    token_parts, grad_w_gate, grad_w_up, grad_w_down, grad_w_out, qkv_last, sums = fence(
-        token_parts, grad_w_gate, grad_w_up, grad_w_down, grad_w_out, qkv_last, sums
-    )
-
     total = lax.dynamic_slice_in_dim(sums, shard * gain_width, gain_width, 1)
     for step in range(1, n_shard):
         to = lax.dynamic_slice_in_dim(sums, (shard + step) % n_shard * gain_width, gain_width, 1)
         total = total + lax.ppermute(to, "shard", [(z, (z + step) % n_shard) for z in range(n_shard)])
-    grad_w_query, grad_w_key, grad_w_value = head_columns(where, both_cores([qkv_sum, qkv_y, qkv_x, qkv_last]))
+    head_grads = head_columns(where, both_cores([qkv_sum, qkv_y, qkv_x, qkv_last]))
+    token_parts, grad_w_gate, grad_w_up, grad_w_down, grad_w_out, head_grads, total = fence(
+        token_parts, grad_w_gate, grad_w_up, grad_w_down, grad_w_out, head_grads, total
+    )
+    grad_w_query, grad_w_key, grad_w_value = head_grads
     grad_tokens = from_slots(token_parts)
 
     return (

time: 884 us -> 806 us (0.912)
  waiting for transfers between devices: 170 us -> 98.1 us
    ppermute x22 -> x23, waiting for transfers between devices: 62.6 us -> 32.6 us  [chip_layer(): over_y = lambda a: lax.ppermute(a, 'batch', [(0, 1), (1, 0)])]
    ppermute x2, waiting for transfers between devices: 14.9 us -> 0.01 us  [chip_layer(): over_both = lambda a: lax.ppermute(a, 'ctx', perm_both)]
    ppermute x2 -> x1, waiting for transfers between devices: 13.6 us -> 0.01 us  [chip_layer(): over_diagonal = lambda a: lax.ppermute(a, ('ctx', 'batch'), perm_diagonal)]
    ppermute x20 -> x21, waiting for transfers between devices: 58.7 us -> 48.9 us  [chip_layer(): over_x = lambda a: lax.ppermute(a, 'ctx', perm_x)]
    ppermute x34 -> x36, waiting for transfers between devices: 12.7 us -> 3.38 us  [chip_layer(): over_core = lambda a: lax.ppermute(a, 'ctx', perm_core)]
    ppermute x22 -> x23, starting transfers between devices: 24 us -> 23.4 us  [chip_layer(): over_y = lambda a: lax.ppermute(a, 'batch', [(0, 1), (1, 0)])]
    ppermute x20 -> x21, starting transfers between devices: 23.3 us -> 23.2 us  [chip_layer(): over_x = lambda a: lax.ppermute(a, 'ctx', perm_x)]
  transfers between devices with their start and end apart: 94 -> 97, of which waited for: 31 -> 27; matrix products, arithmetic and copies ran while one was open for 7% -> 8% of each run, Pallas kernels for 53% -> 63%
where the time goes in v3:
time: 806 us; the launch traced here: 798 us
  Pallas kernels  505 us (63%)
  waiting for transfers between devices  98.1 us (12%)
  starting transfers between devices  59.7 us (7%)
  other arithmetic  51.2 us (6%)
  local copies, waits for them, and re-layouts  43.6 us (5%)
  blocking collectives  24.6 us (3%)
  between operations  15.5 us (2%)
    pallas_call x37, Pallas kernels, call(): pl.pallas_call(kernel, grid_spec=pltpu.PrefetchScalarGridSpec(num_scalar_...  505 us
    ppermute x21, waiting for transfers between devices, chip_layer(): over_x = lambda a: lax.ppermute(a, 'ctx', perm_x)  48.9 us
    ppermute x23, waiting for transfers between devices, chip_layer(): over_y = lambda a: lax.ppermute(a, 'batch', [(0, 1), (1, 0)])  32.6 us
    convert_element_type x9, other arithmetic, add(): functools.reduce(lambda a, b: a + b, [t.astype(f32) for t in terms])  25.2 us
    all_gather x1, blocking collectives, over_z(): gathered = lax.all_gather(piece, 'shard', axis=0, tiled=True)  24.6 us
    ppermute x23, starting transfers between devices, chip_layer(): over_y = lambda a: lax.ppermute(a, 'batch', [(0, 1), (1, 0)])  23.4 us
    ppermute x21, starting transfers between devices, chip_layer(): over_x = lambda a: lax.ppermute(a, 'ctx', perm_x)  23.2 us
  transfers between devices with their start and end apart: 97, of which 27 were waited for; matrix products, arithmetic and copies ran while one was open for 8% of the time, Pallas kernels for 63%

profile of v3, /device:TPU:0, one launch (start us, length us, event | category | flops | bytes accessed | tf_op | source)
XLA Modules:
  0.0 797.6 jit_solution(150625775946270773)
XLA Ops:
  24.6 27.0 %collective-permute-done.1 = s32[512]{0:T(512)S(1)} collective-permute-done((s32[512]{0:T(512)S(1)}, s32[512]{0:T(512)S(1)}, u32[]{:S(2)}, u32[]{:S(2)}) %collective-permute-start.1) | collective-permute-done | bytes 2080 | tf_op jit(solution)/shard_map/ppermute | solution.py:812
  61.3 24.6 %all_gather.17 = bf16[768,384]{1,0:T(8,128)(2,1)} all-gather(bf16[192,384]{1,0:T(8,128)(2,1)S(1)} %pad_maximum_fusion.12), channel_id=1, replica_groups=mesh['shard'=4,'ctx'=4,'batch'=2] {'shard'}, dimensions={0}, use_global_device_ids=true | all-gather | bytes 737280 | tf_op jit(solution)/shard_map/all_gather | solution.py:819
  112.7 28.3 %front.1 = (bf16[2048,1536]{1,0:T(8,128)(2,1)}, bf16[2048,1536]{1,0:T(8,128)(2,1)}, bf16[1536,2048]{1,0:T(8,128)(2,1)}, bf16[2048,1024]{1,0:T(8,128)(2,1)}, bf16...) custom-call(s32[16]{0:T(128)} %get-tuple-element.679.near_ref, ...), custom_call_target="tpu_custom_call" | custom-call | flops 1000 | bytes 1000 | tf_op jit(solution)/shard_map/front/pallas_call | solution.py:74
  141.0 33.2 %attend.1 = (bf16[2048,1024]{1,0:T(8,128)(2,1)}, bf16[2048,1024]{1,0:T(8,128)(2,1)}) custom-call(bf16[2048,1024]{1,0:T(8,128)(2,1)} %get-tuple-element.348.q_ref, bf16[2048,512]{1,0:T(8,128)(2,1)} %get-tuple-element.349.k_ref, bf16[2048,512]{1,0:T(8,128)(2,1)} %get-tuple-element.350.v_ref), custom_call_target="tpu_custom_call" | custom-call | flops 1000 | bytes 1000 | tf_op jit(solution)/shard_map/attend/pallas_call | solution.py:74
  197.8 11.0 %out_own.1 = (f32[1024,1536]{1,0:T(8,128)}, bf16[1024,512]{1,0:T(8,128)(2,1)}, bf16[1024,512]{1,0:T(8,128)(2,1)}, bf16[1024,512]{1,0:T(8,128)(2,1)}) custom-call(s32[1]{0:T(128)S(6)} %mul.113.base_ref, bf16[2048,1024]{1,0:T(8,128)(2,1)} %get-tuple-element.360.refs_0_.mixed_ref.o_ref, bf16[1024,1536]{1,0:T(8,128)(2,1)} %out_rows.1.refs_1_.refs_6_, ...), custom_call_target="tpu_custom_call" | custom-call | flops 1000 | bytes 1000 | tf_op jit(solution)/shard_map/out_own/pallas_call | solution.py:74
  209.7 9.1 %span_join.1 = bf16[16,128,1536]{2,1,0:T(8,128)(2,1)} custom-call(s32[16]{0:T(128)} %get-tuple-element.679.near_ref, s32[16]{0:T(128)} %get-tuple-element.678.far_ref, s32[16]{0:T(128)} %copy-done.36, bf16[8,128,1536]{2,1,0:T(8,128)(2,1)} %bitcast.89, bf16[8,128,1536]{2,1,0:T(8,128)(2,1)} %bitcast.90, bf16[8,128,1536]{2,1,0:T(8,128)(2,1)} %bitcast.91, ...), custom_call_target="tpu_custom_call" | custom-call | flops 1000 | bytes 1000 | tf_op jit(solution)/shard_map/span_join/pallas_call | solution.py:74
  218.8 10.5 %collective-permute-done.20.gate_ref.refs_10_ = bf16[4,384,512]{2,1,0:T(8,128)(2,1)} collective-permute-done((bf16[4,384,512]{2,1,0:T(8,128)(2,1)}, bf16[4,384,512]{2,1,0:T(8,128)(2,1)}, u32[]{:S(2)}, u32[]{:S(2)}) %collective-permute-start.20) | collective-permute-done | bytes 1572896 | tf_op jit(solution)/shard_map/ppermute | solution.py:812
  234.9 9.5 %join_halves.1 = (bf16[2048,1536]{1,0:T(8,128)(2,1)}, bf16[1536,2048]{1,0:T(8,128)(2,1)}) custom-call(s32[1]{0:T(128)} %bitcast.3.core_ref, bf16[1024,512]{1,0:T(8,128)(2,1)} %get-tuple-element.376.refs_0_, bf16[1024,512]{1,0:T(8,128)(2,1)} %get-tuple-element.377.refs_1_, bf16[1024,512]{1,0:T(8,128)(2,1)} %get-tuple-element.378.refs_2_, ...), custom_call_target="tpu_custom_call" | custom-call | flops 1000 | bytes 1000 | tf_op jit(solution)/shard_map/join_halves/pallas_call | solution.py:74
  244.4 15.1 %hidden_units.4 = (bf16[2048,512]{1,0:T(8,128)(2,1)}, bf16[2048,1024]{1,0:T(8,128)(2,1)}) custom-call(bf16[2048,1536]{1,0:T(8,128)(2,1)} %get-tuple-element.420.n_ref, bf16[2048,1536]{1,0:T(8,128)(2,1)} %bitcast.70, bf16[4,384,512]{2,1,0:T(8,128)(2,1)} %bitcast.97, bf16[4,384,512]{2,1,0:T(8,128)(2,1)} %get-tuple-element.389.up_ref.refs_5_, ...), custom_call_target="tpu_custom_call" | custom-call | flops 1000 | bytes 1000 | tf_op jit(solution)/shard_map/hidden_units/pallas_call | solution.py:74
  259.6 17.4 %feed_grads.4 = (bf16[1536,512]{1,0:T(8,128)(2,1)}, bf16[1536,512]{1,0:T(8,128)(2,1)}, bf16[512,1536]{1,0:T(8,128)(2,1)}) custom-call(bf16[1536,2048]{1,0:T(8,128)(2,1)} %get-tuple-element.386.n_ref, bf16[2048,1536]{1,0:T(8,128)(2,1)} %bitcast.71, bf16[2048,512]{1,0:T(8,128)(2,1)} %get-tuple-element.440.product_ref.refs_0_, ...), custom_call_target="tpu_custom_call" | custom-call | flops 1000 | bytes 1000 | tf_op jit(solution)/shard_map/feed_grads/pallas_call | solution.py:74
  279.0 15.2 %hidden_units.5 = (bf16[2048,512]{1,0:T(8,128)(2,1)}, bf16[2048,1024]{1,0:T(8,128)(2,1)}) custom-call(bf16[2048,1536]{1,0:T(8,128)(2,1)} %get-tuple-element.420.n_ref, bf16[2048,1536]{1,0:T(8,128)(2,1)} %bitcast.72, bf16[4,384,512]{2,1,0:T(8,128)(2,1)} %collective-permute-done.9.gate_ref.refs_6_, ...), custom_call_target="tpu_custom_call" | custom-call | flops 1000 | bytes 1000 | tf_op jit(solution)/shard_map/hidden_units/pallas_call | solution.py:74
  294.2 17.5 %feed_grads.5 = (bf16[1536,512]{1,0:T(8,128)(2,1)}, bf16[1536,512]{1,0:T(8,128)(2,1)}, bf16[512,1536]{1,0:T(8,128)(2,1)}) custom-call(bf16[1536,2048]{1,0:T(8,128)(2,1)} %get-tuple-element.386.n_ref, bf16[2048,1536]{1,0:T(8,128)(2,1)} %bitcast.73, bf16[2048,512]{1,0:T(8,128)(2,1)} %get-tuple-element.441.product_ref.refs_1_, ...), custom_call_target="tpu_custom_call" | custom-call | flops 1000 | bytes 1000 | tf_op jit(solution)/shard_map/feed_grads/pallas_call | solution.py:74
  314.4 15.3 %hidden_units.6 = (bf16[2048,512]{1,0:T(8,128)(2,1)}, bf16[2048,1024]{1,0:T(8,128)(2,1)}) custom-call(bf16[2048,1536]{1,0:T(8,128)(2,1)} %get-tuple-element.420.n_ref, bf16[2048,1536]{1,0:T(8,128)(2,1)} %bitcast.74, bf16[4,384,512]{2,1,0:T(8,128)(2,1)} %copy-done.6, bf16[4,768,512]{2,1,0:T(8,128)(2,1)} %bitcast.79, bf16[4,768,512]{2,1,0:T(8,128)(2,1)} %bitcast.80), custom_call_target="tpu_custom_call" | custom-call | flops 1000 | bytes 1000 | tf_op jit(solution)/shard_map/hidden_units/pallas_call | solution.py:74
  329.8 17.5 %feed_grads.6 = (bf16[1536,512]{1,0:T(8,128)(2,1)}, bf16[1536,512]{1,0:T(8,128)(2,1)}, bf16[512,1536]{1,0:T(8,128)(2,1)}) custom-call(bf16[1536,2048]{1,0:T(8,128)(2,1)} %get-tuple-element.386.n_ref, bf16[2048,1536]{1,0:T(8,128)(2,1)} %bitcast.75, bf16[2048,512]{1,0:T(8,128)(2,1)} %get-tuple-element.442.product_ref.refs_2_, ...), custom_call_target="tpu_custom_call" | custom-call | flops 1000 | bytes 1000 | tf_op jit(solution)/shard_map/feed_grads/pallas_call | solution.py:74
  349.5 15.1 %hidden_units.7 = (bf16[2048,512]{1,0:T(8,128)(2,1)}, bf16[2048,1024]{1,0:T(8,128)(2,1)}) custom-call(bf16[2048,1536]{1,0:T(8,128)(2,1)} %get-tuple-element.420.n_ref, bf16[2048,1536]{1,0:T(8,128)(2,1)} %bitcast.76, bf16[4,384,512]{2,1,0:T(8,128)(2,1)} %collective-permute-done.20.gate_ref.refs_10_, bf16[4,384,512]{2,1,0:T(8,128)(2,1)} %copy-done.5, ...), custom_call_target="tpu_custom_call" | custom-call | flops 1000 | bytes 1000 | tf_op jit(solution)/shard_map/hidden_units/pallas_call | solution.py:74
  364.6 17.5 %feed_grads.7 = (bf16[1536,512]{1,0:T(8,128)(2,1)}, bf16[1536,512]{1,0:T(8,128)(2,1)}, bf16[512,1536]{1,0:T(8,128)(2,1)}) custom-call(bf16[1536,2048]{1,0:T(8,128)(2,1)} %get-tuple-element.386.n_ref, bf16[2048,1536]{1,0:T(8,128)(2,1)} %bitcast.77, bf16[2048,512]{1,0:T(8,128)(2,1)} %get-tuple-element.443.product_ref.refs_3_, ...), custom_call_target="tpu_custom_call" | custom-call | flops 1000 | bytes 1000 | tf_op jit(solution)/shard_map/feed_grads/pallas_call | solution.py:74
  387.0 20.9 %back_other.1 = (bf16[1024,512]{1,0:T(8,128)(2,1)}, bf16[1024,512]{1,0:T(8,128)(2,1)}, bf16[1024,512]{1,0:T(8,128)(2,1)}) custom-call(s32[1]{0:T(128)S(6)} %mul.134.base_ref, bf16[2048,1024]{1,0:T(8,128)(2,1)} %get-tuple-element.433.both_ref.refs_0_, bf16[2048,1024]{1,0:T(8,128)(2,1)} %get-tuple-element.434.both_ref.refs_1_, ...), custom_call_target="tpu_custom_call" | custom-call | flops 1000 | bytes 1000 | tf_op jit(solution)/shard_map/back_other/pallas_call | solution.py:74
  408.5 11.3 %down_other.1 = (bf16[1024,512]{1,0:T(8,128)(2,1)}, bf16[1024,512]{1,0:T(8,128)(2,1)}, bf16[1024,512]{1,0:T(8,128)(2,1)}) custom-call(s32[1]{0:T(128)S(6)} %mul.134.base_ref, bf16[2048,512]{1,0:T(8,128)(2,1)} %get-tuple-element.440.product_ref.refs_0_, bf16[2048,512]{1,0:T(8,128)(2,1)} %get-tuple-element.441.product_ref.refs_1_, ...), custom_call_target="tpu_custom_call" | custom-call | flops 1000 | bytes 1000 | tf_op jit(solution)/shard_map/down_other/pallas_call | solution.py:74
  427.9 24.5 %back_own.1 = (f32[1024,1536]{1,0:T(8,128)}, f32[8,1536]{1,0:T(8,128)}, bf16[1024,512]{1,0:T(8,128)(2,1)}, bf16[1024,512]{1,0:T(8,128)(2,1)}, bf16[1024,512]{1,0:T(8,128)(2,1)}) custom-call(s32[1]{0:T(128)S(6)} %mul.113.base_ref, bf16[2048,1024]{1,0:T(8,128)(2,1)} %get-tuple-element.433.both_ref.refs_0_, ...), custom_call_target="tpu_custom_call" | custom-call | flops 1000 | bytes 1000 | tf_op jit(solution)/shard_map/back_own/pallas_call | solution.py:74
  454.0 12.7 %down_own.1 = bf16[1024,1536]{1,0:T(8,128)(2,1)} custom-call(s32[1]{0:T(128)S(6)} %mul.113.base_ref, bf16[2048,512]{1,0:T(8,128)(2,1)} %get-tuple-element.440.product_ref.refs_0_, bf16[2048,512]{1,0:T(8,128)(2,1)} %get-tuple-element.441.product_ref.refs_1_, bf16[2048,512]{1,0:T(8,128)(2,1)} %get-tuple-element.442.product_ref.refs_2_, ...), custom_call_target="tpu_custom_call" | custom-call | flops 1000 | bytes 1000 | tf_op jit(solution)/shard_map/down_own/pallas_call | solution.py:74
  480.5 12.2 %mixed_back.1 = (bf16[2048,1536]{1,0:T(8,128)(2,1)}, bf16[2048,1024]{1,0:T(8,128)(2,1)}) custom-call(s32[1]{0:T(128)} %bitcast.3.core_ref, bf16[1024,512]{1,0:T(8,128)(2,1)} %get-tuple-element.470.refs_0_, bf16[1024,512]{1,0:T(8,128)(2,1)} %get-tuple-element.471.refs_1_, bf16[1024,512]{1,0:T(8,128)(2,1)} %get-tuple-element.472.refs_2_, ...), custom_call_target="tpu_custom_call" | custom-call | flops 1000 | bytes 1000 | tf_op jit(solution)/shard_map/mixed_back/pallas_call | solution.py:74
  492.7 12.1 %out_grads.1 = (bf16[4,48,1536]{2,1,0:T(8,128)(2,1)}, bf16[4,48,1536]{2,1,0:T(8,128)(2,1)}, bf16[4,48,1536]{2,1,0:T(8,128)(2,1)}, bf16[4,48,1536]{2,1,0:T(8,128)(2,1)}) custom-call(s32[1]{0:T(128)} %bitcast.21.place_ref, bf16[2048,1024]{1,0:T(8,128)(2,1)} %get-tuple-element.360.refs_0_.mixed_ref.o_ref, bf16[2048,1536]{1,0:T(8,128)(2,1)} %get-tuple-element.477.grad_ref), custom_call_target="tpu_custom_call" | custom-call | flops 1000 | bytes 1000 | tf_op jit(solution)/shard_map/out_grads/pallas_call | solution.py:74
  520.8 20.7 %attend_back.4 = (bf16[2048,256]{1,0:T(8,128)(2,1)}, bf16[2048,128]{1,0:T(8,128)(2,1)}, bf16[2048,128]{1,0:T(8,128)(2,1)}) custom-call(bf16[2048,1024]{1,0:T(8,128)(2,1)} %get-tuple-element.546.q_ref, bf16[2048,512]{1,0:T(8,128)(2,1)} %get-tuple-element.349.k_ref, bf16[2048,512]{1,0:T(8,128)(2,1)} %get-tuple-element.350.v_ref, ...), custom_call_target="tpu_custom_call" | custom-call | flops 1000 | bytes 1000 | tf_op jit(solution)/shard_map/attend_back/pallas_call | solution.py:74
  543.5 8.1 %qkv_grad.4 = bf16[1536,384]{1,0:T(8,128)(2,1)} custom-call(bf16[1536,2048]{1,0:T(8,128)(2,1)} %get-tuple-element.347.n_ref, bf16[2048,256]{1,0:T(8,128)(2,1)} %get-tuple-element.496.q_ref.refs_9_, bf16[2048,128]{1,0:T(8,128)(2,1)} %get-tuple-element.497.k_ref.refs_10_, bf16[2048,128]{1,0:T(8,128)(2,1)} %get-tuple-element.498.v_ref.refs_11_, ...), custom_call_target="tpu_custom_call" | custom-call | flops 1000 | bytes 1000 | tf_op jit(solution)/shard_map/qkv_grad/pallas_call | solution.py:74
  556.4 20.8 %attend_back.5 = (bf16[2048,256]{1,0:T(8,128)(2,1)}, bf16[2048,128]{1,0:T(8,128)(2,1)}, bf16[2048,128]{1,0:T(8,128)(2,1)}) custom-call(bf16[2048,1024]{1,0:T(8,128)(2,1)} %get-tuple-element.546.q_ref, bf16[2048,512]{1,0:T(8,128)(2,1)} %get-tuple-element.349.k_ref, bf16[2048,512]{1,0:T(8,128)(2,1)} %get-tuple-element.350.v_ref, ...), custom_call_target="tpu_custom_call" | custom-call | flops 1000 | bytes 1000 | tf_op jit(solution)/shard_map/attend_back/pallas_call | solution.py:74
  599.3 20.6 %attend_back.6 = (bf16[2048,256]{1,0:T(8,128)(2,1)}, bf16[2048,128]{1,0:T(8,128)(2,1)}, bf16[2048,128]{1,0:T(8,128)(2,1)}) custom-call(bf16[2048,1024]{1,0:T(8,128)(2,1)} %get-tuple-element.546.q_ref, bf16[2048,512]{1,0:T(8,128)(2,1)} %get-tuple-element.349.k_ref, bf16[2048,512]{1,0:T(8,128)(2,1)} %get-tuple-element.350.v_ref, ...), custom_call_target="tpu_custom_call" | custom-call | flops 1000 | bytes 1000 | tf_op jit(solution)/shard_map/attend_back/pallas_call | solution.py:74
  620.0 8.4 %qkv_grad.6 = bf16[1536,384]{1,0:T(8,128)(2,1)} custom-call(bf16[1536,2048]{1,0:T(8,128)(2,1)} %get-tuple-element.347.n_ref, bf16[2048,256]{1,0:T(8,128)(2,1)} %get-tuple-element.535.q_ref.refs_3_, bf16[2048,128]{1,0:T(8,128)(2,1)} %get-tuple-element.536.k_ref.refs_4_, bf16[2048,128]{1,0:T(8,128)(2,1)} %get-tuple-element.537.v_ref.refs_5_, ...), custom_call_target="tpu_custom_call" | custom-call | flops 1000 | bytes 1000 | tf_op jit(solution)/shard_map/qkv_grad/pallas_call | solution.py:74
  638.8 20.6 %attend_back.7 = (bf16[2048,256]{1,0:T(8,128)(2,1)}, bf16[2048,128]{1,0:T(8,128)(2,1)}, bf16[2048,128]{1,0:T(8,128)(2,1)}) custom-call(bf16[2048,1024]{1,0:T(8,128)(2,1)} %get-tuple-element.546.q_ref, bf16[2048,512]{1,0:T(8,128)(2,1)} %get-tuple-element.349.k_ref, bf16[2048,512]{1,0:T(8,128)(2,1)} %get-tuple-element.350.v_ref, ...), custom_call_target="tpu_custom_call" | custom-call | flops 1000 | bytes 1000 | tf_op jit(solution)/shard_map/attend_back/pallas_call | solution.py:74
  660.7 8.1 %qkv_grad.7 = bf16[1536,384]{1,0:T(8,128)(2,1)} custom-call(bf16[1536,2048]{1,0:T(8,128)(2,1)} %get-tuple-element.347.n_ref, bf16[2048,256]{1,0:T(8,128)(2,1)} %get-tuple-element.564.q_ref.refs_0_, bf16[2048,128]{1,0:T(8,128)(2,1)} %get-tuple-element.565.k_ref.refs_1_, bf16[2048,128]{1,0:T(8,128)(2,1)} %get-tuple-element.566.v_ref.refs_2_, ...), custom_call_target="tpu_custom_call" | custom-call | flops 1000 | bytes 1000 | tf_op jit(solution)/shard_map/qkv_grad/pallas_call | solution.py:74
  674.6 11.6 %in_other.1 = (bf16[1024,512]{1,0:T(8,128)(2,1)}, bf16[1024,512]{1,0:T(8,128)(2,1)}, bf16[1024,512]{1,0:T(8,128)(2,1)}) custom-call(s32[1]{0:T(128)S(6)} %mul.134.base_ref, bf16[2048,256]{1,0:T(8,128)(2,1)} %get-tuple-element.564.q_ref.refs_0_, bf16[2048,128]{1,0:T(8,128)(2,1)} %get-tuple-element.565.k_ref.refs_1_, ...), custom_call_target="tpu_custom_call" | custom-call | flops 1000 | bytes 1000 | tf_op jit(solution)/shard_map/in_other/pallas_call | solution.py:74
  691.5 10.3 %collective-permute-done.69.refs_3_ = bf16[176,1536]{1,0:T(8,128)(2,1)} collective-permute-done((bf16[176,1536]{1,0:T(8,128)(2,1)}, bf16[176,1536]{1,0:T(8,128)(2,1)}, u32[]{:S(2)}, u32[]{:S(2)}) %collective-permute-start.69) | collective-permute-done | bytes 540704 | tf_op jit(solution)/shard_map/ppermute | solution.py:815
  702.3 15.3 %in_own.1 = (bf16[1024,1536]{1,0:T(8,128)(2,1)}, f32[8,1536]{1,0:T(8,128)}) custom-call(s32[1]{0:T(128)S(6)} %mul.113.base_ref, bf16[2048,256]{1,0:T(8,128)(2,1)} %get-tuple-element.564.q_ref.refs_0_, bf16[2048,128]{1,0:T(8,128)(2,1)} %get-tuple-element.565.k_ref.refs_1_, bf16[2048,128]{1,0:T(8,128)(2,1)} %get-tuple-element.566.v_ref.refs_2_, ...), custom_call_target="tpu_custom_call" | custom-call | flops 1000 | bytes 1000 | tf_op jit(solution)/shard_map/in_own/pallas_call | solution.py:74
  (393 shorter events, 260.0 us)
Async XLA Ops:
  7.2 46.6 %all-gather.5.cloned.1.call-start = ((), (), s32[]{:S(2)}) async-start(), calls=%async_computation.7 | async-start | bytes 1536000 | tf_op jit(solution)/shard_map/all_gather | solution.py:819
  14.2 37.5 %collective-permute-start = (bf16[512,1536]{1,0:T(8,128)(2,1)S(1)}, bf16[512,1536]{1,0:T(8,128)(2,1)}, u32[]{:S(2)}, u32[]{:S(2)}) collective-permute-start(bf16[512,1536]{1,0:T(8,128)(2,1)S(1)} %get-tuple-element.319), channel_id=1, source_target_pairs={{0,4},{2,6},{4,0},{6,2},{1,5},{3,7},{5,1},{7,3},{8,12},{10,14},{12... | collective-permute-start | bytes 4718600 | tf_op jit(solution)/shard_map/ppermute | solution.py:812
  17.2 85.1 %all-gather.7.cloned.1.call-start = ((), (), s32[]{:S(2)}) async-start(), calls=%async_computation.8 | async-start | bytes 1966080 | tf_op jit(solution)/shard_map/all_gather | solution.py:819
  57.3 119.0 %all-gather.9.cloned.1.call-start = ((), (), s32[]{:S(2)}) async-start(), calls=%async_computation.9 | async-start | bytes 3932160 | tf_op jit(solution)/shard_map/all_gather | solution.py:819
  104.7 207.0 %all-gather.11.cloned.1.call-start = ((), (), s32[]{:S(2)}) async-start(), calls=%async_computation.10 | async-start | bytes 3932160 | tf_op jit(solution)/shard_map/all_gather | solution.py:819
  104.9 69.3 %collective-permute-start.8 = (bf16[512,1536]{1,0:T(8,128)(2,1)S(1)}, bf16[512,1536]{1,0:T(8,128)(2,1)}, u32[]{:S(2)}, u32[]{:S(2)}) collective-permute-start(bf16[512,1536]{1,0:T(8,128)(2,1)S(1)} %copy-done.19), channel_id=1, source_target_pairs={{0,4},{2,6},{4,0},{6,2},{1,5},{3,7},{5,1},{7,3},{8,12},{10,14},{12... | collective-permute-start | bytes 4718600 | tf_op jit(solution)/shard_map/ppermute | solution.py:812
  106.0 75.2 %collective-permute-start.9 = (bf16[4,384,512]{2,1,0:T(8,128)(2,1)}, bf16[4,384,512]{2,1,0:T(8,128)(2,1)}, u32[]{:S(2)}, u32[]{:S(2)}) collective-permute-start(bf16[4,384,512]{2,1,0:T(8,128)(2,1)} %bitcast.95), channel_id=1, source_target_pairs={{0,1},{1,0},{2,3},{3,2},{4,5},{5,4},{6,7},{7,6},{8,9},{9,8},{10,11... | collective-permute-start | bytes 4718600 | tf_op jit(solution)/shard_map/ppermute | solution.py:815
  109.2 72.0 %collective-permute-start.10 = (bf16[4,192,384]{2,1,0:T(8,128)(2,1)}, bf16[4,192,384]{2,1,0:T(8,128)(2,1)}, u32[]{:S(2)}, u32[]{:S(2)}) collective-permute-start(bf16[4,192,384]{2,1,0:T(8,128)(2,1)} %bitcast.18.refs_0_), channel_id=1, source_target_pairs={{0,1},{1,0},{2,3},{3,2},{4,5},{5,4},{6,7},{7,6},{8,9},{9,8},{10,11... | collective-permute-start | bytes 1769480 | tf_op jit(solution)/shard_map/ppermute | solution.py:815
  110.0 71.2 %collective-permute-start.11 = (bf16[4,192,384]{2,1,0:T(8,128)(2,1)}, bf16[4,192,384]{2,1,0:T(8,128)(2,1)}, u32[]{:S(2)}, u32[]{:S(2)}) collective-permute-start(bf16[4,192,384]{2,1,0:T(8,128)(2,1)} %bitcast.18.refs_0_), channel_id=1, source_target_pairs={{0,4},{2,6},{4,0},{6,2},{1,5},{3,7},{5,1},{7,3},{8,12},{10,14},{12... | collective-permute-start | bytes 1769480 | tf_op jit(solution)/shard_map/ppermute | solution.py:812
  111.0 70.2 %collective-permute-start.12 = (bf16[4,192,384]{2,1,0:T(8,128)(2,1)}, bf16[4,192,384]{2,1,0:T(8,128)(2,1)}, u32[]{:S(2)}, u32[]{:S(2)}) collective-permute-start(bf16[4,192,384]{2,1,0:T(8,128)(2,1)} %bitcast.18.refs_0_), channel_id=1, source_target_pairs={{0,5},{1,4},{2,7},{3,6},{4,1},{5,0},{6,3},{7,2},{8,13},{9,12},{10,... | collective-permute-start | bytes 1769480 | tf_op jit(solution)/shard_map/ppermute | solution.py:816
  192.7 36.6 %collective-permute-start.20 = (bf16[4,384,512]{2,1,0:T(8,128)(2,1)}, bf16[4,384,512]{2,1,0:T(8,128)(2,1)}, u32[]{:S(2)}, u32[]{:S(2)}) collective-permute-start(bf16[4,384,512]{2,1,0:T(8,128)(2,1)} %bitcast.96), channel_id=1, source_target_pairs={{0,4},{2,6},{4,0},{6,2},{1,5},{3,7},{5,1},{7,3},{8,12},{10,14},{12... | collective-permute-start | bytes 4718600 | tf_op jit(solution)/shard_map/ppermute | solution.py:812
  194.8 37.0 %collective-permute-start.21 = (bf16[4,384,512]{2,1,0:T(8,128)(2,1)}, bf16[4,384,512]{2,1,0:T(8,128)(2,1)}, u32[]{:S(2)}, u32[]{:S(2)}) collective-permute-start(bf16[4,384,512]{2,1,0:T(8,128)(2,1)} %get-tuple-element.389.up_ref.refs_5_), channel_id=1, source_target_pairs={{0,1},{1,0},{2,3},{3,2},{4,5},{5,4},{6,7},{7,6},{8,9},{9,8},{10,11... | collective-permute-start | bytes 4718600 | tf_op jit(solution)/shard_map/ppermute | solution.py:815
  195.9 188.0 %reduce-scatter.8.cloned.1.call-start = ((), (), s32[]{:S(2)}) async-start(), calls=%async_computation.11 | async-start | bytes 1966080 | tf_op jit(solution)/shard_map/reduce_scatter | solution.py:826
  232.7 44.3 %collective-permute-start.22 = (bf16[4,384,512]{2,1,0:T(8,128)(2,1)S(1)}, bf16[4,384,512]{2,1,0:T(8,128)(2,1)S(1)}, u32[]{:S(2)}, u32[]{:S(2)}) collective-permute-start(bf16[4,384,512]{2,1,0:T(8,128)(2,1)S(1)} %copy-done.4), channel_id=1, source_target_pairs={{0,4},{2,6},{4,0},{6,2},{1,5},{3,7},{5,1},{7,3},{8,12},{10,14},{12... | collective-permute-start | bytes 4718600 | tf_op jit(solution)/shard_map/ppermute | solution.py:812
  233.7 43.4 %collective-permute-start.23 = (bf16[4,384,512]{2,1,0:T(8,128)(2,1)}, bf16[4,384,512]{2,1,0:T(8,128)(2,1)}, u32[]{:S(2)}, u32[]{:S(2)}) collective-permute-start(bf16[4,384,512]{2,1,0:T(8,128)(2,1)} %get-tuple-element.407.down_ref.refs_4_), channel_id=1, source_target_pairs={{0,1},{1,0},{2,3},{3,2},{4,5},{5,4},{6,7},{7,6},{8,9},{9,8},{10,11... | collective-permute-start | bytes 4718600 | tf_op jit(solution)/shard_map/ppermute | solution.py:815
  347.6 73.9 %reduce-scatter.10.cloned.1.call-start = ((), (), s32[]{:S(2)}) async-start(), calls=%async_computation.12 | async-start | bytes 1966080 | tf_op jit(solution)/shard_map/reduce_scatter | solution.py:826
  383.9 82.9 %reduce-scatter.12.cloned.1.call-start = ((), (), s32[]{:S(2)}) async-start(), calls=%async_computation.13 | async-start | bytes 1966080 | tf_op jit(solution)/shard_map/reduce_scatter | solution.py:826
  384.0 36.3 %collective-permute-start.31 = (bf16[1536,512]{1,0:T(8,128)(2,1)}, bf16[1536,512]{1,0:T(8,128)(2,1)}, u32[]{:S(2)}, u32[]{:S(2)}) collective-permute-start(bf16[1536,512]{1,0:T(8,128)(2,1)} %get-tuple-element.447), channel_id=1, source_target_pairs={{0,1},{1,0},{2,3},{3,2},{4,5},{5,4},{6,7},{7,6},{8,9},{9,8},{10,11... | collective-permute-start | bytes 4718600 | tf_op jit(solution)/shard_map/ppermute | solution.py:815
  385.5 36.0 %collective-permute-start.32 = (bf16[1536,512]{1,0:T(8,128)(2,1)}, bf16[1536,512]{1,0:T(8,128)(2,1)}, u32[]{:S(2)}, u32[]{:S(2)}) collective-permute-start(bf16[1536,512]{1,0:T(8,128)(2,1)} %get-tuple-element.448), channel_id=1, source_target_pairs={{0,4},{2,6},{4,0},{6,2},{1,5},{3,7},{5,1},{7,3},{8,12},{10,14},{12... | collective-permute-start | bytes 4718600 | tf_op jit(solution)/shard_map/ppermute | solution.py:812
  425.2 88.2 %reduce-scatter.14.cloned.1.call-start = ((), (), s32[]{:S(2)}) async-start(), calls=%async_computation.14 | async-start | bytes 1966080 | tf_op jit(solution)/shard_map/reduce_scatter | solution.py:826
  425.9 40.8 %collective-permute-start.39 = (bf16[1536,512]{1,0:T(8,128)(2,1)}, bf16[1536,512]{1,0:T(8,128)(2,1)}, u32[]{:S(2)}, u32[]{:S(2)}) collective-permute-start(bf16[1536,512]{1,0:T(8,128)(2,1)} %get-tuple-element.463), channel_id=1, source_target_pairs={{0,4},{2,6},{4,0},{6,2},{1,5},{3,7},{5,1},{7,3},{8,12},{10,14},{12... | collective-permute-start | bytes 4718600 | tf_op jit(solution)/shard_map/ppermute | solution.py:812
  427.4 39.4 %collective-permute-start.40 = (bf16[512,1536]{1,0:T(8,128)(2,1)}, bf16[512,1536]{1,0:T(8,128)(2,1)}, u32[]{:S(2)}, u32[]{:S(2)}) collective-permute-start(bf16[512,1536]{1,0:T(8,128)(2,1)} %get-tuple-element.464), channel_id=1, source_target_pairs={{0,1},{1,0},{2,3},{3,2},{4,5},{5,4},{6,7},{7,6},{8,9},{9,8},{10,11... | collective-permute-start | bytes 4718600 | tf_op jit(solution)/shard_map/ppermute | solution.py:815
  470.5 111.5 %reduce-scatter.16.cloned.1.call-start = ((), (), s32[]{:S(2)}) async-start(), calls=%async_computation.15 | async-start | bytes 1966080 | tf_op jit(solution)/shard_map/reduce_scatter | solution.py:826
  474.8 38.5 %collective-permute-start.41 = (bf16[512,1536]{1,0:T(8,128)(2,1)}, bf16[512,1536]{1,0:T(8,128)(2,1)}, u32[]{:S(2)}, u32[]{:S(2)}) collective-permute-start(bf16[512,1536]{1,0:T(8,128)(2,1)} %add_convert_fusion.2), channel_id=1, source_target_pairs={{0,4},{2,6},{4,0},{6,2},{1,5},{3,7},{5,1},{7,3},{8,12},{10,14},{12... | collective-permute-start | bytes 4718600 | tf_op jit(solution)/shard_map/ppermute | solution.py:812
  516.6 103.4 %reduce-scatter.18.cloned.1.call-start = ((), (), s32[]{:S(2)}) async-start(), calls=%async_computation.16 | async-start | bytes 737280 | tf_op jit(solution)/shard_map/reduce_scatter | solution.py:826
  596.0 132.7 %reduce-scatter.20.cloned.1.call-start = ((), (), s32[]{:S(2)}) async-start(), calls=%async_computation.17 | async-start | bytes 1474560 | tf_op jit(solution)/shard_map/reduce_scatter | solution.py:826
  596.0 37.6 %collective-permute-start.53 = (bf16[1536,384]{1,0:T(8,128)(2,1)}, bf16[1536,384]{1,0:T(8,128)(2,1)}, u32[]{:S(2)}, u32[]{:S(2)}) collective-permute-start(bf16[1536,384]{1,0:T(8,128)(2,1)} %add_convert_fusion.5), channel_id=1, source_target_pairs={{0,4},{2,6},{4,0},{6,2},{1,5},{3,7},{5,1},{7,3},{8,12},{10,14},{12... | collective-permute-start | bytes 3538952 | tf_op jit(solution)/shard_map/ppermute | solution.py:812
  635.3 39.2 %collective-permute-start.61 = (bf16[256,1536]{1,0:T(8,128)(2,1)}, bf16[256,1536]{1,0:T(8,128)(2,1)S(1)}, u32[]{:S(2)}, u32[]{:S(2)}) collective-permute-start(bf16[256,1536]{1,0:T(8,128)(2,1)} %bitcast.115), channel_id=1, source_target_pairs={{0,6},{2,4},{4,2},{6,0},{1,7},{3,5},{5,3},{7,1},{8,14},{10,12},{12... | collective-permute-start | bytes 2359304 | tf_op jit(solution)/shard_map/ppermute | solution.py:814
  660.7 67.9 %collective-permute-start.66 = (bf16[176,1536]{1,0:T(8,128)(2,1)}, bf16[176,1536]{1,0:T(8,128)(2,1)}, u32[]{:S(2)}, u32[]{:S(2)}) collective-permute-start(bf16[176,1536]{1,0:T(8,128)(2,1)} %pad_maximum_fusion.9.refs_0_), channel_id=1, source_target_pairs={{0,2},{2,0},{4,6},{6,4},{1,3},{3,1},{5,7},{7,5},{8,10},{10,8},{12,... | collective-permute-start | bytes 1622024 | tf_op jit(solution)/shard_map/ppermute | solution.py:813
  738.2 48.9 %collective-permute-start.73 = (bf16[256,1536]{1,0:T(8,128)(2,1)}, bf16[256,1536]{1,0:T(8,128)(2,1)S(1)}, u32[]{:S(2)}, u32[]{:S(2)}) collective-permute-start(bf16[256,1536]{1,0:T(8,128)(2,1)} %bitcast.38), channel_id=1, source_target_pairs={{0,2},{2,0},{4,6},{6,4},{1,3},{3,1},{5,7},{7,5},{8,10},{10,8},{12,... | collective-permute-start | bytes 2359304 | tf_op jit(solution)/shard_map/ppermute | solution.py:813
  738.9 48.1 %collective-permute-start.74 = (bf16[256,1536]{1,0:T(8,128)(2,1)}, bf16[256,1536]{1,0:T(8,128)(2,1)S(1)}, u32[]{:S(2)}, u32[]{:S(2)}) collective-permute-start(bf16[256,1536]{1,0:T(8,128)(2,1)} %bitcast.39), channel_id=1, source_target_pairs={{0,4},{2,6},{4,0},{6,2},{1,5},{3,7},{5,1},{7,3},{8,12},{10,14},{12... | collective-permute-start | bytes 2359304 | tf_op jit(solution)/shard_map/ppermute | solution.py:812
  740.5 46.5 %collective-permute-start.75 = (bf16[256,1536]{1,0:T(8,128)(2,1)}, bf16[256,1536]{1,0:T(8,128)(2,1)S(1)}, u32[]{:S(2)}, u32[]{:S(2)}) collective-permute-start(bf16[256,1536]{1,0:T(8,128)(2,1)} %bitcast.40), channel_id=1, source_target_pairs={{0,6},{2,4},{4,2},{6,0},{1,7},{3,5},{5,3},{7,1},{8,14},{10,12},{12... | collective-permute-start | bytes 2359304 | tf_op jit(solution)/shard_map/ppermute | solution.py:814
  (108 other events, 1752.6 us)
Sparse Core Ops, SparseCore 0:
  17.3 31.6 all-gather.4
  57.4 44.8 all-gather.6
  104.8 64.4 all-gather.8
  196.0 63.9 all-gather.10
  347.7 36.1 reduce-scatter.7
  386.0 34.2 reduce-scatter.9
  425.3 33.5 reduce-scatter.11
  470.6 33.5 reduce-scatter.13
  516.7 33.6 reduce-scatter.15
  596.1 20.1 reduce-scatter.17
  687.8 28.2 reduce-scatter.19

commit v4 on v3

--- a/solution.py
+++ b/solution.py
@@ -911,9 +911,9 @@
     cot_received, gate_y = over_x(cot_sent), over_y(gate_own)
     mixed, q_aug = attend(queries, keys, values)
     cot_near = jnp.concatenate([cot_own, cot_received], axis=0)
-    up_own, down_own = second_own[:, :gain_width], second_own[:, gain_width:]
-    mixed, q_aug, cot_near, gate_y, up_own, down_own, second_last, gate_sent, *out_blocks = fence(
-        mixed, q_aug, cot_near, gate_y, up_own, down_own, second_last, gate_own, *out_blocks
+    up_own = second_own[:, :gain_width]
+    mixed, q_aug, cot_near, gate_y, up_own, second_own, second_last, gate_sent, *out_blocks = fence(
+        mixed, q_aug, cot_near, gate_y, up_own, second_own, second_last, gate_own, *out_blocks
     )
 
     second_last = over_z(second_last)
@@ -993,6 +993,7 @@
     )
     normed_two_far = [over_core(a) for a in normed_two_own]
     cot = span_join(places, cot_near, cot_far)
+    down_own = second_own[:, gain_width:]
     normed_two_own, normed_two_far, cot, gate_x, up_y, up_own, down_own = fence(
         normed_two_own, normed_two_far, cot, gate_x, up_y, up_own, down_own
     )
@@ -1166,7 +1167,7 @@
     qkv_sum = scatter(qkv_sum)
     row_last = over_y(row_x)
     received_in = [over_core(a) for a in sent_parts(in_lhs, in_rhs, in_dot, "in_other")]
-    row_far = [over_core(a) for a in (row_sum, row_y, row_x, row_last)]
+    row_far = [over_core(a) for a in (row_sum, row_y, row_x)]
 
     def in_body(left, right, others, outs):
         *received_refs, x_ref, grad_ref, gain_ref = others
@@ -1193,11 +1194,14 @@
     )
     sums = jnp.stack([gain_one_sums.sum(0), gain_two_sums.sum(0)])
     sums = sums + over_x(sums)
-    token_parts, sums, qkv_sum, row_far = fence(arrange(grad_rows), sums, qkv_sum, row_far)
+    sums = sums + over_core(sums)
+    token_parts, sums, qkv_sum, row_far, row_last = fence(arrange(grad_rows), sums, qkv_sum, row_far, row_last)
 
     qkv_x, qkv_y = over_x(qkv_sum), over_y(qkv_sum)
+    row_far.append(over_core(row_last))
+    sums = sums + over_y(sums)
     layer_out = from_slots(layer_parts)
-    token_parts, sums, qkv_x, qkv_y, layer_out = fence(token_parts, sums, qkv_x, qkv_y, layer_out)
+    token_parts, sums, qkv_x, qkv_y, layer_out, row_far = fence(token_parts, sums, qkv_x, qkv_y, layer_out, row_far)
 
     token_parts = to_slots(token_parts)
     qkv_last = over_y(qkv_x)
@@ -1206,8 +1210,6 @@
     grad_w_gate = unit_columns(where, both_pieces, n_shard, 0)
     grad_w_up = unit_columns(where, both_pieces, n_shard, 1)
     grad_w_down, grad_w_out = unit_rows(where, [row_sum, row_y, row_x, row_last] + row_far, unit_cols)
-    for step in (over_core, over_y):
-        sums = sums + step(sums)
     total = lax.dynamic_slice_in_dim(sums, shard * gain_width, gain_width, 1)
     for step in range(1, n_shard):
         to = lax.dynamic_slice_in_dim(sums, (shard + step) % n_shard * gain_width, gain_width, 1)

time: 806 us -> 796 us (0.988)
  waiting for transfers between devices: 98.1 us -> 84.7 us
    ppermute x21, waiting for transfers between devices: 48.9 us -> 40.2 us  [chip_layer(): over_x = lambda a: lax.ppermute(a, 'ctx', perm_x)]
  transfers between devices with their start and end apart: 97 -> 97, of which waited for: 27 -> 25; matrix products, arithmetic and copies ran while one was open for 8% -> 9% of each run, Pallas kernels for 63% -> 63%
where the time goes in v4:
time: 796 us; the launch traced here: 788 us
  Pallas kernels  505 us (63%)
  waiting for transfers between devices  84.7 us (11%)
  starting transfers between devices  60.7 us (8%)
  other arithmetic  50.6 us (6%)
  local copies, waits for them, and re-layouts  46.7 us (6%)
  blocking collectives  24.6 us (3%)
  between operations  15.6 us (2%)
    pallas_call x37, Pallas kernels, call(): pl.pallas_call(kernel, grid_spec=pltpu.PrefetchScalarGridSpec(num_scalar_...  505 us
    ppermute x21, waiting for transfers between devices, chip_layer(): over_x = lambda a: lax.ppermute(a, 'ctx', perm_x)  40.2 us
    ppermute x23, waiting for transfers between devices, chip_layer(): over_y = lambda a: lax.ppermute(a, 'batch', [(0, 1), (1, 0)])  26.1 us
    convert_element_type x9, other arithmetic, add(): functools.reduce(lambda a, b: a + b, [t.astype(f32) for t in terms])  25.2 us
    all_gather x1, blocking collectives, over_z(): gathered = lax.all_gather(piece, 'shard', axis=0, tiled=True)  24.6 us
    ppermute x23, starting transfers between devices, chip_layer(): over_y = lambda a: lax.ppermute(a, 'batch', [(0, 1), (1, 0)])  24.5 us
    ppermute x21, starting transfers between devices, chip_layer(): over_x = lambda a: lax.ppermute(a, 'ctx', perm_x)  22.8 us
  transfers between devices with their start and end apart: 97, of which 25 were waited for; matrix products, arithmetic and copies ran while one was open for 9% of the time, Pallas kernels for 63%

profile of v4, /device:TPU:0, one launch (start us, length us, event | category | flops | bytes accessed | tf_op | source)
XLA Modules:
  0.0 787.6 jit_solution(1401700670986426310)
XLA Ops:
  24.6 27.0 %collective-permute-done.1 = s32[512]{0:T(512)S(1)} collective-permute-done((s32[512]{0:T(512)S(1)}, s32[512]{0:T(512)S(1)}, u32[]{:S(2)}, u32[]{:S(2)}) %collective-permute-start.1) | collective-permute-done | bytes 2080 | tf_op jit(solution)/shard_map/ppermute | solution.py:812
  61.3 24.6 %all_gather.17 = bf16[768,384]{1,0:T(8,128)(2,1)} all-gather(bf16[192,384]{1,0:T(8,128)(2,1)S(1)} %pad_maximum_fusion.12), channel_id=1, replica_groups=mesh['shard'=4,'ctx'=4,'batch'=2] {'shard'}, dimensions={0}, use_global_device_ids=true | all-gather | bytes 737280 | tf_op jit(solution)/shard_map/all_gather | solution.py:819
  112.7 28.3 %front.1 = (bf16[2048,1536]{1,0:T(8,128)(2,1)}, bf16[2048,1536]{1,0:T(8,128)(2,1)}, bf16[1536,2048]{1,0:T(8,128)(2,1)}, bf16[2048,1024]{1,0:T(8,128)(2,1)}, bf16...) custom-call(s32[16]{0:T(128)} %get-tuple-element.685.near_ref, ...), custom_call_target="tpu_custom_call" | custom-call | flops 1000 | bytes 1000 | tf_op jit(solution)/shard_map/front/pallas_call | solution.py:74
  141.1 33.2 %attend.1 = (bf16[2048,1024]{1,0:T(8,128)(2,1)}, bf16[2048,1024]{1,0:T(8,128)(2,1)}) custom-call(bf16[2048,1024]{1,0:T(8,128)(2,1)} %get-tuple-element.352.q_ref, bf16[2048,512]{1,0:T(8,128)(2,1)} %get-tuple-element.353.k_ref, bf16[2048,512]{1,0:T(8,128)(2,1)} %get-tuple-element.354.v_ref), custom_call_target="tpu_custom_call" | custom-call | flops 1000 | bytes 1000 | tf_op jit(solution)/shard_map/attend/pallas_call | solution.py:74
  196.7 11.0 %out_own.1 = (f32[1024,1536]{1,0:T(8,128)}, bf16[1024,512]{1,0:T(8,128)(2,1)}, bf16[1024,512]{1,0:T(8,128)(2,1)}, bf16[1024,512]{1,0:T(8,128)(2,1)}) custom-call(s32[1]{0:T(128)S(6)} %mul.113.base_ref, bf16[2048,1024]{1,0:T(8,128)(2,1)} %get-tuple-element.364.refs_0_.mixed_ref.o_ref, bf16[1024,1536]{1,0:T(8,128)(2,1)} %out_rows.1.refs_1_.refs_6_, ...), custom_call_target="tpu_custom_call" | custom-call | flops 1000 | bytes 1000 | tf_op jit(solution)/shard_map/out_own/pallas_call | solution.py:74
  211.3 9.0 %span_join.1 = bf16[16,128,1536]{2,1,0:T(8,128)(2,1)} custom-call(s32[16]{0:T(128)} %get-tuple-element.685.near_ref, s32[16]{0:T(128)} %get-tuple-element.684.far_ref, s32[16]{0:T(128)} %copy-done.43, bf16[8,128,1536]{2,1,0:T(8,128)(2,1)} %bitcast.89, bf16[8,128,1536]{2,1,0:T(8,128)(2,1)} %bitcast.90, bf16[8,128,1536]{2,1,0:T(8,128)(2,1)} %bitcast.91, ...), custom_call_target="tpu_custom_call" | custom-call | flops 1000 | bytes 1000 | tf_op jit(solution)/shard_map/span_join/pallas_call | solution.py:74
  220.3 7.9 %collective-permute-done.20.gate_ref.refs_10_ = bf16[4,384,512]{2,1,0:T(8,128)(2,1)} collective-permute-done((bf16[4,384,512]{2,1,0:T(8,128)(2,1)}, bf16[4,384,512]{2,1,0:T(8,128)(2,1)}, u32[]{:S(2)}, u32[]{:S(2)}) %collective-permute-start.20) | collective-permute-done | bytes 1572896 | tf_op jit(solution)/shard_map/ppermute | solution.py:812
  233.8 9.5 %join_halves.1 = (bf16[2048,1536]{1,0:T(8,128)(2,1)}, bf16[1536,2048]{1,0:T(8,128)(2,1)}) custom-call(s32[1]{0:T(128)} %bitcast.3.core_ref, bf16[1024,512]{1,0:T(8,128)(2,1)} %get-tuple-element.380.refs_0_, bf16[1024,512]{1,0:T(8,128)(2,1)} %get-tuple-element.381.refs_1_, bf16[1024,512]{1,0:T(8,128)(2,1)} %get-tuple-element.382.refs_2_, ...), custom_call_target="tpu_custom_call" | custom-call | flops 1000 | bytes 1000 | tf_op jit(solution)/shard_map/join_halves/pallas_call | solution.py:74
  243.3 15.1 %hidden_units.4 = (bf16[2048,512]{1,0:T(8,128)(2,1)}, bf16[2048,1024]{1,0:T(8,128)(2,1)}) custom-call(bf16[2048,1536]{1,0:T(8,128)(2,1)} %get-tuple-element.424.n_ref, bf16[2048,1536]{1,0:T(8,128)(2,1)} %bitcast.70, bf16[4,384,512]{2,1,0:T(8,128)(2,1)} %bitcast.97, bf16[4,384,512]{2,1,0:T(8,128)(2,1)} %slice.125.up_ref.refs_5_, ...), custom_call_target="tpu_custom_call" | custom-call | flops 1000 | bytes 1000 | tf_op jit(solution)/shard_map/hidden_units/pallas_call | solution.py:74
  258.5 17.4 %feed_grads.4 = (bf16[1536,512]{1,0:T(8,128)(2,1)}, bf16[1536,512]{1,0:T(8,128)(2,1)}, bf16[512,1536]{1,0:T(8,128)(2,1)}) custom-call(bf16[1536,2048]{1,0:T(8,128)(2,1)} %get-tuple-element.390.n_ref, bf16[2048,1536]{1,0:T(8,128)(2,1)} %bitcast.71, bf16[2048,512]{1,0:T(8,128)(2,1)} %get-tuple-element.444.product_ref.refs_0_, ...), custom_call_target="tpu_custom_call" | custom-call | flops 1000 | bytes 1000 | tf_op jit(solution)/shard_map/feed_grads/pallas_call | solution.py:74
  277.9 15.2 %hidden_units.5 = (bf16[2048,512]{1,0:T(8,128)(2,1)}, bf16[2048,1024]{1,0:T(8,128)(2,1)}) custom-call(bf16[2048,1536]{1,0:T(8,128)(2,1)} %get-tuple-element.424.n_ref, bf16[2048,1536]{1,0:T(8,128)(2,1)} %bitcast.72, bf16[4,384,512]{2,1,0:T(8,128)(2,1)} %collective-permute-done.9.gate_ref.refs_6_, ...), custom_call_target="tpu_custom_call" | custom-call | flops 1000 | bytes 1000 | tf_op jit(solution)/shard_map/hidden_units/pallas_call | solution.py:74
  293.0 17.4 %feed_grads.5 = (bf16[1536,512]{1,0:T(8,128)(2,1)}, bf16[1536,512]{1,0:T(8,128)(2,1)}, bf16[512,1536]{1,0:T(8,128)(2,1)}) custom-call(bf16[1536,2048]{1,0:T(8,128)(2,1)} %get-tuple-element.390.n_ref, bf16[2048,1536]{1,0:T(8,128)(2,1)} %bitcast.73, bf16[2048,512]{1,0:T(8,128)(2,1)} %get-tuple-element.445.product_ref.refs_1_, ...), custom_call_target="tpu_custom_call" | custom-call | flops 1000 | bytes 1000 | tf_op jit(solution)/shard_map/feed_grads/pallas_call | solution.py:74
  313.3 15.3 %hidden_units.6 = (bf16[2048,512]{1,0:T(8,128)(2,1)}, bf16[2048,1024]{1,0:T(8,128)(2,1)}) custom-call(bf16[2048,1536]{1,0:T(8,128)(2,1)} %get-tuple-element.424.n_ref, bf16[2048,1536]{1,0:T(8,128)(2,1)} %bitcast.74, bf16[4,384,512]{2,1,0:T(8,128)(2,1)} %copy-done.6, bf16[4,768,512]{2,1,0:T(8,128)(2,1)} %bitcast.79, bf16[4,768,512]{2,1,0:T(8,128)(2,1)} %bitcast.80), custom_call_target="tpu_custom_call" | custom-call | flops 1000 | bytes 1000 | tf_op jit(solution)/shard_map/hidden_units/pallas_call | solution.py:74
  328.6 17.5 %feed_grads.6 = (bf16[1536,512]{1,0:T(8,128)(2,1)}, bf16[1536,512]{1,0:T(8,128)(2,1)}, bf16[512,1536]{1,0:T(8,128)(2,1)}) custom-call(bf16[1536,2048]{1,0:T(8,128)(2,1)} %get-tuple-element.390.n_ref, bf16[2048,1536]{1,0:T(8,128)(2,1)} %bitcast.75, bf16[2048,512]{1,0:T(8,128)(2,1)} %get-tuple-element.446.product_ref.refs_2_, ...), custom_call_target="tpu_custom_call" | custom-call | flops 1000 | bytes 1000 | tf_op jit(solution)/shard_map/feed_grads/pallas_call | solution.py:74
  348.3 15.1 %hidden_units.7 = (bf16[2048,512]{1,0:T(8,128)(2,1)}, bf16[2048,1024]{1,0:T(8,128)(2,1)}) custom-call(bf16[2048,1536]{1,0:T(8,128)(2,1)} %get-tuple-element.424.n_ref, bf16[2048,1536]{1,0:T(8,128)(2,1)} %bitcast.76, bf16[4,384,512]{2,1,0:T(8,128)(2,1)} %collective-permute-done.20.gate_ref.refs_10_, bf16[4,384,512]{2,1,0:T(8,128)(2,1)} %copy-done.5, ...), custom_call_target="tpu_custom_call" | custom-call | flops 1000 | bytes 1000 | tf_op jit(solution)/shard_map/hidden_units/pallas_call | solution.py:74
  363.4 17.5 %feed_grads.7 = (bf16[1536,512]{1,0:T(8,128)(2,1)}, bf16[1536,512]{1,0:T(8,128)(2,1)}, bf16[512,1536]{1,0:T(8,128)(2,1)}) custom-call(bf16[1536,2048]{1,0:T(8,128)(2,1)} %get-tuple-element.390.n_ref, bf16[2048,1536]{1,0:T(8,128)(2,1)} %bitcast.77, bf16[2048,512]{1,0:T(8,128)(2,1)} %get-tuple-element.447.product_ref.refs_3_, ...), custom_call_target="tpu_custom_call" | custom-call | flops 1000 | bytes 1000 | tf_op jit(solution)/shard_map/feed_grads/pallas_call | solution.py:74
  385.9 20.9 %back_other.1 = (bf16[1024,512]{1,0:T(8,128)(2,1)}, bf16[1024,512]{1,0:T(8,128)(2,1)}, bf16[1024,512]{1,0:T(8,128)(2,1)}) custom-call(s32[1]{0:T(128)S(6)} %mul.134.base_ref, bf16[2048,1024]{1,0:T(8,128)(2,1)} %get-tuple-element.437.both_ref.refs_0_, bf16[2048,1024]{1,0:T(8,128)(2,1)} %get-tuple-element.438.both_ref.refs_1_, ...), custom_call_target="tpu_custom_call" | custom-call | flops 1000 | bytes 1000 | tf_op jit(solution)/shard_map/back_other/pallas_call | solution.py:74
  407.4 11.3 %down_other.1 = (bf16[1024,512]{1,0:T(8,128)(2,1)}, bf16[1024,512]{1,0:T(8,128)(2,1)}, bf16[1024,512]{1,0:T(8,128)(2,1)}) custom-call(s32[1]{0:T(128)S(6)} %mul.134.base_ref, bf16[2048,512]{1,0:T(8,128)(2,1)} %get-tuple-element.444.product_ref.refs_0_, bf16[2048,512]{1,0:T(8,128)(2,1)} %get-tuple-element.445.product_ref.refs_1_, ...), custom_call_target="tpu_custom_call" | custom-call | flops 1000 | bytes 1000 | tf_op jit(solution)/shard_map/down_other/pallas_call | solution.py:74
  426.9 24.5 %back_own.1 = (f32[1024,1536]{1,0:T(8,128)}, f32[8,1536]{1,0:T(8,128)}, bf16[1024,512]{1,0:T(8,128)(2,1)}, bf16[1024,512]{1,0:T(8,128)(2,1)}, bf16[1024,512]{1,0:T(8,128)(2,1)}) custom-call(s32[1]{0:T(128)S(6)} %mul.113.base_ref, bf16[2048,1024]{1,0:T(8,128)(2,1)} %get-tuple-element.437.both_ref.refs_0_, ...), custom_call_target="tpu_custom_call" | custom-call | flops 1000 | bytes 1000 | tf_op jit(solution)/shard_map/back_own/pallas_call | solution.py:74
  453.0 12.7 %down_own.1 = bf16[1024,1536]{1,0:T(8,128)(2,1)} custom-call(s32[1]{0:T(128)S(6)} %mul.113.base_ref, bf16[2048,512]{1,0:T(8,128)(2,1)} %get-tuple-element.444.product_ref.refs_0_, bf16[2048,512]{1,0:T(8,128)(2,1)} %get-tuple-element.445.product_ref.refs_1_, bf16[2048,512]{1,0:T(8,128)(2,1)} %get-tuple-element.446.product_ref.refs_2_, ...), custom_call_target="tpu_custom_call" | custom-call | flops 1000 | bytes 1000 | tf_op jit(solution)/shard_map/down_own/pallas_call | solution.py:74
  479.5 12.3 %mixed_back.1 = (bf16[2048,1536]{1,0:T(8,128)(2,1)}, bf16[2048,1024]{1,0:T(8,128)(2,1)}) custom-call(s32[1]{0:T(128)} %bitcast.3.core_ref, bf16[1024,512]{1,0:T(8,128)(2,1)} %get-tuple-element.474.refs_0_, bf16[1024,512]{1,0:T(8,128)(2,1)} %get-tuple-element.475.refs_1_, bf16[1024,512]{1,0:T(8,128)(2,1)} %get-tuple-element.476.refs_2_, ...), custom_call_target="tpu_custom_call" | custom-call | flops 1000 | bytes 1000 | tf_op jit(solution)/shard_map/mixed_back/pallas_call | solution.py:74
  491.7 12.1 %out_grads.1 = (bf16[4,48,1536]{2,1,0:T(8,128)(2,1)}, bf16[4,48,1536]{2,1,0:T(8,128)(2,1)}, bf16[4,48,1536]{2,1,0:T(8,128)(2,1)}, bf16[4,48,1536]{2,1,0:T(8,128)(2,1)}) custom-call(s32[1]{0:T(128)} %bitcast.21.place_ref, bf16[2048,1024]{1,0:T(8,128)(2,1)} %get-tuple-element.364.refs_0_.mixed_ref.o_ref, bf16[2048,1536]{1,0:T(8,128)(2,1)} %get-tuple-element.481.grad_ref), custom_call_target="tpu_custom_call" | custom-call | flops 1000 | bytes 1000 | tf_op jit(solution)/shard_map/out_grads/pallas_call | solution.py:74
  519.8 20.6 %attend_back.4 = (bf16[2048,256]{1,0:T(8,128)(2,1)}, bf16[2048,128]{1,0:T(8,128)(2,1)}, bf16[2048,128]{1,0:T(8,128)(2,1)}) custom-call(bf16[2048,1024]{1,0:T(8,128)(2,1)} %get-tuple-element.550.q_ref, bf16[2048,512]{1,0:T(8,128)(2,1)} %get-tuple-element.353.k_ref, bf16[2048,512]{1,0:T(8,128)(2,1)} %get-tuple-element.354.v_ref, ...), custom_call_target="tpu_custom_call" | custom-call | flops 1000 | bytes 1000 | tf_op jit(solution)/shard_map/attend_back/pallas_call | solution.py:74
  542.5 8.1 %qkv_grad.4 = bf16[1536,384]{1,0:T(8,128)(2,1)} custom-call(bf16[1536,2048]{1,0:T(8,128)(2,1)} %get-tuple-element.351.n_ref, bf16[2048,256]{1,0:T(8,128)(2,1)} %get-tuple-element.500.q_ref.refs_9_, bf16[2048,128]{1,0:T(8,128)(2,1)} %get-tuple-element.501.k_ref.refs_10_, bf16[2048,128]{1,0:T(8,128)(2,1)} %get-tuple-element.502.v_ref.refs_11_, ...), custom_call_target="tpu_custom_call" | custom-call | flops 1000 | bytes 1000 | tf_op jit(solution)/shard_map/qkv_grad/pallas_call | solution.py:74
  555.3 20.8 %attend_back.5 = (bf16[2048,256]{1,0:T(8,128)(2,1)}, bf16[2048,128]{1,0:T(8,128)(2,1)}, bf16[2048,128]{1,0:T(8,128)(2,1)}) custom-call(bf16[2048,1024]{1,0:T(8,128)(2,1)} %get-tuple-element.550.q_ref, bf16[2048,512]{1,0:T(8,128)(2,1)} %get-tuple-element.353.k_ref, bf16[2048,512]{1,0:T(8,128)(2,1)} %get-tuple-element.354.v_ref, ...), custom_call_target="tpu_custom_call" | custom-call | flops 1000 | bytes 1000 | tf_op jit(solution)/shard_map/attend_back/pallas_call | solution.py:74
  583.2 7.8 qkv_grad.5
  598.2 20.6 %attend_back.6 = (bf16[2048,256]{1,0:T(8,128)(2,1)}, bf16[2048,128]{1,0:T(8,128)(2,1)}, bf16[2048,128]{1,0:T(8,128)(2,1)}) custom-call(bf16[2048,1024]{1,0:T(8,128)(2,1)} %get-tuple-element.550.q_ref, bf16[2048,512]{1,0:T(8,128)(2,1)} %get-tuple-element.353.k_ref, bf16[2048,512]{1,0:T(8,128)(2,1)} %get-tuple-element.354.v_ref, ...), custom_call_target="tpu_custom_call" | custom-call | flops 1000 | bytes 1000 | tf_op jit(solution)/shard_map/attend_back/pallas_call | solution.py:74
  619.0 8.4 %qkv_grad.6 = bf16[1536,384]{1,0:T(8,128)(2,1)} custom-call(bf16[1536,2048]{1,0:T(8,128)(2,1)} %get-tuple-element.351.n_ref, bf16[2048,256]{1,0:T(8,128)(2,1)} %get-tuple-element.539.q_ref.refs_3_, bf16[2048,128]{1,0:T(8,128)(2,1)} %get-tuple-element.540.k_ref.refs_4_, bf16[2048,128]{1,0:T(8,128)(2,1)} %get-tuple-element.541.v_ref.refs_5_, ...), custom_call_target="tpu_custom_call" | custom-call | flops 1000 | bytes 1000 | tf_op jit(solution)/shard_map/qkv_grad/pallas_call | solution.py:74
  635.5 20.6 %attend_back.7 = (bf16[2048,256]{1,0:T(8,128)(2,1)}, bf16[2048,128]{1,0:T(8,128)(2,1)}, bf16[2048,128]{1,0:T(8,128)(2,1)}) custom-call(bf16[2048,1024]{1,0:T(8,128)(2,1)} %get-tuple-element.550.q_ref, bf16[2048,512]{1,0:T(8,128)(2,1)} %get-tuple-element.353.k_ref, bf16[2048,512]{1,0:T(8,128)(2,1)} %get-tuple-element.354.v_ref, ...), custom_call_target="tpu_custom_call" | custom-call | flops 1000 | bytes 1000 | tf_op jit(solution)/shard_map/attend_back/pallas_call | solution.py:74
  657.4 8.1 %qkv_grad.7 = bf16[1536,384]{1,0:T(8,128)(2,1)} custom-call(bf16[1536,2048]{1,0:T(8,128)(2,1)} %get-tuple-element.351.n_ref, bf16[2048,256]{1,0:T(8,128)(2,1)} %get-tuple-element.568.q_ref.refs_0_, bf16[2048,128]{1,0:T(8,128)(2,1)} %get-tuple-element.569.k_ref.refs_1_, bf16[2048,128]{1,0:T(8,128)(2,1)} %get-tuple-element.570.v_ref.refs_2_, ...), custom_call_target="tpu_custom_call" | custom-call | flops 1000 | bytes 1000 | tf_op jit(solution)/shard_map/qkv_grad/pallas_call | solution.py:74
  671.5 11.7 %in_other.1 = (bf16[1024,512]{1,0:T(8,128)(2,1)}, bf16[1024,512]{1,0:T(8,128)(2,1)}, bf16[1024,512]{1,0:T(8,128)(2,1)}) custom-call(s32[1]{0:T(128)S(6)} %mul.134.base_ref, bf16[2048,256]{1,0:T(8,128)(2,1)} %get-tuple-element.568.q_ref.refs_0_, bf16[2048,128]{1,0:T(8,128)(2,1)} %get-tuple-element.569.k_ref.refs_1_, ...), custom_call_target="tpu_custom_call" | custom-call | flops 1000 | bytes 1000 | tf_op jit(solution)/shard_map/in_other/pallas_call | solution.py:74
  690.2 15.3 %in_own.1 = (bf16[1024,1536]{1,0:T(8,128)(2,1)}, f32[8,1536]{1,0:T(8,128)}) custom-call(s32[1]{0:T(128)S(6)} %mul.113.base_ref, bf16[2048,256]{1,0:T(8,128)(2,1)} %get-tuple-element.568.q_ref.refs_0_, bf16[2048,128]{1,0:T(8,128)(2,1)} %get-tuple-element.569.k_ref.refs_1_, bf16[2048,128]{1,0:T(8,128)(2,1)} %get-tuple-element.570.v_ref.refs_2_, ...), custom_call_target="tpu_custom_call" | custom-call | flops 1000 | bytes 1000 | tf_op jit(solution)/shard_map/in_own/pallas_call | solution.py:74
  (404 shorter events, 254.9 us)
Async XLA Ops:
  7.2 46.6 %all-gather.5.cloned.1.call-start = ((), (), s32[]{:S(2)}) async-start(), calls=%async_computation.7 | async-start | bytes 1536000 | tf_op jit(solution)/shard_map/all_gather | solution.py:819
  14.2 37.5 %collective-permute-start = (bf16[512,1536]{1,0:T(8,128)(2,1)S(1)}, bf16[512,1536]{1,0:T(8,128)(2,1)}, u32[]{:S(2)}, u32[]{:S(2)}) collective-permute-start(bf16[512,1536]{1,0:T(8,128)(2,1)S(1)} %get-tuple-element.323), channel_id=1, source_target_pairs={{0,4},{2,6},{4,0},{6,2},{1,5},{3,7},{5,1},{7,3},{8,12},{10,14},{12... | collective-permute-start | bytes 4718600 | tf_op jit(solution)/shard_map/ppermute | solution.py:812
  17.2 85.1 %all-gather.7.cloned.1.call-start = ((), (), s32[]{:S(2)}) async-start(), calls=%async_computation.8 | async-start | bytes 1966080 | tf_op jit(solution)/shard_map/all_gather | solution.py:819
  57.3 119.1 %all-gather.9.cloned.1.call-start = ((), (), s32[]{:S(2)}) async-start(), calls=%async_computation.9 | async-start | bytes 3932160 | tf_op jit(solution)/shard_map/all_gather | solution.py:819
  104.7 205.8 %all-gather.11.cloned.1.call-start = ((), (), s32[]{:S(2)}) async-start(), calls=%async_computation.10 | async-start | bytes 3932160 | tf_op jit(solution)/shard_map/all_gather | solution.py:819
  104.9 69.3 %collective-permute-start.8 = (bf16[512,1536]{1,0:T(8,128)(2,1)S(1)}, bf16[512,1536]{1,0:T(8,128)(2,1)}, u32[]{:S(2)}, u32[]{:S(2)}) collective-permute-start(bf16[512,1536]{1,0:T(8,128)(2,1)S(1)} %copy-done.18), channel_id=1, source_target_pairs={{0,4},{2,6},{4,0},{6,2},{1,5},{3,7},{5,1},{7,3},{8,12},{10,14},{12... | collective-permute-start | bytes 4718600 | tf_op jit(solution)/shard_map/ppermute | solution.py:812
  106.0 74.1 %collective-permute-start.9 = (bf16[4,384,512]{2,1,0:T(8,128)(2,1)}, bf16[4,384,512]{2,1,0:T(8,128)(2,1)}, u32[]{:S(2)}, u32[]{:S(2)}) collective-permute-start(bf16[4,384,512]{2,1,0:T(8,128)(2,1)} %bitcast.95), channel_id=1, source_target_pairs={{0,1},{1,0},{2,3},{3,2},{4,5},{5,4},{6,7},{7,6},{8,9},{9,8},{10,11... | collective-permute-start | bytes 4718600 | tf_op jit(solution)/shard_map/ppermute | solution.py:815
  107.2 72.9 %collective-permute-start.10 = (bf16[4,192,384]{2,1,0:T(8,128)(2,1)}, bf16[4,192,384]{2,1,0:T(8,128)(2,1)}, u32[]{:S(2)}, u32[]{:S(2)}) collective-permute-start(bf16[4,192,384]{2,1,0:T(8,128)(2,1)} %bitcast.18.refs_0_), channel_id=1, source_target_pairs={{0,1},{1,0},{2,3},{3,2},{4,5},{5,4},{6,7},{7,6},{8,9},{9,8},{10,11... | collective-permute-start | bytes 1769480 | tf_op jit(solution)/shard_map/ppermute | solution.py:815
  108.1 72.1 %collective-permute-start.11 = (bf16[4,192,384]{2,1,0:T(8,128)(2,1)}, bf16[4,192,384]{2,1,0:T(8,128)(2,1)}, u32[]{:S(2)}, u32[]{:S(2)}) collective-permute-start(bf16[4,192,384]{2,1,0:T(8,128)(2,1)} %bitcast.18.refs_0_), channel_id=1, source_target_pairs={{0,4},{2,6},{4,0},{6,2},{1,5},{3,7},{5,1},{7,3},{8,12},{10,14},{12... | collective-permute-start | bytes 1769480 | tf_op jit(solution)/shard_map/ppermute | solution.py:812
  109.0 71.1 %collective-permute-start.12 = (bf16[4,192,384]{2,1,0:T(8,128)(2,1)}, bf16[4,192,384]{2,1,0:T(8,128)(2,1)}, u32[]{:S(2)}, u32[]{:S(2)}) collective-permute-start(bf16[4,192,384]{2,1,0:T(8,128)(2,1)} %bitcast.18.refs_0_), channel_id=1, source_target_pairs={{0,5},{1,4},{2,7},{3,6},{4,1},{5,0},{6,3},{7,2},{8,13},{9,12},{10,... | collective-permute-start | bytes 1769480 | tf_op jit(solution)/shard_map/ppermute | solution.py:816
  191.6 36.6 %collective-permute-start.20 = (bf16[4,384,512]{2,1,0:T(8,128)(2,1)}, bf16[4,384,512]{2,1,0:T(8,128)(2,1)}, u32[]{:S(2)}, u32[]{:S(2)}) collective-permute-start(bf16[4,384,512]{2,1,0:T(8,128)(2,1)} %bitcast.96), channel_id=1, source_target_pairs={{0,4},{2,6},{4,0},{6,2},{1,5},{3,7},{5,1},{7,3},{8,12},{10,14},{12... | collective-permute-start | bytes 4718600 | tf_op jit(solution)/shard_map/ppermute | solution.py:812
  193.7 37.0 %collective-permute-start.21 = (bf16[4,384,512]{2,1,0:T(8,128)(2,1)}, bf16[4,384,512]{2,1,0:T(8,128)(2,1)}, u32[]{:S(2)}, u32[]{:S(2)}) collective-permute-start(bf16[4,384,512]{2,1,0:T(8,128)(2,1)} %slice.125.up_ref.refs_5_), channel_id=1, source_target_pairs={{0,1},{1,0},{2,3},{3,2},{4,5},{5,4},{6,7},{7,6},{8,9},{9,8},{10,11... | collective-permute-start | bytes 4718600 | tf_op jit(solution)/shard_map/ppermute | solution.py:815
  194.8 188.1 %reduce-scatter.8.cloned.1.call-start = ((), (), s32[]{:S(2)}) async-start(), calls=%async_computation.11 | async-start | bytes 1966080 | tf_op jit(solution)/shard_map/reduce_scatter | solution.py:826
  231.7 44.2 %collective-permute-start.22 = (bf16[4,384,512]{2,1,0:T(8,128)(2,1)S(1)}, bf16[4,384,512]{2,1,0:T(8,128)(2,1)S(1)}, u32[]{:S(2)}, u32[]{:S(2)}) collective-permute-start(bf16[4,384,512]{2,1,0:T(8,128)(2,1)S(1)} %copy-done.4), channel_id=1, source_target_pairs={{0,4},{2,6},{4,0},{6,2},{1,5},{3,7},{5,1},{7,3},{8,12},{10,14},{12... | collective-permute-start | bytes 4718600 | tf_op jit(solution)/shard_map/ppermute | solution.py:812
  232.6 43.3 %collective-permute-start.23 = (bf16[4,384,512]{2,1,0:T(8,128)(2,1)}, bf16[4,384,512]{2,1,0:T(8,128)(2,1)}, u32[]{:S(2)}, u32[]{:S(2)}) collective-permute-start(bf16[4,384,512]{2,1,0:T(8,128)(2,1)} %slice.110.down_ref.refs_4_), channel_id=1, source_target_pairs={{0,1},{1,0},{2,3},{3,2},{4,5},{5,4},{6,7},{7,6},{8,9},{9,8},{10,11... | collective-permute-start | bytes 4718600 | tf_op jit(solution)/shard_map/ppermute | solution.py:815
  275.9 35.5 %collective-permute-start.24 = (bf16[4,384,512]{2,1,0:T(8,128)(2,1)}, bf16[4,384,512]{2,1,0:T(8,128)(2,1)S(1)}, u32[]{:S(2)}, u32[]{:S(2)}) collective-permute-start(bf16[4,384,512]{2,1,0:T(8,128)(2,1)} %collective-permute-done.20.gate_ref.refs_10_), channel_id=1, source_target_pairs={{0,1},{1,0},{2,3},{3,2},{4,5},{5,4},{6,7},{7,6},{8,9},{9,8},{10,11... | collective-permute-start | bytes 4718600 | tf_op jit(solution)/shard_map/ppermute | solution.py:815
  346.4 74.1 %reduce-scatter.10.cloned.1.call-start = ((), (), s32[]{:S(2)}) async-start(), calls=%async_computation.12 | async-start | bytes 1966080 | tf_op jit(solution)/shard_map/reduce_scatter | solution.py:826
  382.9 82.9 %reduce-scatter.12.cloned.1.call-start = ((), (), s32[]{:S(2)}) async-start(), calls=%async_computation.13 | async-start | bytes 1966080 | tf_op jit(solution)/shard_map/reduce_scatter | solution.py:826
  382.9 36.3 %collective-permute-start.31 = (bf16[1536,512]{1,0:T(8,128)(2,1)}, bf16[1536,512]{1,0:T(8,128)(2,1)}, u32[]{:S(2)}, u32[]{:S(2)}) collective-permute-start(bf16[1536,512]{1,0:T(8,128)(2,1)} %get-tuple-element.451), channel_id=1, source_target_pairs={{0,1},{1,0},{2,3},{3,2},{4,5},{5,4},{6,7},{7,6},{8,9},{9,8},{10,11... | collective-permute-start | bytes 4718600 | tf_op jit(solution)/shard_map/ppermute | solution.py:815
  384.4 36.0 %collective-permute-start.32 = (bf16[1536,512]{1,0:T(8,128)(2,1)}, bf16[1536,512]{1,0:T(8,128)(2,1)}, u32[]{:S(2)}, u32[]{:S(2)}) collective-permute-start(bf16[1536,512]{1,0:T(8,128)(2,1)} %get-tuple-element.452), channel_id=1, source_target_pairs={{0,4},{2,6},{4,0},{6,2},{1,5},{3,7},{5,1},{7,3},{8,12},{10,14},{12... | collective-permute-start | bytes 4718600 | tf_op jit(solution)/shard_map/ppermute | solution.py:812
  424.2 88.2 %reduce-scatter.14.cloned.1.call-start = ((), (), s32[]{:S(2)}) async-start(), calls=%async_computation.14 | async-start | bytes 1966080 | tf_op jit(solution)/shard_map/reduce_scatter | solution.py:826
  424.9 40.8 %collective-permute-start.39 = (bf16[1536,512]{1,0:T(8,128)(2,1)}, bf16[1536,512]{1,0:T(8,128)(2,1)}, u32[]{:S(2)}, u32[]{:S(2)}) collective-permute-start(bf16[1536,512]{1,0:T(8,128)(2,1)} %get-tuple-element.467), channel_id=1, source_target_pairs={{0,4},{2,6},{4,0},{6,2},{1,5},{3,7},{5,1},{7,3},{8,12},{10,14},{12... | collective-permute-start | bytes 4718600 | tf_op jit(solution)/shard_map/ppermute | solution.py:812
  426.3 39.4 %collective-permute-start.40 = (bf16[512,1536]{1,0:T(8,128)(2,1)}, bf16[512,1536]{1,0:T(8,128)(2,1)}, u32[]{:S(2)}, u32[]{:S(2)}) collective-permute-start(bf16[512,1536]{1,0:T(8,128)(2,1)} %get-tuple-element.468), channel_id=1, source_target_pairs={{0,1},{1,0},{2,3},{3,2},{4,5},{5,4},{6,7},{7,6},{8,9},{9,8},{10,11... | collective-permute-start | bytes 4718600 | tf_op jit(solution)/shard_map/ppermute | solution.py:815
  469.5 111.5 %reduce-scatter.16.cloned.1.call-start = ((), (), s32[]{:S(2)}) async-start(), calls=%async_computation.15 | async-start | bytes 1966080 | tf_op jit(solution)/shard_map/reduce_scatter | solution.py:826
  473.8 38.6 %collective-permute-start.41 = (bf16[512,1536]{1,0:T(8,128)(2,1)}, bf16[512,1536]{1,0:T(8,128)(2,1)}, u32[]{:S(2)}, u32[]{:S(2)}) collective-permute-start(bf16[512,1536]{1,0:T(8,128)(2,1)} %add_convert_fusion.2), channel_id=1, source_target_pairs={{0,4},{2,6},{4,0},{6,2},{1,5},{3,7},{5,1},{7,3},{8,12},{10,14},{12... | collective-permute-start | bytes 4718600 | tf_op jit(solution)/shard_map/ppermute | solution.py:812
  515.6 103.3 %reduce-scatter.18.cloned.1.call-start = ((), (), s32[]{:S(2)}) async-start(), calls=%async_computation.16 | async-start | bytes 737280 | tf_op jit(solution)/shard_map/reduce_scatter | solution.py:826
  594.9 122.8 %reduce-scatter.20.cloned.1.call-start = ((), (), s32[]{:S(2)}) async-start(), calls=%async_computation.17 | async-start | bytes 1474560 | tf_op jit(solution)/shard_map/reduce_scatter | solution.py:826
  595.0 37.6 %collective-permute-start.53 = (bf16[1536,384]{1,0:T(8,128)(2,1)}, bf16[1536,384]{1,0:T(8,128)(2,1)}, u32[]{:S(2)}, u32[]{:S(2)}) collective-permute-start(bf16[1536,384]{1,0:T(8,128)(2,1)} %add_convert_fusion.5), channel_id=1, source_target_pairs={{0,4},{2,6},{4,0},{6,2},{1,5},{3,7},{5,1},{7,3},{8,12},{10,14},{12... | collective-permute-start | bytes 3538952 | tf_op jit(solution)/shard_map/ppermute | solution.py:812
  634.3 37.2 %collective-permute-start.61 = (bf16[256,1536]{1,0:T(8,128)(2,1)}, bf16[256,1536]{1,0:T(8,128)(2,1)S(1)}, u32[]{:S(2)}, u32[]{:S(2)}) collective-permute-start(bf16[256,1536]{1,0:T(8,128)(2,1)} %bitcast.117), channel_id=1, source_target_pairs={{0,6},{2,4},{4,2},{6,0},{1,7},{3,5},{5,3},{7,1},{8,14},{10,12},{12... | collective-permute-start | bytes 2359304 | tf_op jit(solution)/shard_map/ppermute | solution.py:814
  730.4 45.6 %collective-permute-start.75 = (bf16[256,1536]{1,0:T(8,128)(2,1)}, bf16[256,1536]{1,0:T(8,128)(2,1)S(1)}, u32[]{:S(2)}, u32[]{:S(2)}) collective-permute-start(bf16[256,1536]{1,0:T(8,128)(2,1)} %bitcast.38), channel_id=1, source_target_pairs={{0,2},{2,0},{4,6},{6,4},{1,3},{3,1},{5,7},{7,5},{8,10},{10,8},{12,... | collective-permute-start | bytes 2359304 | tf_op jit(solution)/shard_map/ppermute | solution.py:813
  731.2 44.7 %collective-permute-start.76 = (bf16[256,1536]{1,0:T(8,128)(2,1)}, bf16[256,1536]{1,0:T(8,128)(2,1)S(1)}, u32[]{:S(2)}, u32[]{:S(2)}) collective-permute-start(bf16[256,1536]{1,0:T(8,128)(2,1)} %bitcast.39), channel_id=1, source_target_pairs={{0,4},{2,6},{4,0},{6,2},{1,5},{3,7},{5,1},{7,3},{8,12},{10,14},{12... | collective-permute-start | bytes 2359304 | tf_op jit(solution)/shard_map/ppermute | solution.py:812
  732.6 43.3 %collective-permute-start.77 = (bf16[256,1536]{1,0:T(8,128)(2,1)S(1)}, bf16[256,1536]{1,0:T(8,128)(2,1)}, u32[]{:S(2)}, u32[]{:S(2)}) collective-permute-start(bf16[256,1536]{1,0:T(8,128)(2,1)S(1)} %bitcast.116), channel_id=1, source_target_pairs={{0,6},{2,4},{4,2},{6,0},{1,7},{3,5},{5,3},{7,1},{8,14},{10,12},{12... | collective-permute-start | bytes 2359304 | tf_op jit(solution)/shard_map/ppermute | solution.py:814
  (113 other events, 1738.7 us)
Sparse Core Ops, SparseCore 0:
  17.3 31.6 all-gather.4
  57.4 44.8 all-gather.6
  104.8 64.3 all-gather.8
  194.9 63.9 all-gather.10
  346.5 36.3 reduce-scatter.7
  385.0 34.2 reduce-scatter.9
  424.3 33.5 reduce-scatter.11
  469.6 33.5 reduce-scatter.13
  515.7 33.5 reduce-scatter.15
  595.0 20.1 reduce-scatter.17
  684.3 28.2 reduce-scatter.19

commit v5 on v4

--- a/solution.py
+++ b/solution.py
@@ -1210,14 +1210,14 @@
     grad_w_gate = unit_columns(where, both_pieces, n_shard, 0)
     grad_w_up = unit_columns(where, both_pieces, n_shard, 1)
     grad_w_down, grad_w_out = unit_rows(where, [row_sum, row_y, row_x, row_last] + row_far, unit_cols)
+    head_grads = head_columns(where, both_cores([qkv_sum, qkv_y, qkv_x, qkv_last]))
+    token_parts, grad_w_gate, grad_w_up, grad_w_down, grad_w_out, head_grads, sums = fence(
+        token_parts, grad_w_gate, grad_w_up, grad_w_down, grad_w_out, head_grads, sums
+    )
     total = lax.dynamic_slice_in_dim(sums, shard * gain_width, gain_width, 1)
     for step in range(1, n_shard):
         to = lax.dynamic_slice_in_dim(sums, (shard + step) % n_shard * gain_width, gain_width, 1)
         total = total + lax.ppermute(to, "shard", [(z, (z + step) % n_shard) for z in range(n_shard)])
-    head_grads = head_columns(where, both_cores([qkv_sum, qkv_y, qkv_x, qkv_last]))
-    token_parts, grad_w_gate, grad_w_up, grad_w_down, grad_w_out, head_grads, total = fence(
-        token_parts, grad_w_gate, grad_w_up, grad_w_down, grad_w_out, head_grads, total
-    )
     grad_w_query, grad_w_key, grad_w_value = head_grads
     grad_tokens = from_slots(token_parts)
 

time: 796 us -> 795 us (level)
  transfers between devices with their start and end apart: 97 -> 97, of which waited for: 25 -> 23; matrix products, arithmetic and copies ran while one was open for 9% -> 9% of each run, Pallas kernels for 63% -> 63%
where the time goes in v5:
time: 795 us; the launch traced here: 787 us
  Pallas kernels  504 us (63%)
  waiting for transfers between devices  83.3 us (10%)
  starting transfers between devices  63.6 us (8%)
  other arithmetic  50.6 us (6%)
  local copies, waits for them, and re-layouts  45.2 us (6%)
  blocking collectives  24.6 us (3%)
  between operations  15.5 us (2%)
    pallas_call x37, Pallas kernels, call(): pl.pallas_call(kernel, grid_spec=pltpu.PrefetchScalarGridSpec(num_scalar_...  504 us
    ppermute x21, waiting for transfers between devices, chip_layer(): over_x = lambda a: lax.ppermute(a, 'ctx', perm_x)  41.1 us
    ppermute x23, waiting for transfers between devices, chip_layer(): over_y = lambda a: lax.ppermute(a, 'batch', [(0, 1), (1, 0)])  29.4 us
    convert_element_type x9, other arithmetic, add(): functools.reduce(lambda a, b: a + b, [t.astype(f32) for t in terms])  25.2 us
    all_gather x1, blocking collectives, over_z(): gathered = lax.all_gather(piece, 'shard', axis=0, tiled=True)  24.6 us
    ppermute x23, starting transfers between devices, chip_layer(): over_y = lambda a: lax.ppermute(a, 'batch', [(0, 1), (1, 0)])  24.3 us
    ppermute x21, starting transfers between devices, chip_layer(): over_x = lambda a: lax.ppermute(a, 'ctx', perm_x)  22.8 us
  transfers between devices with their start and end apart: 97, of which 23 were waited for; matrix products, arithmetic and copies ran while one was open for 9% of the time, Pallas kernels for 63%

profile of v5, /device:TPU:0, one launch (start us, length us, event | category | flops | bytes accessed | tf_op | source)
XLA Modules:
  0.0 786.8 jit_solution(7475164664697554071)
XLA Ops:
  24.6 27.0 %collective-permute-done.1 = s32[512]{0:T(512)S(1)} collective-permute-done((s32[512]{0:T(512)S(1)}, s32[512]{0:T(512)S(1)}, u32[]{:S(2)}, u32[]{:S(2)}) %collective-permute-start.1) | collective-permute-done | bytes 2080 | tf_op jit(solution)/shard_map/ppermute | solution.py:812
  61.3 24.6 %all_gather.17 = bf16[768,384]{1,0:T(8,128)(2,1)} all-gather(bf16[192,384]{1,0:T(8,128)(2,1)S(1)} %pad_maximum_fusion.12), channel_id=1, replica_groups=mesh['shard'=4,'ctx'=4,'batch'=2] {'shard'}, dimensions={0}, use_global_device_ids=true | all-gather | bytes 737280 | tf_op jit(solution)/shard_map/all_gather | solution.py:819
  112.7 28.3 %front.1 = (bf16[2048,1536]{1,0:T(8,128)(2,1)}, bf16[2048,1536]{1,0:T(8,128)(2,1)}, bf16[1536,2048]{1,0:T(8,128)(2,1)}, bf16[2048,1024]{1,0:T(8,128)(2,1)}, bf16...) custom-call(s32[16]{0:T(128)} %get-tuple-element.685.near_ref, ...), custom_call_target="tpu_custom_call" | custom-call | flops 1000 | bytes 1000 | tf_op jit(solution)/shard_map/front/pallas_call | solution.py:74
  141.1 33.2 %attend.1 = (bf16[2048,1024]{1,0:T(8,128)(2,1)}, bf16[2048,1024]{1,0:T(8,128)(2,1)}) custom-call(bf16[2048,1024]{1,0:T(8,128)(2,1)} %get-tuple-element.352.q_ref, bf16[2048,512]{1,0:T(8,128)(2,1)} %get-tuple-element.353.k_ref, bf16[2048,512]{1,0:T(8,128)(2,1)} %get-tuple-element.354.v_ref), custom_call_target="tpu_custom_call" | custom-call | flops 1000 | bytes 1000 | tf_op jit(solution)/shard_map/attend/pallas_call | solution.py:74
  196.7 11.0 %out_own.1 = (f32[1024,1536]{1,0:T(8,128)}, bf16[1024,512]{1,0:T(8,128)(2,1)}, bf16[1024,512]{1,0:T(8,128)(2,1)}, bf16[1024,512]{1,0:T(8,128)(2,1)}) custom-call(s32[1]{0:T(128)S(6)} %mul.113.base_ref, bf16[2048,1024]{1,0:T(8,128)(2,1)} %get-tuple-element.364.refs_0_.mixed_ref.o_ref, bf16[1024,1536]{1,0:T(8,128)(2,1)} %out_rows.1.refs_1_.refs_6_, ...), custom_call_target="tpu_custom_call" | custom-call | flops 1000 | bytes 1000 | tf_op jit(solution)/shard_map/out_own/pallas_call | solution.py:74
  211.3 8.1 %span_join.1 = bf16[16,128,1536]{2,1,0:T(8,128)(2,1)} custom-call(s32[16]{0:T(128)} %get-tuple-element.685.near_ref, s32[16]{0:T(128)} %get-tuple-element.684.far_ref, s32[16]{0:T(128)} %copy-done.42, bf16[8,128,1536]{2,1,0:T(8,128)(2,1)} %bitcast.89, bf16[8,128,1536]{2,1,0:T(8,128)(2,1)} %bitcast.90, bf16[8,128,1536]{2,1,0:T(8,128)(2,1)} %bitcast.91, ...), custom_call_target="tpu_custom_call" | custom-call | flops 1000 | bytes 1000 | tf_op jit(solution)/shard_map/span_join/pallas_call | solution.py:74
  219.4 8.8 %collective-permute-done.20.gate_ref.refs_10_ = bf16[4,384,512]{2,1,0:T(8,128)(2,1)} collective-permute-done((bf16[4,384,512]{2,1,0:T(8,128)(2,1)}, bf16[4,384,512]{2,1,0:T(8,128)(2,1)}, u32[]{:S(2)}, u32[]{:S(2)}) %collective-permute-start.20) | collective-permute-done | bytes 1572896 | tf_op jit(solution)/shard_map/ppermute | solution.py:812
  233.8 9.5 %join_halves.1 = (bf16[2048,1536]{1,0:T(8,128)(2,1)}, bf16[1536,2048]{1,0:T(8,128)(2,1)}) custom-call(s32[1]{0:T(128)} %bitcast.3.core_ref, bf16[1024,512]{1,0:T(8,128)(2,1)} %get-tuple-element.380.refs_0_, bf16[1024,512]{1,0:T(8,128)(2,1)} %get-tuple-element.381.refs_1_, bf16[1024,512]{1,0:T(8,128)(2,1)} %get-tuple-element.382.refs_2_, ...), custom_call_target="tpu_custom_call" | custom-call | flops 1000 | bytes 1000 | tf_op jit(solution)/shard_map/join_halves/pallas_call | solution.py:74
  243.3 15.1 %hidden_units.4 = (bf16[2048,512]{1,0:T(8,128)(2,1)}, bf16[2048,1024]{1,0:T(8,128)(2,1)}) custom-call(bf16[2048,1536]{1,0:T(8,128)(2,1)} %get-tuple-element.424.n_ref, bf16[2048,1536]{1,0:T(8,128)(2,1)} %bitcast.70, bf16[4,384,512]{2,1,0:T(8,128)(2,1)} %bitcast.97, bf16[4,384,512]{2,1,0:T(8,128)(2,1)} %slice.125.up_ref.refs_5_, ...), custom_call_target="tpu_custom_call" | custom-call | flops 1000 | bytes 1000 | tf_op jit(solution)/shard_map/hidden_units/pallas_call | solution.py:74
  258.4 17.5 %feed_grads.4 = (bf16[1536,512]{1,0:T(8,128)(2,1)}, bf16[1536,512]{1,0:T(8,128)(2,1)}, bf16[512,1536]{1,0:T(8,128)(2,1)}) custom-call(bf16[1536,2048]{1,0:T(8,128)(2,1)} %get-tuple-element.390.n_ref, bf16[2048,1536]{1,0:T(8,128)(2,1)} %bitcast.71, bf16[2048,512]{1,0:T(8,128)(2,1)} %get-tuple-element.444.product_ref.refs_0_, ...), custom_call_target="tpu_custom_call" | custom-call | flops 1000 | bytes 1000 | tf_op jit(solution)/shard_map/feed_grads/pallas_call | solution.py:74
  277.9 15.2 %hidden_units.5 = (bf16[2048,512]{1,0:T(8,128)(2,1)}, bf16[2048,1024]{1,0:T(8,128)(2,1)}) custom-call(bf16[2048,1536]{1,0:T(8,128)(2,1)} %get-tuple-element.424.n_ref, bf16[2048,1536]{1,0:T(8,128)(2,1)} %bitcast.72, bf16[4,384,512]{2,1,0:T(8,128)(2,1)} %collective-permute-done.9.gate_ref.refs_6_, ...), custom_call_target="tpu_custom_call" | custom-call | flops 1000 | bytes 1000 | tf_op jit(solution)/shard_map/hidden_units/pallas_call | solution.py:74
  293.0 17.5 %feed_grads.5 = (bf16[1536,512]{1,0:T(8,128)(2,1)}, bf16[1536,512]{1,0:T(8,128)(2,1)}, bf16[512,1536]{1,0:T(8,128)(2,1)}) custom-call(bf16[1536,2048]{1,0:T(8,128)(2,1)} %get-tuple-element.390.n_ref, bf16[2048,1536]{1,0:T(8,128)(2,1)} %bitcast.73, bf16[2048,512]{1,0:T(8,128)(2,1)} %get-tuple-element.445.product_ref.refs_1_, ...), custom_call_target="tpu_custom_call" | custom-call | flops 1000 | bytes 1000 | tf_op jit(solution)/shard_map/feed_grads/pallas_call | solution.py:74
  313.3 15.4 %hidden_units.6 = (bf16[2048,512]{1,0:T(8,128)(2,1)}, bf16[2048,1024]{1,0:T(8,128)(2,1)}) custom-call(bf16[2048,1536]{1,0:T(8,128)(2,1)} %get-tuple-element.424.n_ref, bf16[2048,1536]{1,0:T(8,128)(2,1)} %bitcast.74, bf16[4,384,512]{2,1,0:T(8,128)(2,1)} %copy-done.6, bf16[4,768,512]{2,1,0:T(8,128)(2,1)} %bitcast.79, bf16[4,768,512]{2,1,0:T(8,128)(2,1)} %bitcast.80), custom_call_target="tpu_custom_call" | custom-call | flops 1000 | bytes 1000 | tf_op jit(solution)/shard_map/hidden_units/pallas_call | solution.py:74
  328.7 17.5 %feed_grads.6 = (bf16[1536,512]{1,0:T(8,128)(2,1)}, bf16[1536,512]{1,0:T(8,128)(2,1)}, bf16[512,1536]{1,0:T(8,128)(2,1)}) custom-call(bf16[1536,2048]{1,0:T(8,128)(2,1)} %get-tuple-element.390.n_ref, bf16[2048,1536]{1,0:T(8,128)(2,1)} %bitcast.75, bf16[2048,512]{1,0:T(8,128)(2,1)} %get-tuple-element.446.product_ref.refs_2_, ...), custom_call_target="tpu_custom_call" | custom-call | flops 1000 | bytes 1000 | tf_op jit(solution)/shard_map/feed_grads/pallas_call | solution.py:74
  348.4 15.1 %hidden_units.7 = (bf16[2048,512]{1,0:T(8,128)(2,1)}, bf16[2048,1024]{1,0:T(8,128)(2,1)}) custom-call(bf16[2048,1536]{1,0:T(8,128)(2,1)} %get-tuple-element.424.n_ref, bf16[2048,1536]{1,0:T(8,128)(2,1)} %bitcast.76, bf16[4,384,512]{2,1,0:T(8,128)(2,1)} %collective-permute-done.20.gate_ref.refs_10_, bf16[4,384,512]{2,1,0:T(8,128)(2,1)} %copy-done.5, ...), custom_call_target="tpu_custom_call" | custom-call | flops 1000 | bytes 1000 | tf_op jit(solution)/shard_map/hidden_units/pallas_call | solution.py:74
  363.5 17.5 %feed_grads.7 = (bf16[1536,512]{1,0:T(8,128)(2,1)}, bf16[1536,512]{1,0:T(8,128)(2,1)}, bf16[512,1536]{1,0:T(8,128)(2,1)}) custom-call(bf16[1536,2048]{1,0:T(8,128)(2,1)} %get-tuple-element.390.n_ref, bf16[2048,1536]{1,0:T(8,128)(2,1)} %bitcast.77, bf16[2048,512]{1,0:T(8,128)(2,1)} %get-tuple-element.447.product_ref.refs_3_, ...), custom_call_target="tpu_custom_call" | custom-call | flops 1000 | bytes 1000 | tf_op jit(solution)/shard_map/feed_grads/pallas_call | solution.py:74
  385.9 20.9 %back_other.1 = (bf16[1024,512]{1,0:T(8,128)(2,1)}, bf16[1024,512]{1,0:T(8,128)(2,1)}, bf16[1024,512]{1,0:T(8,128)(2,1)}) custom-call(s32[1]{0:T(128)S(6)} %mul.134.base_ref, bf16[2048,1024]{1,0:T(8,128)(2,1)} %get-tuple-element.437.both_ref.refs_0_, bf16[2048,1024]{1,0:T(8,128)(2,1)} %get-tuple-element.438.both_ref.refs_1_, ...), custom_call_target="tpu_custom_call" | custom-call | flops 1000 | bytes 1000 | tf_op jit(solution)/shard_map/back_other/pallas_call | solution.py:74
  407.4 11.3 %down_other.1 = (bf16[1024,512]{1,0:T(8,128)(2,1)}, bf16[1024,512]{1,0:T(8,128)(2,1)}, bf16[1024,512]{1,0:T(8,128)(2,1)}) custom-call(s32[1]{0:T(128)S(6)} %mul.134.base_ref, bf16[2048,512]{1,0:T(8,128)(2,1)} %get-tuple-element.444.product_ref.refs_0_, bf16[2048,512]{1,0:T(8,128)(2,1)} %get-tuple-element.445.product_ref.refs_1_, ...), custom_call_target="tpu_custom_call" | custom-call | flops 1000 | bytes 1000 | tf_op jit(solution)/shard_map/down_other/pallas_call | solution.py:74
  426.9 24.5 %back_own.1 = (f32[1024,1536]{1,0:T(8,128)}, f32[8,1536]{1,0:T(8,128)}, bf16[1024,512]{1,0:T(8,128)(2,1)}, bf16[1024,512]{1,0:T(8,128)(2,1)}, bf16[1024,512]{1,0:T(8,128)(2,1)}) custom-call(s32[1]{0:T(128)S(6)} %mul.113.base_ref, bf16[2048,1024]{1,0:T(8,128)(2,1)} %get-tuple-element.437.both_ref.refs_0_, ...), custom_call_target="tpu_custom_call" | custom-call | flops 1000 | bytes 1000 | tf_op jit(solution)/shard_map/back_own/pallas_call | solution.py:74
  453.0 12.7 %down_own.1 = bf16[1024,1536]{1,0:T(8,128)(2,1)} custom-call(s32[1]{0:T(128)S(6)} %mul.113.base_ref, bf16[2048,512]{1,0:T(8,128)(2,1)} %get-tuple-element.444.product_ref.refs_0_, bf16[2048,512]{1,0:T(8,128)(2,1)} %get-tuple-element.445.product_ref.refs_1_, bf16[2048,512]{1,0:T(8,128)(2,1)} %get-tuple-element.446.product_ref.refs_2_, ...), custom_call_target="tpu_custom_call" | custom-call | flops 1000 | bytes 1000 | tf_op jit(solution)/shard_map/down_own/pallas_call | solution.py:74
  479.5 12.3 %mixed_back.1 = (bf16[2048,1536]{1,0:T(8,128)(2,1)}, bf16[2048,1024]{1,0:T(8,128)(2,1)}) custom-call(s32[1]{0:T(128)} %bitcast.3.core_ref, bf16[1024,512]{1,0:T(8,128)(2,1)} %get-tuple-element.474.refs_0_, bf16[1024,512]{1,0:T(8,128)(2,1)} %get-tuple-element.475.refs_1_, bf16[1024,512]{1,0:T(8,128)(2,1)} %get-tuple-element.476.refs_2_, ...), custom_call_target="tpu_custom_call" | custom-call | flops 1000 | bytes 1000 | tf_op jit(solution)/shard_map/mixed_back/pallas_call | solution.py:74
  491.7 12.1 %out_grads.1 = (bf16[4,48,1536]{2,1,0:T(8,128)(2,1)}, bf16[4,48,1536]{2,1,0:T(8,128)(2,1)}, bf16[4,48,1536]{2,1,0:T(8,128)(2,1)}, bf16[4,48,1536]{2,1,0:T(8,128)(2,1)}) custom-call(s32[1]{0:T(128)} %bitcast.21.place_ref, bf16[2048,1024]{1,0:T(8,128)(2,1)} %get-tuple-element.364.refs_0_.mixed_ref.o_ref, bf16[2048,1536]{1,0:T(8,128)(2,1)} %get-tuple-element.481.grad_ref), custom_call_target="tpu_custom_call" | custom-call | flops 1000 | bytes 1000 | tf_op jit(solution)/shard_map/out_grads/pallas_call | solution.py:74
  519.8 20.6 %attend_back.4 = (bf16[2048,256]{1,0:T(8,128)(2,1)}, bf16[2048,128]{1,0:T(8,128)(2,1)}, bf16[2048,128]{1,0:T(8,128)(2,1)}) custom-call(bf16[2048,1024]{1,0:T(8,128)(2,1)} %get-tuple-element.550.q_ref, bf16[2048,512]{1,0:T(8,128)(2,1)} %get-tuple-element.353.k_ref, bf16[2048,512]{1,0:T(8,128)(2,1)} %get-tuple-element.354.v_ref, ...), custom_call_target="tpu_custom_call" | custom-call | flops 1000 | bytes 1000 | tf_op jit(solution)/shard_map/attend_back/pallas_call | solution.py:74
  542.5 8.1 %qkv_grad.4 = bf16[1536,384]{1,0:T(8,128)(2,1)} custom-call(bf16[1536,2048]{1,0:T(8,128)(2,1)} %get-tuple-element.351.n_ref, bf16[2048,256]{1,0:T(8,128)(2,1)} %get-tuple-element.500.q_ref.refs_9_, bf16[2048,128]{1,0:T(8,128)(2,1)} %get-tuple-element.501.k_ref.refs_10_, bf16[2048,128]{1,0:T(8,128)(2,1)} %get-tuple-element.502.v_ref.refs_11_, ...), custom_call_target="tpu_custom_call" | custom-call | flops 1000 | bytes 1000 | tf_op jit(solution)/shard_map/qkv_grad/pallas_call | solution.py:74
  555.3 20.8 %attend_back.5 = (bf16[2048,256]{1,0:T(8,128)(2,1)}, bf16[2048,128]{1,0:T(8,128)(2,1)}, bf16[2048,128]{1,0:T(8,128)(2,1)}) custom-call(bf16[2048,1024]{1,0:T(8,128)(2,1)} %get-tuple-element.550.q_ref, bf16[2048,512]{1,0:T(8,128)(2,1)} %get-tuple-element.353.k_ref, bf16[2048,512]{1,0:T(8,128)(2,1)} %get-tuple-element.354.v_ref, ...), custom_call_target="tpu_custom_call" | custom-call | flops 1000 | bytes 1000 | tf_op jit(solution)/shard_map/attend_back/pallas_call | solution.py:74
  598.2 20.6 %attend_back.6 = (bf16[2048,256]{1,0:T(8,128)(2,1)}, bf16[2048,128]{1,0:T(8,128)(2,1)}, bf16[2048,128]{1,0:T(8,128)(2,1)}) custom-call(bf16[2048,1024]{1,0:T(8,128)(2,1)} %get-tuple-element.550.q_ref, bf16[2048,512]{1,0:T(8,128)(2,1)} %get-tuple-element.353.k_ref, bf16[2048,512]{1,0:T(8,128)(2,1)} %get-tuple-element.354.v_ref, ...), custom_call_target="tpu_custom_call" | custom-call | flops 1000 | bytes 1000 | tf_op jit(solution)/shard_map/attend_back/pallas_call | solution.py:74
  618.9 8.4 %qkv_grad.6 = bf16[1536,384]{1,0:T(8,128)(2,1)} custom-call(bf16[1536,2048]{1,0:T(8,128)(2,1)} %get-tuple-element.351.n_ref, bf16[2048,256]{1,0:T(8,128)(2,1)} %get-tuple-element.539.q_ref.refs_3_, bf16[2048,128]{1,0:T(8,128)(2,1)} %get-tuple-element.540.k_ref.refs_4_, bf16[2048,128]{1,0:T(8,128)(2,1)} %get-tuple-element.541.v_ref.refs_5_, ...), custom_call_target="tpu_custom_call" | custom-call | flops 1000 | bytes 1000 | tf_op jit(solution)/shard_map/qkv_grad/pallas_call | solution.py:74
  635.4 20.6 %attend_back.7 = (bf16[2048,256]{1,0:T(8,128)(2,1)}, bf16[2048,128]{1,0:T(8,128)(2,1)}, bf16[2048,128]{1,0:T(8,128)(2,1)}) custom-call(bf16[2048,1024]{1,0:T(8,128)(2,1)} %get-tuple-element.550.q_ref, bf16[2048,512]{1,0:T(8,128)(2,1)} %get-tuple-element.353.k_ref, bf16[2048,512]{1,0:T(8,128)(2,1)} %get-tuple-element.354.v_ref, ...), custom_call_target="tpu_custom_call" | custom-call | flops 1000 | bytes 1000 | tf_op jit(solution)/shard_map/attend_back/pallas_call | solution.py:74
  657.3 8.1 %qkv_grad.7 = bf16[1536,384]{1,0:T(8,128)(2,1)} custom-call(bf16[1536,2048]{1,0:T(8,128)(2,1)} %get-tuple-element.351.n_ref, bf16[2048,256]{1,0:T(8,128)(2,1)} %get-tuple-element.568.q_ref.refs_0_, bf16[2048,128]{1,0:T(8,128)(2,1)} %get-tuple-element.569.k_ref.refs_1_, bf16[2048,128]{1,0:T(8,128)(2,1)} %get-tuple-element.570.v_ref.refs_2_, ...), custom_call_target="tpu_custom_call" | custom-call | flops 1000 | bytes 1000 | tf_op jit(solution)/shard_map/qkv_grad/pallas_call | solution.py:74
  671.5 11.7 %in_other.1 = (bf16[1024,512]{1,0:T(8,128)(2,1)}, bf16[1024,512]{1,0:T(8,128)(2,1)}, bf16[1024,512]{1,0:T(8,128)(2,1)}) custom-call(s32[1]{0:T(128)S(6)} %mul.134.base_ref, bf16[2048,256]{1,0:T(8,128)(2,1)} %get-tuple-element.568.q_ref.refs_0_, bf16[2048,128]{1,0:T(8,128)(2,1)} %get-tuple-element.569.k_ref.refs_1_, ...), custom_call_target="tpu_custom_call" | custom-call | flops 1000 | bytes 1000 | tf_op jit(solution)/shard_map/in_other/pallas_call | solution.py:74
  690.2 15.3 %in_own.1 = (bf16[1024,1536]{1,0:T(8,128)(2,1)}, f32[8,1536]{1,0:T(8,128)}) custom-call(s32[1]{0:T(128)S(6)} %mul.113.base_ref, bf16[2048,256]{1,0:T(8,128)(2,1)} %get-tuple-element.568.q_ref.refs_0_, bf16[2048,128]{1,0:T(8,128)(2,1)} %get-tuple-element.569.k_ref.refs_1_, bf16[2048,128]{1,0:T(8,128)(2,1)} %get-tuple-element.570.v_ref.refs_2_, ...), custom_call_target="tpu_custom_call" | custom-call | flops 1000 | bytes 1000 | tf_op jit(solution)/shard_map/in_own/pallas_call | solution.py:74
  733.6 8.3 %collective-permute-done.78.refs_3_ = bf16[384,384]{1,0:T(8,128)(2,1)} collective-permute-done((bf16[384,384]{1,0:T(8,128)(2,1)}, bf16[384,384]{1,0:T(8,128)(2,1)}, u32[]{:S(2)}, u32[]{:S(2)}) %collective-permute-start.78) | collective-permute-done | bytes 294944 | tf_op jit(solution)/shard_map/ppermute | solution.py:815
  (402 shorter events, 253.7 us)
Async XLA Ops:
  7.2 46.6 %all-gather.5.cloned.1.call-start = ((), (), s32[]{:S(2)}) async-start(), calls=%async_computation.7 | async-start | bytes 1536000 | tf_op jit(solution)/shard_map/all_gather | solution.py:819
  14.2 37.5 %collective-permute-start = (bf16[512,1536]{1,0:T(8,128)(2,1)S(1)}, bf16[512,1536]{1,0:T(8,128)(2,1)}, u32[]{:S(2)}, u32[]{:S(2)}) collective-permute-start(bf16[512,1536]{1,0:T(8,128)(2,1)S(1)} %get-tuple-element.323), channel_id=1, source_target_pairs={{0,4},{2,6},{4,0},{6,2},{1,5},{3,7},{5,1},{7,3},{8,12},{10,14},{12... | collective-permute-start | bytes 4718600 | tf_op jit(solution)/shard_map/ppermute | solution.py:812
  17.2 85.1 %all-gather.7.cloned.1.call-start = ((), (), s32[]{:S(2)}) async-start(), calls=%async_computation.8 | async-start | bytes 1966080 | tf_op jit(solution)/shard_map/all_gather | solution.py:819
  57.3 119.1 %all-gather.9.cloned.1.call-start = ((), (), s32[]{:S(2)}) async-start(), calls=%async_computation.9 | async-start | bytes 3932160 | tf_op jit(solution)/shard_map/all_gather | solution.py:819
  104.7 205.9 %all-gather.11.cloned.1.call-start = ((), (), s32[]{:S(2)}) async-start(), calls=%async_computation.10 | async-start | bytes 3932160 | tf_op jit(solution)/shard_map/all_gather | solution.py:819
  104.9 69.3 %collective-permute-start.8 = (bf16[512,1536]{1,0:T(8,128)(2,1)S(1)}, bf16[512,1536]{1,0:T(8,128)(2,1)}, u32[]{:S(2)}, u32[]{:S(2)}) collective-permute-start(bf16[512,1536]{1,0:T(8,128)(2,1)S(1)} %copy-done.18), channel_id=1, source_target_pairs={{0,4},{2,6},{4,0},{6,2},{1,5},{3,7},{5,1},{7,3},{8,12},{10,14},{12... | collective-permute-start | bytes 4718600 | tf_op jit(solution)/shard_map/ppermute | solution.py:812
  106.0 74.1 %collective-permute-start.9 = (bf16[4,384,512]{2,1,0:T(8,128)(2,1)}, bf16[4,384,512]{2,1,0:T(8,128)(2,1)}, u32[]{:S(2)}, u32[]{:S(2)}) collective-permute-start(bf16[4,384,512]{2,1,0:T(8,128)(2,1)} %bitcast.95), channel_id=1, source_target_pairs={{0,1},{1,0},{2,3},{3,2},{4,5},{5,4},{6,7},{7,6},{8,9},{9,8},{10,11... | collective-permute-start | bytes 4718600 | tf_op jit(solution)/shard_map/ppermute | solution.py:815
  107.2 72.9 %collective-permute-start.10 = (bf16[4,192,384]{2,1,0:T(8,128)(2,1)}, bf16[4,192,384]{2,1,0:T(8,128)(2,1)}, u32[]{:S(2)}, u32[]{:S(2)}) collective-permute-start(bf16[4,192,384]{2,1,0:T(8,128)(2,1)} %bitcast.18.refs_0_), channel_id=1, source_target_pairs={{0,1},{1,0},{2,3},{3,2},{4,5},{5,4},{6,7},{7,6},{8,9},{9,8},{10,11... | collective-permute-start | bytes 1769480 | tf_op jit(solution)/shard_map/ppermute | solution.py:815
  108.1 72.1 %collective-permute-start.11 = (bf16[4,192,384]{2,1,0:T(8,128)(2,1)}, bf16[4,192,384]{2,1,0:T(8,128)(2,1)}, u32[]{:S(2)}, u32[]{:S(2)}) collective-permute-start(bf16[4,192,384]{2,1,0:T(8,128)(2,1)} %bitcast.18.refs_0_), channel_id=1, source_target_pairs={{0,4},{2,6},{4,0},{6,2},{1,5},{3,7},{5,1},{7,3},{8,12},{10,14},{12... | collective-permute-start | bytes 1769480 | tf_op jit(solution)/shard_map/ppermute | solution.py:812
  109.0 71.1 %collective-permute-start.12 = (bf16[4,192,384]{2,1,0:T(8,128)(2,1)}, bf16[4,192,384]{2,1,0:T(8,128)(2,1)}, u32[]{:S(2)}, u32[]{:S(2)}) collective-permute-start(bf16[4,192,384]{2,1,0:T(8,128)(2,1)} %bitcast.18.refs_0_), channel_id=1, source_target_pairs={{0,5},{1,4},{2,7},{3,6},{4,1},{5,0},{6,3},{7,2},{8,13},{9,12},{10,... | collective-permute-start | bytes 1769480 | tf_op jit(solution)/shard_map/ppermute | solution.py:816
  191.6 36.6 %collective-permute-start.20 = (bf16[4,384,512]{2,1,0:T(8,128)(2,1)}, bf16[4,384,512]{2,1,0:T(8,128)(2,1)}, u32[]{:S(2)}, u32[]{:S(2)}) collective-permute-start(bf16[4,384,512]{2,1,0:T(8,128)(2,1)} %bitcast.96), channel_id=1, source_target_pairs={{0,4},{2,6},{4,0},{6,2},{1,5},{3,7},{5,1},{7,3},{8,12},{10,14},{12... | collective-permute-start | bytes 4718600 | tf_op jit(solution)/shard_map/ppermute | solution.py:812
  193.7 37.0 %collective-permute-start.21 = (bf16[4,384,512]{2,1,0:T(8,128)(2,1)}, bf16[4,384,512]{2,1,0:T(8,128)(2,1)}, u32[]{:S(2)}, u32[]{:S(2)}) collective-permute-start(bf16[4,384,512]{2,1,0:T(8,128)(2,1)} %slice.125.up_ref.refs_5_), channel_id=1, source_target_pairs={{0,1},{1,0},{2,3},{3,2},{4,5},{5,4},{6,7},{7,6},{8,9},{9,8},{10,11... | collective-permute-start | bytes 4718600 | tf_op jit(solution)/shard_map/ppermute | solution.py:815
  194.8 188.0 %reduce-scatter.8.cloned.1.call-start = ((), (), s32[]{:S(2)}) async-start(), calls=%async_computation.11 | async-start | bytes 1966080 | tf_op jit(solution)/shard_map/reduce_scatter | solution.py:826
  231.7 44.2 %collective-permute-start.22 = (bf16[4,384,512]{2,1,0:T(8,128)(2,1)S(1)}, bf16[4,384,512]{2,1,0:T(8,128)(2,1)S(1)}, u32[]{:S(2)}, u32[]{:S(2)}) collective-permute-start(bf16[4,384,512]{2,1,0:T(8,128)(2,1)S(1)} %copy-done.4), channel_id=1, source_target_pairs={{0,4},{2,6},{4,0},{6,2},{1,5},{3,7},{5,1},{7,3},{8,12},{10,14},{12... | collective-permute-start | bytes 4718600 | tf_op jit(solution)/shard_map/ppermute | solution.py:812
  232.6 43.3 %collective-permute-start.23 = (bf16[4,384,512]{2,1,0:T(8,128)(2,1)}, bf16[4,384,512]{2,1,0:T(8,128)(2,1)}, u32[]{:S(2)}, u32[]{:S(2)}) collective-permute-start(bf16[4,384,512]{2,1,0:T(8,128)(2,1)} %slice.110.down_ref.refs_4_), channel_id=1, source_target_pairs={{0,1},{1,0},{2,3},{3,2},{4,5},{5,4},{6,7},{7,6},{8,9},{9,8},{10,11... | collective-permute-start | bytes 4718600 | tf_op jit(solution)/shard_map/ppermute | solution.py:815
  275.9 35.6 %collective-permute-start.24 = (bf16[4,384,512]{2,1,0:T(8,128)(2,1)}, bf16[4,384,512]{2,1,0:T(8,128)(2,1)S(1)}, u32[]{:S(2)}, u32[]{:S(2)}) collective-permute-start(bf16[4,384,512]{2,1,0:T(8,128)(2,1)} %collective-permute-done.20.gate_ref.refs_10_), channel_id=1, source_target_pairs={{0,1},{1,0},{2,3},{3,2},{4,5},{5,4},{6,7},{7,6},{8,9},{9,8},{10,11... | collective-permute-start | bytes 4718600 | tf_op jit(solution)/shard_map/ppermute | solution.py:815
  346.5 73.9 %reduce-scatter.10.cloned.1.call-start = ((), (), s32[]{:S(2)}) async-start(), calls=%async_computation.12 | async-start | bytes 1966080 | tf_op jit(solution)/shard_map/reduce_scatter | solution.py:826
  382.8 82.9 %reduce-scatter.12.cloned.1.call-start = ((), (), s32[]{:S(2)}) async-start(), calls=%async_computation.13 | async-start | bytes 1966080 | tf_op jit(solution)/shard_map/reduce_scatter | solution.py:826
  382.9 36.4 %collective-permute-start.31 = (bf16[1536,512]{1,0:T(8,128)(2,1)}, bf16[1536,512]{1,0:T(8,128)(2,1)}, u32[]{:S(2)}, u32[]{:S(2)}) collective-permute-start(bf16[1536,512]{1,0:T(8,128)(2,1)} %get-tuple-element.451), channel_id=1, source_target_pairs={{0,1},{1,0},{2,3},{3,2},{4,5},{5,4},{6,7},{7,6},{8,9},{9,8},{10,11... | collective-permute-start | bytes 4718600 | tf_op jit(solution)/shard_map/ppermute | solution.py:815
  384.4 36.0 %collective-permute-start.32 = (bf16[1536,512]{1,0:T(8,128)(2,1)}, bf16[1536,512]{1,0:T(8,128)(2,1)}, u32[]{:S(2)}, u32[]{:S(2)}) collective-permute-start(bf16[1536,512]{1,0:T(8,128)(2,1)} %get-tuple-element.452), channel_id=1, source_target_pairs={{0,4},{2,6},{4,0},{6,2},{1,5},{3,7},{5,1},{7,3},{8,12},{10,14},{12... | collective-permute-start | bytes 4718600 | tf_op jit(solution)/shard_map/ppermute | solution.py:812
  424.1 88.2 %reduce-scatter.14.cloned.1.call-start = ((), (), s32[]{:S(2)}) async-start(), calls=%async_computation.14 | async-start | bytes 1966080 | tf_op jit(solution)/shard_map/reduce_scatter | solution.py:826
  424.8 40.8 %collective-permute-start.39 = (bf16[1536,512]{1,0:T(8,128)(2,1)}, bf16[1536,512]{1,0:T(8,128)(2,1)}, u32[]{:S(2)}, u32[]{:S(2)}) collective-permute-start(bf16[1536,512]{1,0:T(8,128)(2,1)} %get-tuple-element.467), channel_id=1, source_target_pairs={{0,4},{2,6},{4,0},{6,2},{1,5},{3,7},{5,1},{7,3},{8,12},{10,14},{12... | collective-permute-start | bytes 4718600 | tf_op jit(solution)/shard_map/ppermute | solution.py:812
  426.3 39.4 %collective-permute-start.40 = (bf16[512,1536]{1,0:T(8,128)(2,1)}, bf16[512,1536]{1,0:T(8,128)(2,1)}, u32[]{:S(2)}, u32[]{:S(2)}) collective-permute-start(bf16[512,1536]{1,0:T(8,128)(2,1)} %get-tuple-element.468), channel_id=1, source_target_pairs={{0,1},{1,0},{2,3},{3,2},{4,5},{5,4},{6,7},{7,6},{8,9},{9,8},{10,11... | collective-permute-start | bytes 4718600 | tf_op jit(solution)/shard_map/ppermute | solution.py:815
  469.5 111.5 %reduce-scatter.16.cloned.1.call-start = ((), (), s32[]{:S(2)}) async-start(), calls=%async_computation.15 | async-start | bytes 1966080 | tf_op jit(solution)/shard_map/reduce_scatter | solution.py:826
  473.8 38.5 %collective-permute-start.41 = (bf16[512,1536]{1,0:T(8,128)(2,1)}, bf16[512,1536]{1,0:T(8,128)(2,1)}, u32[]{:S(2)}, u32[]{:S(2)}) collective-permute-start(bf16[512,1536]{1,0:T(8,128)(2,1)} %add_convert_fusion.2), channel_id=1, source_target_pairs={{0,4},{2,6},{4,0},{6,2},{1,5},{3,7},{5,1},{7,3},{8,12},{10,14},{12... | collective-permute-start | bytes 4718600 | tf_op jit(solution)/shard_map/ppermute | solution.py:812
  515.5 103.3 %reduce-scatter.18.cloned.1.call-start = ((), (), s32[]{:S(2)}) async-start(), calls=%async_computation.16 | async-start | bytes 737280 | tf_op jit(solution)/shard_map/reduce_scatter | solution.py:826
  594.9 122.8 %reduce-scatter.20.cloned.1.call-start = ((), (), s32[]{:S(2)}) async-start(), calls=%async_computation.17 | async-start | bytes 1474560 | tf_op jit(solution)/shard_map/reduce_scatter | solution.py:826
  594.9 37.7 %collective-permute-start.53 = (bf16[1536,384]{1,0:T(8,128)(2,1)}, bf16[1536,384]{1,0:T(8,128)(2,1)}, u32[]{:S(2)}, u32[]{:S(2)}) collective-permute-start(bf16[1536,384]{1,0:T(8,128)(2,1)} %add_convert_fusion.5), channel_id=1, source_target_pairs={{0,4},{2,6},{4,0},{6,2},{1,5},{3,7},{5,1},{7,3},{8,12},{10,14},{12... | collective-permute-start | bytes 3538952 | tf_op jit(solution)/shard_map/ppermute | solution.py:812
  634.2 37.3 %collective-permute-start.61 = (bf16[256,1536]{1,0:T(8,128)(2,1)}, bf16[256,1536]{1,0:T(8,128)(2,1)S(1)}, u32[]{:S(2)}, u32[]{:S(2)}) collective-permute-start(bf16[256,1536]{1,0:T(8,128)(2,1)} %bitcast.117), channel_id=1, source_target_pairs={{0,6},{2,4},{4,2},{6,0},{1,7},{3,5},{5,3},{7,1},{8,14},{10,12},{12... | collective-permute-start | bytes 2359304 | tf_op jit(solution)/shard_map/ppermute | solution.py:814
  730.4 40.1 %collective-permute-start.75 = (bf16[256,1536]{1,0:T(8,128)(2,1)}, bf16[256,1536]{1,0:T(8,128)(2,1)S(1)}, u32[]{:S(2)}, u32[]{:S(2)}) collective-permute-start(bf16[256,1536]{1,0:T(8,128)(2,1)} %bitcast.38), channel_id=1, source_target_pairs={{0,2},{2,0},{4,6},{6,4},{1,3},{3,1},{5,7},{7,5},{8,10},{10,8},{12,... | collective-permute-start | bytes 2359304 | tf_op jit(solution)/shard_map/ppermute | solution.py:813
  730.4 40.0 %collective-permute-start.76 = (bf16[256,1536]{1,0:T(8,128)(2,1)}, bf16[256,1536]{1,0:T(8,128)(2,1)S(1)}, u32[]{:S(2)}, u32[]{:S(2)}) collective-permute-start(bf16[256,1536]{1,0:T(8,128)(2,1)} %bitcast.39), channel_id=1, source_target_pairs={{0,4},{2,6},{4,0},{6,2},{1,5},{3,7},{5,1},{7,3},{8,12},{10,14},{12... | collective-permute-start | bytes 2359304 | tf_op jit(solution)/shard_map/ppermute | solution.py:812
  731.9 38.6 %collective-permute-start.77 = (bf16[256,1536]{1,0:T(8,128)(2,1)S(1)}, bf16[256,1536]{1,0:T(8,128)(2,1)}, u32[]{:S(2)}, u32[]{:S(2)}) collective-permute-start(bf16[256,1536]{1,0:T(8,128)(2,1)S(1)} %bitcast.116), channel_id=1, source_target_pairs={{0,6},{2,4},{4,2},{6,0},{1,7},{3,5},{5,3},{7,1},{8,14},{10,12},{12... | collective-permute-start | bytes 2359304 | tf_op jit(solution)/shard_map/ppermute | solution.py:814
  (112 other events, 1761.5 us)
Sparse Core Ops, SparseCore 0:
  17.3 31.6 all-gather.4
  57.4 44.8 all-gather.6
  104.8 64.3 all-gather.8
  194.9 63.9 all-gather.10
  346.6 36.1 reduce-scatter.7
  384.9 34.2 reduce-scatter.9
  424.3 33.5 reduce-scatter.11
  469.6 33.5 reduce-scatter.13
  515.7 33.6 reduce-scatter.15
  595.0 20.1 reduce-scatter.17
  684.2 28.2 reduce-scatter.19
